TPU v7x, 1024 devices: a whole 4x4x32 slice. The times are simulated.
1024 devices in a mesh: dp: 64 (over z, core), expert: 16 (over y, x).
Axes of the slice: x: 4, y: 4, z: 32, core: 2. Of those that a mesh axis runs over, the one named last changes fastest.
Arguments:
- dy_tokens: bfloat16 [32768, 7168], P(('dp', 'expert')), may hold values from -6 to 6
- routing: int32 [32768, 4], P(('dp', 'expert')), may hold values from 0 to 15, all different within a row; in each aligned block of 32 rows (0 to 31, 32 to 63, ...) at most 9 rows name the same one
- route_weight: float32 [32768, 4], P(('dp', 'expert')), may hold values from 0.2 to 2.5
- pre_act: bfloat16 [147456, 256], P(('dp', 'expert')), may hold values from -6 to 6
- gate_weight: bfloat16 [16, 7168, 128], P('expert'), may hold values from -0.0625 to 0.0625
- up_weight: bfloat16 [16, 7168, 128], P('expert'), may hold values from -0.0625 to 0.0625
- down_weight: bfloat16 [16, 128, 7168], P('expert'), may hold values from -0.0625 to 0.0625
Outputs:
- grad_tokens: bfloat16 [32768, 7168], P(('dp', 'expert'))
- grad_down: float32 [16, 128, 7168], P('expert', 'dp')
Inputs may be any that keep to these rules, and one draw needn't show every extreme that they name: `routing`: each token names 4 different experts. The tokens of one device name any one expert at most 9 times, and in every draw some device's tokens name some expert exactly 9 times.
All inputs are finite; a program needn't handle non-finite values.
Results may differ from a plain program's by a relative error of at most 0.0064.
Values may be sent and summed in bfloat16 or wider, within the bound.
No kernel may reach another device: no remote copies, remote signals or barrier semaphores. Data moves between devices by JAX's collectives and lax.ppermute only.
A program may use at most 64 MiB of HBM per device.

v0:
```python
import jax
import jax.numpy as jnp
from jax import lax
from jax.sharding import PartitionSpec as P


def slot_targets(routing, experts, capacity):
    matches = (routing[:, :, None] == jnp.arange(experts, dtype=jnp.int32)[None, None, :]).astype(
        jnp.int32
    )
    per_token = jnp.sum(matches, axis=1)
    before = jnp.cumsum(per_token, axis=0) - per_token
    position = jnp.sum(matches * before[:, None, :], axis=2)
    return routing * capacity + position


def per_device(dy_tokens, routing, route_weight, pre_act, gate_weight, up_weight, down_weight):
    experts = lax.axis_size("expert")
    replicas = lax.axis_size("dp")
    tok_rows, model_width = dy_tokens.shape
    route_count = routing.shape[1]
    slot_rows = pre_act.shape[0]
    capacity = slot_rows // experts
    hidden_units = down_weight.shape[1]
    targets = slot_targets(routing, experts, capacity)
    flat_targets = targets.reshape(-1)
    placer = (jnp.arange(slot_rows, dtype=jnp.int32)[:, None] == flat_targets[None, :]).astype(
        jnp.bfloat16
    )
    scaled = (route_weight[:, :, None] * dy_tokens[:, None, :].astype(jnp.float32)).astype(
        jnp.bfloat16
    )
    scaled = scaled.reshape(tok_rows * route_count, model_width)
    outgoing = jnp.dot(placer, scaled, preferred_element_type=jnp.float32).astype(jnp.bfloat16)
    arrived = lax.all_to_all(
        outgoing.reshape(experts, capacity, model_width),
        "expert",
        split_axis=0,
        concat_axis=0,
        tiled=True,
    )
    arrived = arrived.reshape(slot_rows, model_width)
    gate_pre = pre_act[:, :hidden_units].astype(jnp.float32)
    up_pre = pre_act[:, hidden_units:].astype(jnp.float32)
    contract_last = (((1,), (1,)), ((), ()))
    grad_hidden = lax.dot_general(
        arrived, down_weight[0], contract_last, preferred_element_type=jnp.float32
    )
    sigmoid_gate = jax.nn.sigmoid(gate_pre)
    activated = gate_pre * sigmoid_gate
    hidden = (activated * up_pre).astype(jnp.bfloat16)
    grad_up = (grad_hidden * activated).astype(jnp.bfloat16)
    grad_gate = (
        grad_hidden * up_pre * sigmoid_gate * (1.0 + gate_pre * (1.0 - sigmoid_gate))
    ).astype(jnp.bfloat16)
    grad_rows = lax.dot_general(
        grad_gate, gate_weight[0], contract_last, preferred_element_type=jnp.float32
    )
    grad_rows = grad_rows + lax.dot_general(
        grad_up, up_weight[0], contract_last, preferred_element_type=jnp.float32
    )
    going_back = grad_rows.astype(jnp.bfloat16).reshape(experts, capacity, model_width)
    returned = lax.all_to_all(
        going_back, "expert", split_axis=0, concat_axis=0, tiled=True
    ).reshape(slot_rows, model_width)
    collect = jnp.sum(placer.reshape(slot_rows, tok_rows, route_count), axis=2)
    contract_first = (((0,), (0,)), ((), ()))
    grad_tokens = lax.dot_general(
        collect, returned, contract_first, preferred_element_type=jnp.float32
    ).astype(jnp.bfloat16)
    summed = lax.psum_scatter(
        lax.dot_general(hidden, arrived, contract_first, preferred_element_type=jnp.float32),
        "dp",
        scatter_dimension=0,
        tiled=True,
    )
    grad_down = (summed / replicas)[None]
    return (grad_tokens, grad_down)


def solution(mesh):
    placed = (
        P(("dp", "expert"), None),
        P(("dp", "expert"), None),
        P(("dp", "expert"), None),
        P(("dp", "expert"), None),
        P("expert", None, None),
        P("expert", None, None),
        P("expert", None, None),
    )
    return jax.shard_map(
        per_device,
        mesh=mesh,
        in_specs=placed,
        out_specs=(P(("dp", "expert"), None), P("expert", "dp", None)),
        check_vma=False,
    )
```

profile of v0, /device:TPU:1, one launch (start us, length us, event | category | flops | bytes accessed | tf_op | source)
XLA Modules:
  0.0 526.8 jit_solution(13589420535896372840)
XLA Ops:
  7.2 0.0 copy-start
  7.2 0.0 all-reduce.3.cloned.1.call-start
  7.2 0.8 convert_reduce_fusion
  8.0 0.1 copy.21
  8.1 0.1 reduce_window_sum.11
  8.2 0.1 copy.23
  8.3 0.7 select_reduce_fusion
  9.0 0.7 multiply_add_fusion
  9.6 0.1 copy.24
  9.7 0.1 eq.42
  9.8 0.8 copy.25
  10.6 0.1 mul.57
  10.7 3.7 mul.59
  14.4 5.3 mul.60
  19.7 4.1 convolution_convert_fusion
  23.8 3.5 reshape.43
  27.3 43.5 %all_to_all.10 = bf16[16,9,7168]{2,1,0:T(8,128)(2,1)} all-to-all(bf16[16,9,7168]{2,1,0:T(8,128)(2,1)} %reshape.43), channel_id=1, replica_groups=mesh['dp'=64,'expert'=16] {'expert'}, dimensions={0} | all-to-all | bytes 4128768 | tf_op jit(solution)/shard_map/all_to_all | solution.py:35
  70.8 3.6 reshape.44
  74.4 0.0 copy-start.1
  74.4 0.0 copy-start.3
  74.4 3.0 fusion.4
  77.3 0.0 copy-done.1
  77.3 0.0 copy-done.3
  77.4 2.5 fusion.18
  79.9 0.0 all-reduce.3.cloned.1.call-update
  79.9 0.0 copy-done
  79.9 0.0 copy-start.2
  79.9 0.7 fusion.2
  80.6 0.8 copy-done.2
  81.4 2.1 fusion
  83.5 3.6 reshape.45
  87.1 4.5 all-to-all-start.1
  91.6 1.3 dynamic-slice
  93.6 0.1 fusion.16
  93.7 418.4 %all-reduce.3.cloned.1.call-done = f32[128,7168]{1,0:T(8,128)} async-done(((f32[128,7168]{1,0:T(8,128)}), f32[128,7168]{1,0:T(8,128)}) %all-reduce.3.cloned.1.call-update) | async-done | bytes 3670032
  512.1 1.6 fusion.17
  513.7 0.0 all-to-all-done.1
  513.7 3.6 reshape.46
  517.2 2.8 convolution_convert_fusion.1
  (1 shorter events, 0.0 us)
Async XLA Ops:
  7.2 72.8 %copy-start = (bf16[1,7168,128]{2,1,0:T(8,128)(2,1)S(1)}, bf16[1,7168,128]{2,1,0:T(8,128)(2,1)}, u32[]{:S(2)}) copy-start(bf16[1,7168,128]{2,1,0:T(8,128)(2,1)} %param.11) | copy-start | bytes 5505028
  7.2 504.9 %all-reduce.3.cloned.1.call-start = ((), (), s32[]{:S(2)}) async-start(), calls=%async_computation.2 | async-start | bytes 7340032
  74.4 3.0 copy-start.1
  74.4 3.0 copy-start.3
  79.9 1.5 copy-start.2
  87.1 426.5 %all-to-all-start.1 = ((bf16[16,9,7168]{2,1,0:T(8,128)(2,1)}), bf16[16,9,7168]{2,1,0:T(8,128)(2,1)}, u32[]{:S(2)}, u32[]{:S(2)}) async-start(bf16[16,9,7168]{2,1,0:T(8,128)(2,1)} %reshape.45), calls=%async_computation.1 | async-start | bytes 7340032 | tf_op jit(solution)/shard_map/all_to_all | solution.py:63
Sparse Core Ops, SparseCore 0:
  80.0 431.9 all-reduce.2
where the time goes:
time: 528 us; the launch traced here: 527 us
  waiting for transfers between devices  418 us (79%)
  blocking collectives  43.5 us (8%)
  local copies, waits for them, and re-layouts  26.5 us (5%)
  matrix products  15.2 us (3%)
  between operations  14.8 us (3%)
    unnamed x2, waiting for transfers between devices  418 us
    all_to_all x1, blocking collectives, per_device(): lax.all_to_all(outgoing.reshape(experts, capacity, model_width), 'expert'...  43.5 us
  transfers between devices with their start and end apart: 2, of which 1 were waited for; matrix products, arithmetic and copies ran while one was open for 2% of the time, Pallas kernels for 0%

commit v1 on v0

v1 whole, which is shorter than its diff:
```python
import functools

import jax
import jax.numpy as jnp
from jax import lax
from jax.experimental import pallas as pl
from jax.experimental.pallas import tpu as pltpu
from jax.sharding import PartitionSpec as P

BF = jnp.bfloat16
F32 = jnp.float32
LANES = 128
FIRST = 8
PARAMS = pltpu.CompilerParams(vmem_limit_bytes=40 * 1024 * 1024)


def dot(a, b, contract):
    return lax.dot_general(a, b, (contract, ((), ())), preferred_element_type=F32)


def iota(shape, axis):
    return lax.broadcasted_iota(jnp.int32, shape, axis)


def write_block(ref, tail, pair, first, second, experts):
    main = experts * FIRST
    tiles = [x[:main].reshape(experts, FIRST, LANES) for x in (first, second)]
    ref[:, pair * 16 : pair * 16 + 16, :] = jnp.concatenate(tiles, axis=1).astype(BF)
    tail[:, 2 * pair, :] = first[main:]
    tail[:, 2 * pair + 1, :] = second[main:]


def read_block(ref, tail, pair, experts):
    both = ref[:, pair * 16 : pair * 16 + 16, :].astype(F32)
    main = experts * FIRST
    halves = []
    for at in range(2):
        block = both[:, at * FIRST : (at + 1) * FIRST, :].reshape(main, LANES)
        halves.append(jnp.concatenate([block, tail[:, 2 * pair + at, :]], axis=0))
    return jnp.concatenate(halves, axis=1)


def dispatch_kernel(experts, dy_ref, routing_ref, weight_ref, out_ref, pick_ref, tail):
    tokens, width = dy_ref.shape
    route_count = routing_ref.shape[1]
    main = experts * FIRST
    lanes = pick_ref.shape[1]
    slot = iota((tokens, lanes), 1)
    expert = jnp.where(slot < main, slot // FIRST, slot - main)
    position = jnp.where(slot < main, slot % FIRST, FIRST)
    named = jnp.zeros((tokens, lanes), F32)
    scale = jnp.zeros((tokens, lanes), F32)
    for k in range(route_count):
        hit = routing_ref[:, k : k + 1] == expert
        named = named + jnp.where(hit, 1.0, 0.0)
        scale = scale + jnp.where(hit, weight_ref[:, k : k + 1], 0.0)
    earlier = jnp.where(iota((tokens, tokens), 1) < iota((tokens, tokens), 0), 1.0, 0.0)
    before = dot(earlier.astype(BF), named.astype(BF), ((1,), (0,)))
    pick = jnp.where((named > 0.5) & (before == position.astype(F32)), 1.0, 0.0)
    pick_ref[...] = pick.astype(BF)
    rows = main + experts
    chosen = pick[:, :rows].astype(BF)
    rest = (pick * scale)[:, :rows]
    ones = jnp.ones((tokens, LANES), BF)
    row_weight = jnp.zeros((rows, LANES), F32)
    for _ in range(3):
        piece = rest.astype(BF)
        row_weight = row_weight + dot(piece, ones, ((0,), (0,)))
        rest = rest - piece.astype(F32)
    row_weight = jnp.concatenate([row_weight, row_weight], axis=1)
    for pair in range(width // (2 * LANES)):
        part = dot(chosen, dy_ref[:, pair * 2 * LANES : (pair + 1) * 2 * LANES], ((0,), (0,)))
        part = part * row_weight
        write_block(out_ref, tail, pair, part[:, :LANES], part[:, LANES:], experts)
    out_ref[:, experts_rows(width) :, :] = tail[...].astype(BF)


def experts_rows(width):
    return width // LANES * FIRST


def partial_kernel(
    experts, z_lo, own_ref, got_ref, pre_ref, arrived_ref, keep_ref, send_ref, factor_ref, tail
):
    rows, width = arrived_ref.shape
    hidden_units = pre_ref.shape[1] // 2
    main = experts * FIRST
    capacity = rows // experts
    new, old = iota((rows, rows), 0), iota((rows, rows), 1)
    source = jnp.where(
        new < main, new // FIRST * capacity + new % FIRST, (new - main) * capacity + FIRST
    )
    order = jnp.where(source == old, 1.0, 0.0).astype(BF)
    pre = dot(order, pre_ref[...], ((1,), (0,)))
    gate_pre, up_pre = pre[:, :hidden_units], pre[:, hidden_units:]
    sigmoid = 1.0 / (1.0 + jnp.exp(-gate_pre))
    activated = gate_pre * sigmoid
    factor_ref[:, :hidden_units] = up_pre * sigmoid * (1.0 + gate_pre * (1.0 - sigmoid))
    factor_ref[:, hidden_units:] = activated
    hidden = (activated * up_pre).astype(BF)
    half = hidden_units // 2
    block = half // z_lo
    unit, at = iota((hidden_units, hidden_units), 0), iota((hidden_units, hidden_units), 1)
    core = jnp.where(at < half, own_ref[0], 1 - own_ref[0])
    r = at % half
    target = 4 * (z_lo * ((r % block) // 2) + r // block) + 2 * core + r % 2
    hidden = dot(hidden, jnp.where(unit == target, 1.0, 0.0).astype(BF), ((1,), (0,))).astype(BF)
    tail[...] = got_ref[:, experts_rows(width) :, :].astype(F32)
    for pair in range(width // (2 * LANES)):
        at = slice(pair * 2 * LANES, (pair + 1) * 2 * LANES)
        arrived = read_block(got_ref, tail, pair, experts).astype(BF)
        arrived_ref[:, at] = arrived
        part = dot(hidden, arrived, ((0,), (0,)))
        keep_ref[:, at] = part[:half]
        send_ref[:, at] = part[half:].astype(BF)


def grad_kernel(experts, arrived_ref, factor_ref, gate_ref, up_ref, down_ref, out_ref, tail):
    width = arrived_ref.shape[1]
    hidden_units = down_ref.shape[1]
    grad_hidden = dot(arrived_ref[...], down_ref[0], ((1,), (1,)))
    grad_gate = (grad_hidden * factor_ref[:, :hidden_units]).astype(BF)
    grad_up = (grad_hidden * factor_ref[:, hidden_units:]).astype(BF)
    for pair in range(width // (2 * LANES)):
        at = slice(pair * 2 * LANES, (pair + 1) * 2 * LANES)
        part = dot(grad_gate, gate_ref[0, at, :], ((1,), (1,)))
        part = part + dot(grad_up, up_ref[0, at, :], ((1,), (1,)))
        write_block(out_ref, tail, pair, part[:, :LANES], part[:, LANES:], experts)
    out_ref[:, experts_rows(width) :, :] = tail[...].astype(BF)


def combine_kernel(experts, pick_ref, got_ref, out_ref, tail):
    width = out_ref.shape[1]
    tail[...] = got_ref[:, experts_rows(width) :, :].astype(F32)
    pick = pick_ref[:, : experts * (FIRST + 1)]
    for pair in range(width // (2 * LANES)):
        rows = read_block(got_ref, tail, pair, experts).astype(BF)
        out_ref[:, pair * 2 * LANES : (pair + 1) * 2 * LANES] = dot(
            pick, rows, ((1,), (0,))
        ).astype(BF)


def per_device(dy_tokens, routing, route_weight, pre_act, gate_weight, up_weight, down_weight):
    experts = lax.axis_size("expert")
    replicas = lax.axis_size("dp")
    tokens, width = dy_tokens.shape
    rows = pre_act.shape[0]
    hidden_units = down_weight.shape[1]
    capacity = rows // experts
    assert capacity == FIRST + 1
    block_rows = capacity * width // LANES
    chips = replicas // 2
    z_lo = 4
    z_hi = chips // z_lo
    shape = jax.ShapeDtypeStruct
    vmem = pl.BlockSpec(memory_space=pltpu.VMEM)
    smem = pl.BlockSpec(memory_space=pltpu.SMEM)
    tail = pltpu.VMEM((experts, width // LANES, LANES), F32)
    block = shape((experts, block_rows, LANES), BF)

    outgoing, pick = pl.pallas_call(
        functools.partial(dispatch_kernel, experts),
        out_shape=(block, shape((tokens, 2 * LANES), BF)),
        in_specs=[vmem] * 3,
        out_specs=(vmem, vmem),
        scratch_shapes=[tail],
        compiler_params=PARAMS,
        name="dispatch_rows",
    )(dy_tokens, routing, route_weight)
    got = lax.all_to_all(outgoing, "expert", split_axis=0, concat_axis=0, tiled=True)

    core = lax.axis_index("dp") % 2
    half = hidden_units // 2
    arrived, keep, send, factor = pl.pallas_call(
        functools.partial(partial_kernel, experts, z_lo),
        out_shape=(
            shape((rows, width), BF),
            shape((half, width), F32),
            shape((half, width), BF),
            shape((rows, 2 * hidden_units), F32),
        ),
        in_specs=[smem, vmem, vmem],
        out_specs=(vmem,) * 4,
        scratch_shapes=[tail],
        compiler_params=PARAMS,
        name="down_partial",
    )(core.reshape(1), got, pre_act)
    other = lax.ppermute(send, "dp", [(i, i ^ 1) for i in range(replicas)])

    going_back = pl.pallas_call(
        functools.partial(grad_kernel, experts),
        out_shape=block,
        in_specs=[vmem] * 5,
        out_specs=vmem,
        scratch_shapes=[tail],
        compiler_params=PARAMS,
        name="grad_rows",
    )(arrived, factor, gate_weight, up_weight, down_weight)
    returned = lax.all_to_all(going_back, "expert", split_axis=0, concat_axis=0, tiled=True)

    near = [
        [2 * (z_lo * g + i) + c for i in range(z_lo)] for g in range(z_hi) for c in range(2)
    ]
    far = [[2 * (z_lo * i + g) + c for i in range(z_hi)] for g in range(z_lo) for c in range(2)]
    paired = (keep + other.astype(F32)).astype(BF).reshape(z_lo, half // z_lo, width)
    paired = lax.all_to_all(paired, "dp", 0, 0, axis_index_groups=near, tiled=True)
    summed = jnp.sum(paired.astype(F32), axis=0).astype(BF)
    summed = summed.reshape(z_hi, 2 * width // LANES, LANES)
    summed = lax.all_to_all(summed, "dp", 0, 0, axis_index_groups=far, tiled=True)
    grad_down = (jnp.sum(summed.astype(F32), axis=0) * (1.0 / replicas)).reshape(1, 2, width)

    grad_tokens = pl.pallas_call(
        functools.partial(combine_kernel, experts),
        out_shape=shape((tokens, width), BF),
        in_specs=[vmem] * 2,
        out_specs=vmem,
        scratch_shapes=[tail],
        compiler_params=PARAMS,
        name="combine_rows",
    )(pick, returned)
    return (grad_tokens, grad_down)


def solution(mesh):
    placed = (
        P(("dp", "expert"), None),
        P(("dp", "expert"), None),
        P(("dp", "expert"), None),
        P(("dp", "expert"), None),
        P("expert", None, None),
        P("expert", None, None),
        P("expert", None, None),
    )
    return jax.shard_map(
        per_device,
        mesh=mesh,
        in_specs=placed,
        out_specs=(P(("dp", "expert"), None), P("expert", "dp", None)),
        check_vma=False,
    )
```

time: 528 us -> 176 us (0.33)
  the two profiles are of different devices: /device:TPU:1 before, /device:TPU:8 now
where the time goes in v1:
time: 176 us
  waiting for transfers between devices  98.1 us (56%)
  starting transfers between devices  57.4 us (33%)
  local copies, waits for them, and re-layouts  9.9 us (6%)
  Pallas kernels  8.17 us (5%)
    all_to_all x1, waiting for transfers between devices, per_device(): lax.all_to_all(summed, 'dp', 0, 0, axis_index_groups=far, tiled=True)  34.5 us
    all_to_all x1, waiting for transfers between devices, per_device(): lax.all_to_all(going_back, 'expert', split_axis=0, concat_axis=0, tiled=T...  27.3 us
    all_to_all x1, starting transfers between devices, per_device(): lax.all_to_all(summed, 'dp', 0, 0, axis_index_groups=far, tiled=True)  26.6 us
    all_to_all x1, waiting for transfers between devices, per_device(): lax.all_to_all(outgoing, 'expert', split_axis=0, concat_axis=0, tiled=True)  19.4 us
    all_to_all x1, starting transfers between devices, per_device(): lax.all_to_all(outgoing, 'expert', split_axis=0, concat_axis=0, tiled=True)  16.8 us
    all_to_all x1, waiting for transfers between devices, per_device(): lax.all_to_all(paired, 'dp', 0, 0, axis_index_groups=near, tiled=True)  14.3 us
    unnamed x18, local copies, waits for them, and re-layouts  8.44 us
    all_to_all x1, starting transfers between devices, per_device(): lax.all_to_all(paired, 'dp', 0, 0, axis_index_groups=near, tiled=True)  7.27 us
  transfers between devices with their start and end apart: 5, of which 5 were waited for; matrix products, arithmetic and copies ran while one was open for 1% of the time, Pallas kernels for 3%

profile of v1, /device:TPU:8, one launch (start us, length us, event | category | flops | bytes accessed | tf_op | source)
XLA Modules:
  0.0 175.7 jit_solution(17815142122145803531)
XLA Ops:
  0.6 0.8 copy.11.routing_ref
  1.4 0.8 copy.12.weight_ref
  2.2 0.0 copy-start.6
  2.2 1.0 copy-done.6
  3.2 1.1 dispatch_rows.1
  4.2 0.0 copy-start.2
  4.2 1.3 copy-done.2
  5.6 0.0 copy-start.7
  5.6 16.8 %all-to-all-start = ((bf16[16,504,128]{2,1,0:T(8,128)(2,1)}), bf16[16,504,128]{2,1,0:T(8,128)(2,1)S(1)}, u32[]{:S(2)}, u32[]{:S(2)}) async-start(bf16[16,504,128]{2,1,0:T(8,128)(2,1)} %copy-done.2), calls=%async_computation | async-start | bytes 4128768 | tf_op jit(solution)/shard_map/all_to_all | solution.py:170
  22.3 19.4 %all-to-all-done.got_ref = bf16[16,504,128]{2,1,0:T(8,128)(2,1)S(1)} async-done(((bf16[16,504,128]{2,1,0:T(8,128)(2,1)}), bf16[16,504,128]{2,1,0:T(8,128)(2,1)S(1)}, u32[]{:S(2)}, u32[]{:S(2)}) %all-to-all-start) | async-done | bytes 2064416 | tf_op jit(solution)/shard_map/all_to_all | solution.py:170
  41.8 0.0 copy-done.7
  41.8 1.4 down_partial.1
  43.2 0.0 copy-start
  43.2 1.9 %collective-permute-start = (bf16[64,7168]{1,0:T(8,128)(2,1)S(1)}, bf16[64,7168]{1,0:T(8,128)(2,1)S(1)}, u32[]{:S(2)}, u32[]{:S(2)}) collective-permute-start(bf16[64,7168]{1,0:T(8,128)(2,1)S(1)} %get-tuple-element.13), channel_id=1, source_target_pairs={{0,16},{16,0},{32,48},{48,32},{64,80},{80,64},{96,112},{112,96},{1... | collective-permute-start | bytes 2752520 | tf_op jit(solution)/shard_map/ppermute | solution.py:188
  45.1 2.4 %collective-permute-done = bf16[64,7168]{1,0:T(8,128)(2,1)S(1)} collective-permute-done((bf16[64,7168]{1,0:T(8,128)(2,1)S(1)}, bf16[64,7168]{1,0:T(8,128)(2,1)S(1)}, u32[]{:S(2)}, u32[]{:S(2)}) %collective-permute-start) | collective-permute-done | bytes 917536 | tf_op jit(solution)/shard_map/ppermute | solution.py:188
  47.6 1.1 add_convert_fusion
  48.7 0.0 copy-done
  48.7 0.0 copy-start.3
  48.7 7.3 %all-to-all-start.2 = ((bf16[4,16,7168]{2,1,0:T(8,128)(2,1)}), bf16[4,16,7168]{2,1,0:T(8,128)(2,1)S(1)}, u32[]{:S(2)}, u32[]{:S(2)}) async-start(bf16[4,16,7168]{2,1,0:T(8,128)(2,1)} %bitcast.1), calls=%async_computation.2 | async-start | bytes 1835008 | tf_op jit(solution)/shard_map/all_to_all | solution.py:206
  56.0 0.0 copy-done.3
  56.0 0.0 copy-start.1
  56.0 1.6 copy-done.1
  57.5 0.0 copy-start.4
  57.5 1.5 copy-done.4
  59.0 0.0 copy-start.5
  59.0 1.5 copy-done.5
  60.5 4.3 %grad_rows.1 = bf16[16,504,128]{2,1,0:T(8,128)(2,1)} custom-call(bf16[144,7168]{1,0:T(8,128)(2,1)S(1)} %copy-done.1, f32[144,256]{1,0:T(8,128)S(1)} %get-tuple-element.11.factor_ref, bf16[1,7168,128]{2,1,0:T(8,128)(2,1)S(1)} %copy-done.3, bf16[1,7168,128]{2,1,0:T(8,128)(2,1)S(1)} %copy-done.4, bf16[1,128,7168]{2,1,0:T(8,128)(2,1)S(1)} %copy-done.5), custom_call_target="tpu_custom_call" | custom-call | tf_op jit(solution)/shard_map/grad_rows/pallas_call | solution.py:190
  64.8 14.3 %all-to-all-done.2 = bf16[4,16,7168]{2,1,0:T(8,128)(2,1)S(1)} async-done(((bf16[4,16,7168]{2,1,0:T(8,128)(2,1)}), bf16[4,16,7168]{2,1,0:T(8,128)(2,1)S(1)}, u32[]{:S(2)}, u32[]{:S(2)}) %all-to-all-start.2) | async-done | bytes 917536 | tf_op jit(solution)/shard_map/all_to_all | solution.py:206
  79.2 4.9 %all-to-all-start.1 = ((bf16[16,504,128]{2,1,0:T(8,128)(2,1)}), bf16[16,504,128]{2,1,0:T(8,128)(2,1)S(1)}, u32[]{:S(2)}, u32[]{:S(2)}) async-start(bf16[16,504,128]{2,1,0:T(8,128)(2,1)} %grad_rows.1), calls=%async_computation.1 | async-start | bytes 4128768 | tf_op jit(solution)/shard_map/all_to_all | solution.py:199
  84.1 0.2 reduce_sum.21
  84.3 0.8 reshape.28
  85.1 27.3 %all-to-all-done.1.got_ref = bf16[16,504,128]{2,1,0:T(8,128)(2,1)S(1)} async-done(((bf16[16,504,128]{2,1,0:T(8,128)(2,1)}), bf16[16,504,128]{2,1,0:T(8,128)(2,1)S(1)}, u32[]{:S(2)}, u32[]{:S(2)}) %all-to-all-start.1) | async-done | bytes 2064416 | tf_op jit(solution)/shard_map/all_to_all | solution.py:199
  112.4 26.6 %all-to-all-start.3 = ((bf16[8,112,128]{2,1,0:T(8,128)(2,1)}), bf16[8,112,128]{2,1,0:T(8,128)(2,1)S(1)}, u32[]{:S(2)}, u32[]{:S(2)}) async-start(bf16[8,112,128]{2,1,0:T(8,128)(2,1)} %reshape.28), calls=%async_computation.3 | async-start | bytes 458752 | tf_op jit(solution)/shard_map/all_to_all | solution.py:209
  139.0 1.4 combine_rows.1
  140.4 34.5 %all-to-all-done.3 = bf16[8,112,128]{2,1,0:T(8,128)(2,1)S(1)} async-done(((bf16[8,112,128]{2,1,0:T(8,128)(2,1)}), bf16[8,112,128]{2,1,0:T(8,128)(2,1)S(1)}, u32[]{:S(2)}, u32[]{:S(2)}) %all-to-all-start.3) | async-done | bytes 229408 | tf_op jit(solution)/shard_map/all_to_all | solution.py:209
  175.0 0.7 mul.18
  (2 shorter events, 0.0 us)
Async XLA Ops:
  2.2 1.0 copy-start.6
  4.2 1.3 copy-start.2
  5.6 36.2 %copy-start.7 = (bf16[144,256]{1,0:T(8,128)(2,1)S(1)}, bf16[144,256]{1,0:T(8,128)(2,1)}, u32[]{:S(2)}) copy-start(bf16[144,256]{1,0:T(8,128)(2,1)} %pre_ref.1) | copy-start | bytes 221188
  5.6 36.2 %all-to-all-start = ((bf16[16,504,128]{2,1,0:T(8,128)(2,1)}), bf16[16,504,128]{2,1,0:T(8,128)(2,1)S(1)}, u32[]{:S(2)}, u32[]{:S(2)}) async-start(bf16[16,504,128]{2,1,0:T(8,128)(2,1)} %copy-done.2), calls=%async_computation | async-start | bytes 4128768 | tf_op jit(solution)/shard_map/all_to_all | solution.py:170
  43.2 5.5 %copy-start = (bf16[144,7168]{1,0:T(8,128)(2,1)}, bf16[144,7168]{1,0:T(8,128)(2,1)S(1)}, u32[]{:S(2)}) copy-start(bf16[144,7168]{1,0:T(8,128)(2,1)S(1)} %get-tuple-element.10.arrived_ref) | copy-start | bytes 6193156
  43.2 4.4 %collective-permute-start = (bf16[64,7168]{1,0:T(8,128)(2,1)S(1)}, bf16[64,7168]{1,0:T(8,128)(2,1)S(1)}, u32[]{:S(2)}, u32[]{:S(2)}) collective-permute-start(bf16[64,7168]{1,0:T(8,128)(2,1)S(1)} %get-tuple-element.13), channel_id=1, source_target_pairs={{0,16},{16,0},{32,48},{48,32},{64,80},{80,64},{96,112},{112,96},{1... | collective-permute-start | bytes 2752520 | tf_op jit(solution)/shard_map/ppermute | solution.py:188
  48.7 7.3 %copy-start.3 = (bf16[1,7168,128]{2,1,0:T(8,128)(2,1)S(1)}, bf16[1,7168,128]{2,1,0:T(8,128)(2,1)}, u32[]{:S(2)}) copy-start(bf16[1,7168,128]{2,1,0:T(8,128)(2,1)} %gate_ref.1) | copy-start | bytes 5505028
  48.7 30.5 %all-to-all-start.2 = ((bf16[4,16,7168]{2,1,0:T(8,128)(2,1)}), bf16[4,16,7168]{2,1,0:T(8,128)(2,1)S(1)}, u32[]{:S(2)}, u32[]{:S(2)}) async-start(bf16[4,16,7168]{2,1,0:T(8,128)(2,1)} %bitcast.1), calls=%async_computation.2 | async-start | bytes 1835008 | tf_op jit(solution)/shard_map/all_to_all | solution.py:206
  56.0 1.6 copy-start.1
  57.5 1.5 copy-start.4
  59.0 1.5 copy-start.5
  79.2 33.3 %all-to-all-start.1 = ((bf16[16,504,128]{2,1,0:T(8,128)(2,1)}), bf16[16,504,128]{2,1,0:T(8,128)(2,1)S(1)}, u32[]{:S(2)}, u32[]{:S(2)}) async-start(bf16[16,504,128]{2,1,0:T(8,128)(2,1)} %grad_rows.1), calls=%async_computation.1 | async-start | bytes 4128768 | tf_op jit(solution)/shard_map/all_to_all | solution.py:199
  112.4 62.5 %all-to-all-start.3 = ((bf16[8,112,128]{2,1,0:T(8,128)(2,1)}), bf16[8,112,128]{2,1,0:T(8,128)(2,1)S(1)}, u32[]{:S(2)}, u32[]{:S(2)}) async-start(bf16[8,112,128]{2,1,0:T(8,128)(2,1)} %reshape.28), calls=%async_computation.3 | async-start | bytes 458752 | tf_op jit(solution)/shard_map/all_to_all | solution.py:209

commit v2 on v1

--- a/solution.py
+++ b/solution.py
@@ -11,7 +11,7 @@
 F32 = jnp.float32
 LANES = 128
 FIRST = 8
-PARAMS = pltpu.CompilerParams(vmem_limit_bytes=40 * 1024 * 1024)
+PARAMS = pltpu.CompilerParams(vmem_limit_bytes=16 * 1024 * 1024)
 
 
 def dot(a, b, contract):
@@ -40,39 +40,59 @@
     return jnp.concatenate(halves, axis=1)
 
 
-def dispatch_kernel(experts, dy_ref, routing_ref, weight_ref, out_ref, pick_ref, tail):
+def dispatch_kernel(
+    experts, dy_hbm, routing_hbm, weight_hbm, out_hbm, pick_ref, dy_ref, routing_ref, weight_ref, out_ref, tail, sems
+):
+    loads = [
+        pltpu.make_async_copy(source, target, sems.at[i])
+        for i, (source, target) in enumerate(
+            [(routing_hbm, routing_ref), (weight_hbm, weight_ref), (dy_hbm, dy_ref)]
+        )
+    ]
+    for load in loads:
+        load.start()
+    loads[0].wait()
+    loads[1].wait()
     tokens, width = dy_ref.shape
-    route_count = routing_ref.shape[1]
-    main = experts * FIRST
-    lanes = pick_ref.shape[1]
-    slot = iota((tokens, lanes), 1)
+    route_count = routing_ref.shape[0]
+    main = experts * FIRST
+    rows = main + experts
+    slot = iota((rows, tokens), 0)
     expert = jnp.where(slot < main, slot // FIRST, slot - main)
     position = jnp.where(slot < main, slot % FIRST, FIRST)
-    named = jnp.zeros((tokens, lanes), F32)
-    scale = jnp.zeros((tokens, lanes), F32)
+    named = jnp.zeros((rows, tokens), F32)
+    scale = jnp.zeros((rows, tokens), F32)
     for k in range(route_count):
-        hit = routing_ref[:, k : k + 1] == expert
+        hit = routing_ref[k : k + 1, :] == expert
         named = named + jnp.where(hit, 1.0, 0.0)
-        scale = scale + jnp.where(hit, weight_ref[:, k : k + 1], 0.0)
-    earlier = jnp.where(iota((tokens, tokens), 1) < iota((tokens, tokens), 0), 1.0, 0.0)
-    before = dot(earlier.astype(BF), named.astype(BF), ((1,), (0,)))
+        scale = scale + jnp.where(hit, weight_ref[k : k + 1, :], 0.0)
+    earlier = jnp.where(iota((tokens, tokens), 0) < iota((tokens, tokens), 1), 1.0, 0.0)
+    before = dot(named.astype(BF), earlier.astype(BF), ((1,), (0,)))
     pick = jnp.where((named > 0.5) & (before == position.astype(F32)), 1.0, 0.0)
-    pick_ref[...] = pick.astype(BF)
-    rows = main + experts
-    chosen = pick[:, :rows].astype(BF)
-    rest = (pick * scale)[:, :rows]
-    ones = jnp.ones((tokens, LANES), BF)
-    row_weight = jnp.zeros((rows, LANES), F32)
-    for _ in range(3):
-        piece = rest.astype(BF)
-        row_weight = row_weight + dot(piece, ones, ((0,), (0,)))
-        rest = rest - piece.astype(F32)
-    row_weight = jnp.concatenate([row_weight, row_weight], axis=1)
-    for pair in range(width // (2 * LANES)):
-        part = dot(chosen, dy_ref[:, pair * 2 * LANES : (pair + 1) * 2 * LANES], ((0,), (0,)))
+    chosen = pick.astype(BF)
+    pick_ref[...] = chosen
+    row_weight = jnp.sum(pick * scale, axis=1, keepdims=True)
+    pairs = width // (2 * LANES)
+    parts = 4
+    stores = []
+    loads[2].wait()
+    for pair in range(pairs):
+        part = dot(chosen, dy_ref[:, pair * 2 * LANES : (pair + 1) * 2 * LANES], ((1,), (0,)))
         part = part * row_weight
         write_block(out_ref, tail, pair, part[:, :LANES], part[:, LANES:], experts)
-    out_ref[:, experts_rows(width) :, :] = tail[...].astype(BF)
+        if (pair + 1) % (pairs // parts) == 0:
+            rows_of = slice(len(stores) * pairs // parts * 16, (pair + 1) * 16)
+            if pair + 1 == pairs:
+                out_ref[:, experts_rows(width) :, :] = tail[...].astype(BF)
+                rows_of = slice(rows_of.start, out_ref.shape[1])
+            stores.append(
+                pltpu.make_async_copy(
+                    out_ref.at[:, rows_of, :], out_hbm.at[:, rows_of, :], sems.at[3 + len(stores)]
+                )
+            )
+            stores[-1].start()
+    for store in stores:
+        store.wait()
 
 
 def experts_rows(width):
@@ -80,7 +100,7 @@
 
 
 def partial_kernel(
-    experts, z_lo, own_ref, got_ref, pre_ref, arrived_ref, keep_ref, send_ref, factor_ref, tail
+    experts, chips, at_ref, got_ref, pre_ref, arrived_ref, keep_ref, send_ref, factor_ref, tail
 ):
     rows, width = arrived_ref.shape
     hidden_units = pre_ref.shape[1] // 2
@@ -99,11 +119,16 @@
     factor_ref[:, hidden_units:] = activated
     hidden = (activated * up_pre).astype(BF)
     half = hidden_units // 2
-    block = half // z_lo
     unit, at = iota((hidden_units, hidden_units), 0), iota((hidden_units, hidden_units), 1)
-    core = jnp.where(at < half, own_ref[0], 1 - own_ref[0])
-    r = at % half
-    target = 4 * (z_lo * ((r % block) // 2) + r // block) + 2 * core + r % 2
+    core = jnp.where(at < half, at_ref[1], 1 - at_ref[1])
+    share = half // chips
+    place = at % half // share
+    far = jnp.zeros_like(place)
+    bits = chips.bit_length() - 1
+    for bit in range(bits):
+        far = far + (place // 2**bit) % 2 * 2 ** (bits - 1 - bit)
+    chip = (at_ref[0] + (1 - 2 * core) * far + chips) % chips
+    target = (2 * chip + core) * share + at % share
     hidden = dot(hidden, jnp.where(unit == target, 1.0, 0.0).astype(BF), ((1,), (0,))).astype(BF)
     tail[...] = got_ref[:, experts_rows(width) :, :].astype(F32)
     for pair in range(width // (2 * LANES)):
@@ -132,11 +157,11 @@
 def combine_kernel(experts, pick_ref, got_ref, out_ref, tail):
     width = out_ref.shape[1]
     tail[...] = got_ref[:, experts_rows(width) :, :].astype(F32)
-    pick = pick_ref[:, : experts * (FIRST + 1)]
+    pick = pick_ref[...]
     for pair in range(width // (2 * LANES)):
         rows = read_block(got_ref, tail, pair, experts).astype(BF)
         out_ref[:, pair * 2 * LANES : (pair + 1) * 2 * LANES] = dot(
-            pick, rows, ((1,), (0,))
+            pick, rows, ((0,), (0,))
         ).astype(BF)
 
 
@@ -150,8 +175,7 @@
     assert capacity == FIRST + 1
     block_rows = capacity * width // LANES
     chips = replicas // 2
-    z_lo = 4
-    z_hi = chips // z_lo
+    assert chips & (chips - 1) == 0 and hidden_units % replicas == 0
     shape = jax.ShapeDtypeStruct
     vmem = pl.BlockSpec(memory_space=pltpu.VMEM)
     smem = pl.BlockSpec(memory_space=pltpu.SMEM)
@@ -160,19 +184,26 @@
 
     outgoing, pick = pl.pallas_call(
         functools.partial(dispatch_kernel, experts),
-        out_shape=(block, shape((tokens, 2 * LANES), BF)),
-        in_specs=[vmem] * 3,
-        out_specs=(vmem, vmem),
-        scratch_shapes=[tail],
+        out_shape=(pltpu.HBM(block.shape, BF), shape((rows, tokens), BF)),
+        in_specs=[pl.BlockSpec(memory_space=pl.ANY)] * 3,
+        out_specs=(pl.BlockSpec(memory_space=pltpu.HBM), vmem),
+        scratch_shapes=[
+            pltpu.VMEM((tokens, width), BF),
+            pltpu.VMEM(routing.T.shape, jnp.int32),
+            pltpu.VMEM(route_weight.T.shape, F32),
+            pltpu.VMEM((experts, block_rows, LANES), BF),
+            tail,
+            pltpu.SemaphoreType.DMA((7,)),
+        ],
         compiler_params=PARAMS,
         name="dispatch_rows",
-    )(dy_tokens, routing, route_weight)
+    )(*(pltpu.with_memory_space_constraint(x, pltpu.HBM) for x in (dy_tokens, routing.T, route_weight.T)))
     got = lax.all_to_all(outgoing, "expert", split_axis=0, concat_axis=0, tiled=True)
 
-    core = lax.axis_index("dp") % 2
+    own = lax.axis_index("dp")
     half = hidden_units // 2
     arrived, keep, send, factor = pl.pallas_call(
-        functools.partial(partial_kernel, experts, z_lo),
+        functools.partial(partial_kernel, experts, chips),
         out_shape=(
             shape((rows, width), BF),
             shape((half, width), F32),
@@ -184,7 +215,7 @@
         scratch_shapes=[tail],
         compiler_params=PARAMS,
         name="down_partial",
-    )(core.reshape(1), got, pre_act)
+    )(jnp.stack([own // 2, own % 2]), got, pre_act)
     other = lax.ppermute(send, "dp", [(i, i ^ 1) for i in range(replicas)])
 
     going_back = pl.pallas_call(
@@ -198,17 +229,6 @@
     )(arrived, factor, gate_weight, up_weight, down_weight)
     returned = lax.all_to_all(going_back, "expert", split_axis=0, concat_axis=0, tiled=True)
 
-    near = [
-        [2 * (z_lo * g + i) + c for i in range(z_lo)] for g in range(z_hi) for c in range(2)
-    ]
-    far = [[2 * (z_lo * i + g) + c for i in range(z_hi)] for g in range(z_lo) for c in range(2)]
-    paired = (keep + other.astype(F32)).astype(BF).reshape(z_lo, half // z_lo, width)
-    paired = lax.all_to_all(paired, "dp", 0, 0, axis_index_groups=near, tiled=True)
-    summed = jnp.sum(paired.astype(F32), axis=0).astype(BF)
-    summed = summed.reshape(z_hi, 2 * width // LANES, LANES)
-    summed = lax.all_to_all(summed, "dp", 0, 0, axis_index_groups=far, tiled=True)
-    grad_down = (jnp.sum(summed.astype(F32), axis=0) * (1.0 / replicas)).reshape(1, 2, width)
-
     grad_tokens = pl.pallas_call(
         functools.partial(combine_kernel, experts),
         out_shape=shape((tokens, width), BF),
@@ -218,6 +238,23 @@
         compiler_params=PARAMS,
         name="combine_rows",
     )(pick, returned)
+    terms, count, distance = [keep, other], half, 1
+    while distance < chips:
+        count //= 2
+        going = functools.reduce(jnp.add, [t[count:].astype(F32) for t in terms]).astype(BF)
+        if 2 * distance == chips:
+            going, grad_tokens = lax.optimization_barrier((going, grad_tokens))
+        hops = [
+            (2 * z + c, 2 * ((z + (distance if c == 0 else -distance)) % chips) + c)
+            for z in range(chips)
+            for c in range(2)
+        ]
+        coming = lax.ppermute(going, "dp", hops)
+        terms = [t[:count] for t in terms] + [coming]
+        distance *= 2
+    grad_down = functools.reduce(jnp.add, [t.astype(F32) for t in terms]) * (1.0 / replicas)
+    grad_down = grad_down[None]
+
     return (grad_tokens, grad_down)
 
 

time: 176 us -> 155 us (0.88)
  starting transfers between devices: 57.4 us -> 46.8 us
  local copies, waits for them, and re-layouts: 9.9 us -> 0.03 us
  waiting for transfers between devices: 98.1 us -> 90.8 us
  other arithmetic: 1.37 us -> 5.82 us
  Pallas kernels: 8.17 us -> 10.4 us
    ppermute x0 -> x5, waiting for transfers between devices: none -> 59.9 us  [per_device(): coming = lax.ppermute(going, 'dp', hops)]
    all_to_all x2 -> x0, waiting for transfers between devices: 48.9 us -> none  [the longest x1 34.5 us: per_device(): lax.all_to_all(summed, 'dp', 0, 0, axis_index_groups=far, tiled=True)]
    all_to_all x2 -> x0, starting transfers between devices: 33.9 us -> none  [the longest x1 26.6 us: per_device(): lax.all_to_all(summed, 'dp', 0, 0, axis_index_groups=far, tiled=True)]
    ppermute x0 -> x5, starting transfers between devices: none -> 23.3 us  [per_device(): coming = lax.ppermute(going, 'dp', hops)]
    all_to_all x1, waiting for transfers between devices: 27.3 us -> 9.04 us  [per_device(): lax.all_to_all(going_back, 'expert', split_axis=0, concat_axis=0, tiled=T...]
    unnamed x18 -> x14, local copies, waits for them, and re-layouts: 8.44 us -> 0.03 us
    convert_element_type x1 -> x5, other arithmetic: 1.11 us -> 3.94 us  [per_device(): functools.reduce(jnp.add, [t[count:].astype(F32) for t in terms]).astype(BF)]
    pallas_call x2, Pallas kernels: 2.48 us -> 4.72 us  [the longest x1 2.74 us: per_device(): pl.pallas_call(functools.partial(dispatch_kernel, experts), out_shape=(pl...]
  transfers between devices with their start and end apart: 5 -> 8, of which waited for: 5 -> 8; matrix products, arithmetic and copies ran while one was open for 1% -> 2% of each run, Pallas kernels for 3% -> 3%
where the time goes in v2:
time: 155 us
  waiting for transfers between devices  90.8 us (59%)
  starting transfers between devices  46.8 us (30%)
  Pallas kernels  10.4 us (7%)
  other arithmetic  5.82 us (4%)
    ppermute x5, waiting for transfers between devices, per_device(): coming = lax.ppermute(going, 'dp', hops)  59.9 us
    ppermute x5, starting transfers between devices, per_device(): coming = lax.ppermute(going, 'dp', hops)  23.3 us
    all_to_all x1, waiting for transfers between devices, per_device(): lax.all_to_all(outgoing, 'expert', split_axis=0, concat_axis=0, tiled=True)  19.4 us
    all_to_all x1, starting transfers between devices, per_device(): lax.all_to_all(outgoing, 'expert', split_axis=0, concat_axis=0, tiled=True)  16.8 us
    all_to_all x1, waiting for transfers between devices, per_device(): lax.all_to_all(going_back, 'expert', split_axis=0, concat_axis=0, tiled=T...  9.04 us
    all_to_all x1, starting transfers between devices, per_device(): lax.all_to_all(going_back, 'expert', split_axis=0, concat_axis=0, tiled=T...  4.89 us
    pallas_call x1, Pallas kernels, per_device(): pl.pallas_call(functools.partial(grad_kernel, experts), out_shape=block,...  4.3 us
    convert_element_type x5, other arithmetic, per_device(): functools.reduce(jnp.add, [t[count:].astype(F32) for t in terms]).astype(BF)  3.94 us
  transfers between devices with their start and end apart: 8, of which 8 were waited for; matrix products, arithmetic and copies ran while one was open for 2% of the time, Pallas kernels for 3%

profile of v2, /device:TPU:8, one launch (start us, length us, event | category | flops | bytes accessed | tf_op | source)
XLA Modules:
  0.0 154.7 jit_solution(12700882941104215793)
XLA Ops:
  0.6 2.7 %dispatch_rows.1 = (bf16[16,504,128]{2,1,0:T(8,128)(2,1)}, bf16[144,32]{1,0:T(8,128)(2,1)S(1)}) custom-call(bf16[32,7168]{1,0:T(8,128)(2,1)} %dy_hbm.1, s32[4,32]{1,0:T(4,128)} %bitcast.6, f32[4,32]{1,0:T(4,128)} %bitcast.7), custom_call_target="tpu_custom_call" | custom-call | tf_op jit(solution)/shard_map/dispatch_rows/pallas_call | solution.py:185
  3.4 0.0 copy-start.4
  3.4 16.8 %all-to-all-start = ((bf16[16,504,128]{2,1,0:T(8,128)(2,1)}), bf16[16,504,128]{2,1,0:T(8,128)(2,1)S(1)}, u32[]{:S(2)}, u32[]{:S(2)}) async-start(bf16[16,504,128]{2,1,0:T(8,128)(2,1)} %get-tuple-element.10), calls=%async_computation | async-start | bytes 4128768 | tf_op jit(solution)/shard_map/all_to_all | solution.py:201
  20.2 0.1 pad_add_fusion.at_ref
  20.2 19.4 %all-to-all-done.got_ref = bf16[16,504,128]{2,1,0:T(8,128)(2,1)S(1)} async-done(((bf16[16,504,128]{2,1,0:T(8,128)(2,1)}), bf16[16,504,128]{2,1,0:T(8,128)(2,1)S(1)}, u32[]{:S(2)}, u32[]{:S(2)}) %all-to-all-start) | async-done | bytes 2064416 | tf_op jit(solution)/shard_map/all_to_all | solution.py:201
  39.6 0.0 copy-done.4
  39.6 0.0 copy-start.2
  39.6 2.0 %down_partial.1 = (bf16[144,7168]{1,0:T(8,128)(2,1)S(1)}, f32[64,7168]{1,0:T(8,128)S(1)}, bf16[64,7168]{1,0:T(8,128)(2,1)S(1)}, f32[144,256]{1,0:T(8,128)S(1)}) custom-call(s32[2]{0:T(128)S(1)} %pad_add_fusion.at_ref, bf16[16,504,128]{2,1,0:T(8,128)(2,1)S(1)} %all-to-all-done.got_ref, bf16[144,256]{1,0:T(8,128)(2,1)S(1)} %copy-done.4), custom_call_target="tpu_custom_call" | custom-call | tf_op jit(solution)/shard_map/down_partial/pallas_call | solution.py:205
  41.6 0.0 copy-start.3
  41.6 1.9 %collective-permute-start = (bf16[64,7168]{1,0:T(8,128)(2,1)S(1)}, bf16[64,7168]{1,0:T(8,128)(2,1)S(1)}, u32[]{:S(2)}, u32[]{:S(2)}) collective-permute-start(bf16[64,7168]{1,0:T(8,128)(2,1)S(1)} %get-tuple-element.12), channel_id=1, source_target_pairs={{0,16},{16,0},{32,48},{48,32},{64,80},{80,64},{96,112},{112,96},{1... | collective-permute-start | bytes 2752520 | tf_op jit(solution)/shard_map/ppermute | solution.py:219
  43.5 2.4 %collective-permute-done = bf16[64,7168]{1,0:T(8,128)(2,1)S(1)} collective-permute-done((bf16[64,7168]{1,0:T(8,128)(2,1)S(1)}, bf16[64,7168]{1,0:T(8,128)(2,1)S(1)}, u32[]{:S(2)}, u32[]{:S(2)}) %collective-permute-start) | collective-permute-done | bytes 917536 | tf_op jit(solution)/shard_map/ppermute | solution.py:219
  46.0 0.0 copy-start
  46.0 0.0 copy-start.1
  46.0 0.1 add_convert_fusion
  46.0 5.4 %collective-permute-start.1 = (bf16[32,7168]{1,0:T(8,128)(2,1)S(1)}, bf16[32,7168]{1,0:T(8,128)(2,1)S(1)}, u32[]{:S(2)}, u32[]{:S(2)}) collective-permute-start(bf16[32,7168]{1,0:T(8,128)(2,1)S(1)} %add_convert_fusion), channel_id=1, source_target_pairs={{0,32},{16,1008},{32,64},{48,16},{64,96},{80,48},{96,128},{112,80}... | collective-permute-start | bytes 1376264 | tf_op jit(solution)/shard_map/ppermute | solution.py:252
  51.4 21.3 %collective-permute-done.1 = bf16[32,7168]{1,0:T(8,128)(2,1)S(1)} collective-permute-done((bf16[32,7168]{1,0:T(8,128)(2,1)S(1)}, bf16[32,7168]{1,0:T(8,128)(2,1)S(1)}, u32[]{:S(2)}, u32[]{:S(2)}) %collective-permute-start.1) | collective-permute-done | bytes 458784 | tf_op jit(solution)/shard_map/ppermute | solution.py:252
  72.7 0.1 add_convert_fusion.1
  72.8 1.9 %collective-permute-start.2 = (bf16[16,7168]{1,0:T(8,128)(2,1)S(1)}, bf16[16,7168]{1,0:T(8,128)(2,1)S(1)}, u32[]{:S(2)}, u32[]{:S(2)}) collective-permute-start(bf16[16,7168]{1,0:T(8,128)(2,1)S(1)} %add_convert_fusion.1), channel_id=1, source_target_pairs={{0,64},{16,976},{32,96},{48,1008},{64,128},{80,16},{96,160},{112,4... | collective-permute-start | bytes 688136 | tf_op jit(solution)/shard_map/ppermute | solution.py:252
  74.7 10.4 %collective-permute-done.2 = bf16[16,7168]{1,0:T(8,128)(2,1)S(1)} collective-permute-done((bf16[16,7168]{1,0:T(8,128)(2,1)S(1)}, bf16[16,7168]{1,0:T(8,128)(2,1)S(1)}, u32[]{:S(2)}, u32[]{:S(2)}) %collective-permute-start.2) | collective-permute-done | bytes 229408 | tf_op jit(solution)/shard_map/ppermute | solution.py:252
  85.1 0.0 copy-start.5
  85.1 0.7 add_convert_fusion.2
  85.8 0.0 copy-done.3
  85.8 1.9 %collective-permute-start.3 = (bf16[8,7168]{1,0:T(8,128)(2,1)}, bf16[8,7168]{1,0:T(8,128)(2,1)}, u32[]{:S(2)}, u32[]{:S(2)}) collective-permute-start(bf16[8,7168]{1,0:T(8,128)(2,1)} %add_convert_fusion.2), channel_id=1, source_target_pairs={{0,128},{16,912},{32,160},{48,944},{64,192},{80,976},{96,224},{112... | collective-permute-start | bytes 344072 | tf_op jit(solution)/shard_map/ppermute | solution.py:252
  87.8 0.0 copy-done.5
  87.8 0.0 copy-done.2
  87.8 0.0 copy-done
  87.8 0.0 copy-done.1
  87.8 4.3 %grad_rows.1 = bf16[16,504,128]{2,1,0:T(8,128)(2,1)} custom-call(bf16[144,7168]{1,0:T(8,128)(2,1)S(1)} %get-tuple-element.14.arrived_ref, f32[144,256]{1,0:T(8,128)S(1)} %get-tuple-element.15.factor_ref, bf16[1,7168,128]{2,1,0:T(8,128)(2,1)S(1)} %copy-done, bf16[1,7168,128]{2,1,0:T(8,128)(2,1)S(1)} %copy-done.1, bf16[1,128,7168]{2,1,0:T(8,128)(2,1)S(1)} %copy-done.2), custom_call_target="tpu_custom_call" | custom-call | tf_op jit(solution)/shard_map/grad_rows/pallas_call | solution.py:221
  92.1 4.9 %all-to-all-start.1 = ((bf16[16,504,128]{2,1,0:T(8,128)(2,1)}), bf16[16,504,128]{2,1,0:T(8,128)(2,1)S(1)}, u32[]{:S(2)}, u32[]{:S(2)}) async-start(bf16[16,504,128]{2,1,0:T(8,128)(2,1)} %grad_rows.1), calls=%async_computation.1 | async-start | bytes 4128768 | tf_op jit(solution)/shard_map/all_to_all | solution.py:230
  97.0 3.4 %collective-permute-done.3 = bf16[8,7168]{1,0:T(8,128)(2,1)} collective-permute-done((bf16[8,7168]{1,0:T(8,128)(2,1)}, bf16[8,7168]{1,0:T(8,128)(2,1)}, u32[]{:S(2)}, u32[]{:S(2)}) %collective-permute-start.3) | collective-permute-done | bytes 114720 | tf_op jit(solution)/shard_map/ppermute | solution.py:252
  100.4 1.2 add_convert_fusion.3
  101.6 4.1 %collective-permute-start.4 = (bf16[4,7168]{1,0:T(4,128)(2,1)S(1)}, bf16[4,7168]{1,0:T(4,128)(2,1)S(1)}, u32[]{:S(2)}, u32[]{:S(2)}) collective-permute-start(bf16[4,7168]{1,0:T(4,128)(2,1)S(1)} %add_convert_fusion.3), channel_id=1, source_target_pairs={{0,256},{16,784},{32,288},{48,816},{64,320},{80,848},{96,352},{112... | collective-permute-start | bytes 172040 | tf_op jit(solution)/shard_map/ppermute | solution.py:252
  105.8 10.7 %collective-permute-done.4 = bf16[4,7168]{1,0:T(4,128)(2,1)S(1)} collective-permute-done((bf16[4,7168]{1,0:T(4,128)(2,1)S(1)}, bf16[4,7168]{1,0:T(4,128)(2,1)S(1)}, u32[]{:S(2)}, u32[]{:S(2)}) %collective-permute-start.4) | collective-permute-done | bytes 57376 | tf_op jit(solution)/shard_map/ppermute | solution.py:252
  116.4 1.9 %add_convert_fusion.4 = bf16[2,7168]{1,0:T(2,128)(2,1)} fusion(f32[64,7168]{1,0:T(8,128)} %copy-done.3, bf16[4,7168]{1,0:T(4,128)(2,1)S(1)} %collective-permute-done.4, bf16[8,7168]{1,0:T(8,128)(2,1)} %collective-permute-done.3, bf16[16,7168]{1,0:T(8,128)(2,1)} %copy-done.5, bf16[32,7168]{1,0:T(8,128)(2,1)S(1)} %collective-permute-done.1, ...), kind=kLoop, calls=%fused_computation.5 | loop fusion | flops 157696 | bytes 229376 | tf_op jit(solution)/shard_map/convert_element_type | solution.py:244
  118.3 9.0 %all-to-all-done.1.got_ref = bf16[16,504,128]{2,1,0:T(8,128)(2,1)S(1)} async-done(((bf16[16,504,128]{2,1,0:T(8,128)(2,1)}), bf16[16,504,128]{2,1,0:T(8,128)(2,1)S(1)}, u32[]{:S(2)}, u32[]{:S(2)}) %all-to-all-start.1) | async-done | bytes 2064416 | tf_op jit(solution)/shard_map/all_to_all | solution.py:230
  127.3 0.0 copy-start.6
  127.3 1.4 combine_rows.1
  128.8 0.0 copy-done.6
  128.8 9.9 %collective-permute-start.5 = (bf16[2,7168]{1,0:T(2,128)(2,1)S(1)}, bf16[2,7168]{1,0:T(2,128)(2,1)S(1)}, u32[]{:S(2)}, u32[]{:S(2)}) collective-permute-start(bf16[2,7168]{1,0:T(2,128)(2,1)S(1)} %copy-done.6), channel_id=1, source_target_pairs={{0,512},{16,528},{32,544},{48,560},{64,576},{80,592},{96,608},{112... | collective-permute-start | bytes 86024 | tf_op jit(solution)/shard_map/ppermute | solution.py:252
  138.7 14.2 %collective-permute-done.5 = bf16[2,7168]{1,0:T(2,128)(2,1)S(1)} collective-permute-done((bf16[2,7168]{1,0:T(2,128)(2,1)S(1)}, bf16[2,7168]{1,0:T(2,128)(2,1)S(1)}, u32[]{:S(2)}, u32[]{:S(2)}) %collective-permute-start.5) | collective-permute-done | bytes 28704 | tf_op jit(solution)/shard_map/ppermute | solution.py:252
  152.9 1.8 %multiply_bitcast_fusion = f32[1,2,7168]{2,1,0:T(2,128)} fusion(bf16[2,7168]{1,0:T(2,128)(2,1)S(1)} %collective-permute-done.5, f32[64,7168]{1,0:T(8,128)} %copy-done.3, bf16[4,7168]{1,0:T(4,128)(2,1)S(1)} %collective-permute-done.4, bf16[8,7168]{1,0:T(8,128)(2,1)} %collective-permute-done.3, bf16[16,7168]{1,0:T(8,128)(2,1)} %copy-done.5, ...), kind=kLoop, calls=%fused_computation.4 | loop fusion | flops 186368 | bytes 286720 | tf_op jit(solution)/shard_map/broadcast_in_dim | solution.py:256
Async XLA Ops:
  3.4 36.2 %copy-start.4 = (bf16[144,256]{1,0:T(8,128)(2,1)S(1)}, bf16[144,256]{1,0:T(8,128)(2,1)}, u32[]{:S(2)}) copy-start(bf16[144,256]{1,0:T(8,128)(2,1)} %pre_ref.1) | copy-start | bytes 221188
  3.4 36.2 %all-to-all-start = ((bf16[16,504,128]{2,1,0:T(8,128)(2,1)}), bf16[16,504,128]{2,1,0:T(8,128)(2,1)S(1)}, u32[]{:S(2)}, u32[]{:S(2)}) async-start(bf16[16,504,128]{2,1,0:T(8,128)(2,1)} %get-tuple-element.10), calls=%async_computation | async-start | bytes 4128768 | tf_op jit(solution)/shard_map/all_to_all | solution.py:201
  39.6 48.2 %copy-start.2 = (bf16[1,128,7168]{2,1,0:T(8,128)(2,1)S(1)}, bf16[1,128,7168]{2,1,0:T(8,128)(2,1)}, u32[]{:S(2)}) copy-start(bf16[1,128,7168]{2,1,0:T(8,128)(2,1)} %down_ref.1) | copy-start | bytes 5505028
  41.6 44.2 %copy-start.3 = (f32[64,7168]{1,0:T(8,128)}, f32[64,7168]{1,0:T(8,128)S(1)}, u32[]{:S(2)}) copy-start(f32[64,7168]{1,0:T(8,128)S(1)} %get-tuple-element.11) | copy-start | bytes 5505028
  41.6 4.4 %collective-permute-start = (bf16[64,7168]{1,0:T(8,128)(2,1)S(1)}, bf16[64,7168]{1,0:T(8,128)(2,1)S(1)}, u32[]{:S(2)}, u32[]{:S(2)}) collective-permute-start(bf16[64,7168]{1,0:T(8,128)(2,1)S(1)} %get-tuple-element.12), channel_id=1, source_target_pairs={{0,16},{16,0},{32,48},{48,32},{64,80},{80,64},{96,112},{112,96},{1... | collective-permute-start | bytes 2752520 | tf_op jit(solution)/shard_map/ppermute | solution.py:219
  46.0 41.8 %copy-start = (bf16[1,7168,128]{2,1,0:T(8,128)(2,1)S(1)}, bf16[1,7168,128]{2,1,0:T(8,128)(2,1)}, u32[]{:S(2)}) copy-start(bf16[1,7168,128]{2,1,0:T(8,128)(2,1)} %gate_ref.1) | copy-start | bytes 5505028
  46.0 41.8 %copy-start.1 = (bf16[1,7168,128]{2,1,0:T(8,128)(2,1)S(1)}, bf16[1,7168,128]{2,1,0:T(8,128)(2,1)}, u32[]{:S(2)}) copy-start(bf16[1,7168,128]{2,1,0:T(8,128)(2,1)} %up_ref.1) | copy-start | bytes 5505028
  46.0 26.7 %collective-permute-start.1 = (bf16[32,7168]{1,0:T(8,128)(2,1)S(1)}, bf16[32,7168]{1,0:T(8,128)(2,1)S(1)}, u32[]{:S(2)}, u32[]{:S(2)}) collective-permute-start(bf16[32,7168]{1,0:T(8,128)(2,1)S(1)} %add_convert_fusion), channel_id=1, source_target_pairs={{0,32},{16,1008},{32,64},{48,16},{64,96},{80,48},{96,128},{112,80}... | collective-permute-start | bytes 1376264 | tf_op jit(solution)/shard_map/ppermute | solution.py:252
  72.8 12.3 %collective-permute-start.2 = (bf16[16,7168]{1,0:T(8,128)(2,1)S(1)}, bf16[16,7168]{1,0:T(8,128)(2,1)S(1)}, u32[]{:S(2)}, u32[]{:S(2)}) collective-permute-start(bf16[16,7168]{1,0:T(8,128)(2,1)S(1)} %add_convert_fusion.1), channel_id=1, source_target_pairs={{0,64},{16,976},{32,96},{48,1008},{64,128},{80,16},{96,160},{112,4... | collective-permute-start | bytes 688136 | tf_op jit(solution)/shard_map/ppermute | solution.py:252
  85.1 2.6 %copy-start.5 = (bf16[16,7168]{1,0:T(8,128)(2,1)}, bf16[16,7168]{1,0:T(8,128)(2,1)S(1)}, u32[]{:S(2)}) copy-start(bf16[16,7168]{1,0:T(8,128)(2,1)S(1)} %collective-permute-done.2) | copy-start | bytes 688132
  85.8 14.6 %collective-permute-start.3 = (bf16[8,7168]{1,0:T(8,128)(2,1)}, bf16[8,7168]{1,0:T(8,128)(2,1)}, u32[]{:S(2)}, u32[]{:S(2)}) collective-permute-start(bf16[8,7168]{1,0:T(8,128)(2,1)} %add_convert_fusion.2), channel_id=1, source_target_pairs={{0,128},{16,912},{32,160},{48,944},{64,192},{80,976},{96,224},{112... | collective-permute-start | bytes 344072 | tf_op jit(solution)/shard_map/ppermute | solution.py:252
  92.1 35.2 %all-to-all-start.1 = ((bf16[16,504,128]{2,1,0:T(8,128)(2,1)}), bf16[16,504,128]{2,1,0:T(8,128)(2,1)S(1)}, u32[]{:S(2)}, u32[]{:S(2)}) async-start(bf16[16,504,128]{2,1,0:T(8,128)(2,1)} %grad_rows.1), calls=%async_computation.1 | async-start | bytes 4128768 | tf_op jit(solution)/shard_map/all_to_all | solution.py:230
  101.6 14.8 %collective-permute-start.4 = (bf16[4,7168]{1,0:T(4,128)(2,1)S(1)}, bf16[4,7168]{1,0:T(4,128)(2,1)S(1)}, u32[]{:S(2)}, u32[]{:S(2)}) collective-permute-start(bf16[4,7168]{1,0:T(4,128)(2,1)S(1)} %add_convert_fusion.3), channel_id=1, source_target_pairs={{0,256},{16,784},{32,288},{48,816},{64,320},{80,848},{96,352},{112... | collective-permute-start | bytes 172040 | tf_op jit(solution)/shard_map/ppermute | solution.py:252
  127.3 1.4 copy-start.6
  128.8 24.1 %collective-permute-start.5 = (bf16[2,7168]{1,0:T(2,128)(2,1)S(1)}, bf16[2,7168]{1,0:T(2,128)(2,1)S(1)}, u32[]{:S(2)}, u32[]{:S(2)}) collective-permute-start(bf16[2,7168]{1,0:T(2,128)(2,1)S(1)} %copy-done.6), channel_id=1, source_target_pairs={{0,512},{16,528},{32,544},{48,560},{64,576},{80,592},{96,608},{112... | collective-permute-start | bytes 86024 | tf_op jit(solution)/shard_map/ppermute | solution.py:252

commit v3 on v2

--- a/solution.py
+++ b/solution.py
@@ -100,7 +100,7 @@
 
 
 def partial_kernel(
-    experts, chips, at_ref, got_ref, pre_ref, arrived_ref, keep_ref, send_ref, factor_ref, tail
+    experts, chips, groups, at_ref, got_ref, pre_ref, arrived_ref, keep_ref, send_ref, factor_ref, tail
 ):
     rows, width = arrived_ref.shape
     hidden_units = pre_ref.shape[1] // 2
@@ -123,11 +123,13 @@
     core = jnp.where(at < half, at_ref[1], 1 - at_ref[1])
     share = half // chips
     place = at % half // share
+    ahead = place // groups
     far = jnp.zeros_like(place)
-    bits = chips.bit_length() - 1
+    bits = (chips // groups).bit_length() - 1
     for bit in range(bits):
-        far = far + (place // 2**bit) % 2 * 2 ** (bits - 1 - bit)
-    chip = (at_ref[0] + (1 - 2 * core) * far + chips) % chips
+        far = far + (ahead // 2**bit) % 2 * 2 ** (bits - 1 - bit)
+    period = chips // groups
+    chip = place % groups * period + (at_ref[0] + (1 - 2 * core) * far + chips) % period
     target = (2 * chip + core) * share + at % share
     hidden = dot(hidden, jnp.where(unit == target, 1.0, 0.0).astype(BF), ((1,), (0,))).astype(BF)
     tail[...] = got_ref[:, experts_rows(width) :, :].astype(F32)
@@ -165,6 +167,22 @@
         ).astype(BF)
 
 
+def fold_kernel(total_ref, coming_ref, out_ref, lines):
+    for c in range(lines.shape[1]):
+        at = slice(c * LANES, (c + 1) * LANES)
+        lines[:, c, :] = total_ref[:, at] + coming_ref[:, at].astype(F32)
+    out_ref[...] = lines[...].reshape(out_ref.shape).astype(BF)
+
+
+def finish_kernel(scale, coming_ref, out_ref, lines):
+    total = coming_ref[0].astype(F32)
+    for g in range(1, coming_ref.shape[0]):
+        total = total + coming_ref[g].astype(F32)
+    lines[...] = (total * scale).reshape(lines.shape)
+    for c in range(lines.shape[1]):
+        out_ref[0, :, c * LANES : (c + 1) * LANES] = lines[:, c, :]
+
+
 def per_device(dy_tokens, routing, route_weight, pre_act, gate_weight, up_weight, down_weight):
     experts = lax.axis_size("expert")
     replicas = lax.axis_size("dp")
@@ -176,6 +194,8 @@
     block_rows = capacity * width // LANES
     chips = replicas // 2
     assert chips & (chips - 1) == 0 and hidden_units % replicas == 0
+    groups = 4
+    period = chips // groups
     shape = jax.ShapeDtypeStruct
     vmem = pl.BlockSpec(memory_space=pltpu.VMEM)
     smem = pl.BlockSpec(memory_space=pltpu.SMEM)
@@ -203,7 +223,7 @@
     own = lax.axis_index("dp")
     half = hidden_units // 2
     arrived, keep, send, factor = pl.pallas_call(
-        functools.partial(partial_kernel, experts, chips),
+        functools.partial(partial_kernel, experts, chips, groups),
         out_shape=(
             shape((rows, width), BF),
             shape((half, width), F32),
@@ -229,6 +249,31 @@
     )(arrived, factor, gate_weight, up_weight, down_weight)
     returned = lax.all_to_all(going_back, "expert", split_axis=0, concat_axis=0, tiled=True)
 
+    total, coming, count, distance = keep, other, half, 1
+    while distance < period:
+        count //= 2
+        going = (total[count:] + coming[count:].astype(F32)).astype(BF)
+        hops = [
+            (2 * z + c, 2 * ((z + (distance if c == 0 else -distance)) % chips) + c)
+            for z in range(chips)
+            for c in range(2)
+        ]
+        total = lax.optimization_barrier(total[:count] + coming[:count].astype(F32))
+        coming = lax.ppermute(going, "dp", hops)
+        distance *= 2
+    share = hidden_units // replicas
+    lines = share * width // LANES
+    going = pl.pallas_call(
+        fold_kernel,
+        out_shape=shape((groups, lines, LANES), BF),
+        in_specs=[vmem] * 2,
+        out_specs=vmem,
+        scratch_shapes=[pltpu.VMEM((count, width // LANES, LANES), F32)],
+        compiler_params=PARAMS,
+        name="fold",
+    )(total, coming)
+    members = [[2 * (g * period + i) + c for g in range(groups)] for i in range(period) for c in range(2)]
+    coming = lax.all_to_all(going, "dp", 0, 0, axis_index_groups=members, tiled=True)
     grad_tokens = pl.pallas_call(
         functools.partial(combine_kernel, experts),
         out_shape=shape((tokens, width), BF),
@@ -238,23 +283,16 @@
         compiler_params=PARAMS,
         name="combine_rows",
     )(pick, returned)
-    terms, count, distance = [keep, other], half, 1
-    while distance < chips:
-        count //= 2
-        going = functools.reduce(jnp.add, [t[count:].astype(F32) for t in terms]).astype(BF)
-        if 2 * distance == chips:
-            going, grad_tokens = lax.optimization_barrier((going, grad_tokens))
-        hops = [
-            (2 * z + c, 2 * ((z + (distance if c == 0 else -distance)) % chips) + c)
-            for z in range(chips)
-            for c in range(2)
-        ]
-        coming = lax.ppermute(going, "dp", hops)
-        terms = [t[:count] for t in terms] + [coming]
-        distance *= 2
-    grad_down = functools.reduce(jnp.add, [t.astype(F32) for t in terms]) * (1.0 / replicas)
-    grad_down = grad_down[None]
-
+    coming, grad_tokens = lax.optimization_barrier((coming, grad_tokens))
+    grad_down = pl.pallas_call(
+        functools.partial(finish_kernel, 1.0 / replicas),
+        out_shape=shape((1, share, width), F32),
+        in_specs=[vmem],
+        out_specs=vmem,
+        scratch_shapes=[pltpu.VMEM((share, width // LANES, LANES), F32)],
+        compiler_params=PARAMS,
+        name="finish",
+    )(coming)
     return (grad_tokens, grad_down)
 
 

time: 155 us -> 150 us (0.968)
  the two profiles are of different devices: /device:TPU:8 before, /device:TPU:32 now
where the time goes in v3:
time: 150 us; the launch traced here: 149 us
  waiting for transfers between devices  85.7 us (57%)
  starting transfers between devices  49.7 us (33%)
  Pallas kernels  11.9 us (8%)
    all_to_all x1, waiting for transfers between devices, per_device(): lax.all_to_all(outgoing, 'expert', split_axis=0, concat_axis=0, tiled=True)  31.1 us
    all_to_all x1, waiting for transfers between devices, per_device(): lax.all_to_all(going, 'dp', 0, 0, axis_index_groups=members, tiled=True)  27.5 us
    ppermute x3, waiting for transfers between devices, per_device(): coming = lax.ppermute(going, 'dp', hops)  24.7 us
    all_to_all x1, starting transfers between devices, per_device(): lax.all_to_all(going, 'dp', 0, 0, axis_index_groups=members, tiled=True)  24.7 us
    ppermute x3, starting transfers between devices, per_device(): coming = lax.ppermute(going, 'dp', hops)  12.2 us
    all_to_all x1, starting transfers between devices, per_device(): lax.all_to_all(outgoing, 'expert', split_axis=0, concat_axis=0, tiled=True)  7.19 us
    pallas_call x1, Pallas kernels, per_device(): pl.pallas_call(functools.partial(grad_kernel, experts), out_shape=block,...  4.31 us
    all_to_all x1, starting transfers between devices, per_device(): lax.all_to_all(going_back, 'expert', split_axis=0, concat_axis=0, tiled=T...  3.72 us
  transfers between devices with their start and end apart: 7, of which 5 were waited for; matrix products, arithmetic and copies ran while one was open for 0% of the time, Pallas kernels for 4%

profile of v3, /device:TPU:32, one launch (start us, length us, event | category | flops | bytes accessed | tf_op | source)
XLA Modules:
  0.0 149.2 jit_solution(9623945086846876723)
XLA Ops:
  0.6 2.7 %dispatch_rows.1 = (bf16[16,504,128]{2,1,0:T(8,128)(2,1)}, bf16[144,32]{1,0:T(8,128)(2,1)S(1)}) custom-call(bf16[32,7168]{1,0:T(8,128)(2,1)} %dy_hbm.1, s32[4,32]{1,0:T(4,128)} %bitcast.4, f32[4,32]{1,0:T(4,128)} %bitcast.5), custom_call_target="tpu_custom_call" | custom-call | tf_op jit(solution)/shard_map/dispatch_rows/pallas_call | solution.py:205
  3.4 0.0 copy-start.3
  3.4 7.2 %all-to-all-start = ((bf16[16,504,128]{2,1,0:T(8,128)(2,1)}), bf16[16,504,128]{2,1,0:T(8,128)(2,1)S(1)}, u32[]{:S(2)}, u32[]{:S(2)}) async-start(bf16[16,504,128]{2,1,0:T(8,128)(2,1)} %get-tuple-element.10), calls=%async_computation | async-start | bytes 4128768 | tf_op jit(solution)/shard_map/all_to_all | solution.py:221
  10.6 0.1 pad_add_fusion.at_ref
  10.7 31.1 %all-to-all-done.got_ref = bf16[16,504,128]{2,1,0:T(8,128)(2,1)S(1)} async-done(((bf16[16,504,128]{2,1,0:T(8,128)(2,1)}), bf16[16,504,128]{2,1,0:T(8,128)(2,1)S(1)}, u32[]{:S(2)}, u32[]{:S(2)}) %all-to-all-start) | async-done | bytes 2064416 | tf_op jit(solution)/shard_map/all_to_all | solution.py:221
  41.8 0.0 copy-done.3
  41.8 0.0 copy-start.2
  41.8 2.0 %down_partial.1 = (bf16[144,7168]{1,0:T(8,128)(2,1)S(1)}, f32[64,7168]{1,0:T(8,128)S(1)}, bf16[64,7168]{1,0:T(8,128)(2,1)S(1)}, f32[144,256]{1,0:T(8,128)S(1)}) custom-call(s32[2]{0:T(128)S(1)} %pad_add_fusion.at_ref, bf16[16,504,128]{2,1,0:T(8,128)(2,1)S(1)} %all-to-all-done.got_ref, bf16[144,256]{1,0:T(8,128)(2,1)S(1)} %copy-done.3), custom_call_target="tpu_custom_call" | custom-call | tf_op jit(solution)/shard_map/down_partial/pallas_call | solution.py:225
  43.8 1.9 %collective-permute-start = (bf16[64,7168]{1,0:T(8,128)(2,1)S(1)}, bf16[64,7168]{1,0:T(8,128)(2,1)S(1)}, u32[]{:S(2)}, u32[]{:S(2)}) collective-permute-start(bf16[64,7168]{1,0:T(8,128)(2,1)S(1)} %get-tuple-element.12), channel_id=1, source_target_pairs={{0,16},{16,0},{32,48},{48,32},{64,80},{80,64},{96,112},{112,96},{1... | collective-permute-start | bytes 2752520 | tf_op jit(solution)/shard_map/ppermute | solution.py:239
  45.7 2.4 %collective-permute-done = bf16[64,7168]{1,0:T(8,128)(2,1)S(1)} collective-permute-done((bf16[64,7168]{1,0:T(8,128)(2,1)S(1)}, bf16[64,7168]{1,0:T(8,128)(2,1)S(1)}, u32[]{:S(2)}, u32[]{:S(2)}) %collective-permute-start) | collective-permute-done | bytes 917536 | tf_op jit(solution)/shard_map/ppermute | solution.py:239
  48.1 0.0 copy-start
  48.1 0.0 copy-start.1
  48.1 0.9 add_convert_fusion
  49.0 4.0 %collective-permute-start.1 = (bf16[32,7168]{1,0:T(8,128)(2,1)}, bf16[32,7168]{1,0:T(8,128)(2,1)S(1)}, u32[]{:S(2)}, u32[]{:S(2)}) collective-permute-start(bf16[32,7168]{1,0:T(8,128)(2,1)} %get-tuple-element.18), channel_id=1, source_target_pairs={{0,32},{16,1008},{32,64},{48,16},{64,96},{80,48},{96,128},{112,80}... | collective-permute-start | bytes 1376264 | tf_op jit(solution)/shard_map/ppermute | solution.py:262
  53.0 0.0 copy-done.2
  53.0 0.0 copy-done
  53.0 0.0 copy-done.1
  53.1 4.3 %grad_rows.1 = bf16[16,504,128]{2,1,0:T(8,128)(2,1)} custom-call(bf16[144,7168]{1,0:T(8,128)(2,1)S(1)} %get-tuple-element.14.arrived_ref, f32[144,256]{1,0:T(8,128)S(1)} %get-tuple-element.15.factor_ref, bf16[1,7168,128]{2,1,0:T(8,128)(2,1)S(1)} %copy-done, bf16[1,7168,128]{2,1,0:T(8,128)(2,1)S(1)} %copy-done.1, bf16[1,128,7168]{2,1,0:T(8,128)(2,1)S(1)} %copy-done.2), custom_call_target="tpu_custom_call" | custom-call | tf_op jit(solution)/shard_map/grad_rows/pallas_call | solution.py:241
  57.4 3.7 %all-to-all-start.2 = ((bf16[16,504,128]{2,1,0:T(8,128)(2,1)}), bf16[16,504,128]{2,1,0:T(8,128)(2,1)S(1)}, u32[]{:S(2)}, u32[]{:S(2)}) async-start(bf16[16,504,128]{2,1,0:T(8,128)(2,1)} %grad_rows.1), calls=%async_computation.2 | async-start | bytes 4128768 | tf_op jit(solution)/shard_map/all_to_all | solution.py:250
  61.1 0.0 collective-permute-done.1
  61.1 0.1 fusion
  61.2 6.4 %collective-permute-start.2 = (bf16[16,7168]{1,0:T(8,128)(2,1)S(1)}, bf16[16,7168]{1,0:T(8,128)(2,1)S(1)}, u32[]{:S(2)}, u32[]{:S(2)}) collective-permute-start(bf16[16,7168]{1,0:T(8,128)(2,1)S(1)} %get-tuple-element.20), channel_id=1, source_target_pairs={{0,64},{16,976},{32,96},{48,1008},{64,128},{80,16},{96,160},{112,4... | collective-permute-start | bytes 688136 | tf_op jit(solution)/shard_map/ppermute | solution.py:262
  67.5 14.9 %collective-permute-done.2 = bf16[16,7168]{1,0:T(8,128)(2,1)S(1)} collective-permute-done((bf16[16,7168]{1,0:T(8,128)(2,1)S(1)}, bf16[16,7168]{1,0:T(8,128)(2,1)S(1)}, u32[]{:S(2)}, u32[]{:S(2)}) %collective-permute-start.2) | collective-permute-done | bytes 229408 | tf_op jit(solution)/shard_map/ppermute | solution.py:262
  82.5 1.9 %collective-permute-start.3 = (bf16[8,7168]{1,0:T(8,128)(2,1)S(1)}, bf16[8,7168]{1,0:T(8,128)(2,1)S(1)}, u32[]{:S(2)}, u32[]{:S(2)}) collective-permute-start(bf16[8,7168]{1,0:T(8,128)(2,1)S(1)} %get-tuple-element.22), channel_id=1, source_target_pairs={{0,128},{16,912},{32,160},{48,944},{64,192},{80,976},{96,224},{112... | collective-permute-start | bytes 344072 | tf_op jit(solution)/shard_map/ppermute | solution.py:262
  84.4 9.8 %collective-permute-done.3.coming_ref = bf16[8,7168]{1,0:T(8,128)(2,1)S(1)} collective-permute-done((bf16[8,7168]{1,0:T(8,128)(2,1)S(1)}, bf16[8,7168]{1,0:T(8,128)(2,1)S(1)}, u32[]{:S(2)}, u32[]{:S(2)}) %collective-permute-start.3) | collective-permute-done | bytes 114720 | tf_op jit(solution)/shard_map/ppermute | solution.py:262
  94.2 0.8 fold.1
  95.0 0.0 all-to-all-done.2.got_ref
  95.0 24.7 %all-to-all-start.1 = ((bf16[4,112,128]{2,1,0:T(8,128)(2,1)}), bf16[4,112,128]{2,1,0:T(8,128)(2,1)S(1)}, u32[]{:S(2)}, u32[]{:S(2)}) async-start(bf16[4,112,128]{2,1,0:T(8,128)(2,1)} %fold.1), calls=%async_computation.1 | async-start | bytes 229376 | tf_op jit(solution)/shard_map/all_to_all | solution.py:276
  119.6 1.4 combine_rows.1
  121.1 27.5 %all-to-all-done.1.coming_ref = bf16[4,112,128]{2,1,0:T(8,128)(2,1)S(1)} async-done(((bf16[4,112,128]{2,1,0:T(8,128)(2,1)}), bf16[4,112,128]{2,1,0:T(8,128)(2,1)S(1)}, u32[]{:S(2)}, u32[]{:S(2)}) %all-to-all-start.1) | async-done | bytes 114720 | tf_op jit(solution)/shard_map/all_to_all | solution.py:276
  148.5 0.7 finish.1
  (1 shorter events, 0.0 us)
Async XLA Ops:
  3.4 38.4 %copy-start.3 = (bf16[144,256]{1,0:T(8,128)(2,1)S(1)}, bf16[144,256]{1,0:T(8,128)(2,1)}, u32[]{:S(2)}) copy-start(bf16[144,256]{1,0:T(8,128)(2,1)} %pre_ref.1) | copy-start | bytes 221188
  3.4 38.4 %all-to-all-start = ((bf16[16,504,128]{2,1,0:T(8,128)(2,1)}), bf16[16,504,128]{2,1,0:T(8,128)(2,1)S(1)}, u32[]{:S(2)}, u32[]{:S(2)}) async-start(bf16[16,504,128]{2,1,0:T(8,128)(2,1)} %get-tuple-element.10), calls=%async_computation | async-start | bytes 4128768 | tf_op jit(solution)/shard_map/all_to_all | solution.py:221
  41.8 11.3 %copy-start.2 = (bf16[1,128,7168]{2,1,0:T(8,128)(2,1)S(1)}, bf16[1,128,7168]{2,1,0:T(8,128)(2,1)}, u32[]{:S(2)}) copy-start(bf16[1,128,7168]{2,1,0:T(8,128)(2,1)} %down_ref.1) | copy-start | bytes 5505028
  43.8 4.4 %collective-permute-start = (bf16[64,7168]{1,0:T(8,128)(2,1)S(1)}, bf16[64,7168]{1,0:T(8,128)(2,1)S(1)}, u32[]{:S(2)}, u32[]{:S(2)}) collective-permute-start(bf16[64,7168]{1,0:T(8,128)(2,1)S(1)} %get-tuple-element.12), channel_id=1, source_target_pairs={{0,16},{16,0},{32,48},{48,32},{64,80},{80,64},{96,112},{112,96},{1... | collective-permute-start | bytes 2752520 | tf_op jit(solution)/shard_map/ppermute | solution.py:239
  48.1 4.9 %copy-start = (bf16[1,7168,128]{2,1,0:T(8,128)(2,1)S(1)}, bf16[1,7168,128]{2,1,0:T(8,128)(2,1)}, u32[]{:S(2)}) copy-start(bf16[1,7168,128]{2,1,0:T(8,128)(2,1)} %gate_ref.1) | copy-start | bytes 5505028
  48.1 4.9 %copy-start.1 = (bf16[1,7168,128]{2,1,0:T(8,128)(2,1)S(1)}, bf16[1,7168,128]{2,1,0:T(8,128)(2,1)}, u32[]{:S(2)}) copy-start(bf16[1,7168,128]{2,1,0:T(8,128)(2,1)} %up_ref.1) | copy-start | bytes 5505028
  49.0 12.0 %collective-permute-start.1 = (bf16[32,7168]{1,0:T(8,128)(2,1)}, bf16[32,7168]{1,0:T(8,128)(2,1)S(1)}, u32[]{:S(2)}, u32[]{:S(2)}) collective-permute-start(bf16[32,7168]{1,0:T(8,128)(2,1)} %get-tuple-element.18), channel_id=1, source_target_pairs={{0,32},{16,1008},{32,64},{48,16},{64,96},{80,48},{96,128},{112,80}... | collective-permute-start | bytes 1376264 | tf_op jit(solution)/shard_map/ppermute | solution.py:262
  57.4 37.6 %all-to-all-start.2 = ((bf16[16,504,128]{2,1,0:T(8,128)(2,1)}), bf16[16,504,128]{2,1,0:T(8,128)(2,1)S(1)}, u32[]{:S(2)}, u32[]{:S(2)}) async-start(bf16[16,504,128]{2,1,0:T(8,128)(2,1)} %grad_rows.1), calls=%async_computation.2 | async-start | bytes 4128768 | tf_op jit(solution)/shard_map/all_to_all | solution.py:250
  61.2 21.2 %collective-permute-start.2 = (bf16[16,7168]{1,0:T(8,128)(2,1)S(1)}, bf16[16,7168]{1,0:T(8,128)(2,1)S(1)}, u32[]{:S(2)}, u32[]{:S(2)}) collective-permute-start(bf16[16,7168]{1,0:T(8,128)(2,1)S(1)} %get-tuple-element.20), channel_id=1, source_target_pairs={{0,64},{16,976},{32,96},{48,1008},{64,128},{80,16},{96,160},{112,4... | collective-permute-start | bytes 688136 | tf_op jit(solution)/shard_map/ppermute | solution.py:262
  82.5 11.7 %collective-permute-start.3 = (bf16[8,7168]{1,0:T(8,128)(2,1)S(1)}, bf16[8,7168]{1,0:T(8,128)(2,1)S(1)}, u32[]{:S(2)}, u32[]{:S(2)}) collective-permute-start(bf16[8,7168]{1,0:T(8,128)(2,1)S(1)} %get-tuple-element.22), channel_id=1, source_target_pairs={{0,128},{16,912},{32,160},{48,944},{64,192},{80,976},{96,224},{112... | collective-permute-start | bytes 344072 | tf_op jit(solution)/shard_map/ppermute | solution.py:262
  95.0 53.6 %all-to-all-start.1 = ((bf16[4,112,128]{2,1,0:T(8,128)(2,1)}), bf16[4,112,128]{2,1,0:T(8,128)(2,1)S(1)}, u32[]{:S(2)}, u32[]{:S(2)}) async-start(bf16[4,112,128]{2,1,0:T(8,128)(2,1)} %fold.1), calls=%async_computation.1 | async-start | bytes 229376 | tf_op jit(solution)/shard_map/all_to_all | solution.py:276

commit v4 on v3

--- a/solution.py
+++ b/solution.py
@@ -11,6 +11,7 @@
 F32 = jnp.float32
 LANES = 128
 FIRST = 8
+PARTS = 4
 PARAMS = pltpu.CompilerParams(vmem_limit_bytes=16 * 1024 * 1024)
 
 
@@ -72,22 +73,30 @@
     chosen = pick.astype(BF)
     pick_ref[...] = chosen
     row_weight = jnp.sum(pick * scale, axis=1, keepdims=True)
+    loads[2].wait()
+
+    def columns(at):
+        return dot(chosen, dy_ref[:, at], ((1,), (0,))) * row_weight
+
+    write_all(columns, width, experts, out_ref, out_hbm, tail, [sems.at[3 + i] for i in range(PARTS)])
+
+
+def write_all(columns, width, experts, out_ref, out_hbm, tail, sems):
     pairs = width // (2 * LANES)
-    parts = 4
+    step = pairs // PARTS
     stores = []
-    loads[2].wait()
     for pair in range(pairs):
-        part = dot(chosen, dy_ref[:, pair * 2 * LANES : (pair + 1) * 2 * LANES], ((1,), (0,)))
-        part = part * row_weight
+        part = columns(slice(pair * 2 * LANES, (pair + 1) * 2 * LANES))
         write_block(out_ref, tail, pair, part[:, :LANES], part[:, LANES:], experts)
-        if (pair + 1) % (pairs // parts) == 0:
-            rows_of = slice(len(stores) * pairs // parts * 16, (pair + 1) * 16)
+        if (pair + 1) % step == 0:
+            stop = (pair + 1) * 16
             if pair + 1 == pairs:
-                out_ref[:, experts_rows(width) :, :] = tail[...].astype(BF)
-                rows_of = slice(rows_of.start, out_ref.shape[1])
+                out_ref[:, stop:, :] = tail[...].astype(BF)
+                stop = out_ref.shape[1]
+            rows = slice(len(stores) * step * 16, stop)
             stores.append(
                 pltpu.make_async_copy(
-                    out_ref.at[:, rows_of, :], out_hbm.at[:, rows_of, :], sems.at[3 + len(stores)]
+                    out_ref.at[:, rows, :], out_hbm.at[:, rows, :], sems[len(stores)]
                 )
             )
             stores[-1].start()
@@ -100,7 +109,7 @@
 
 
 def partial_kernel(
-    experts, chips, groups, at_ref, got_ref, pre_ref, arrived_ref, keep_ref, send_ref, factor_ref, tail
+    experts, chips, at_ref, got_ref, pre_ref, arrived_ref, keep_ref, send_ref, factor_ref, tail
 ):
     rows, width = arrived_ref.shape
     hidden_units = pre_ref.shape[1] // 2
@@ -123,13 +132,11 @@
     core = jnp.where(at < half, at_ref[1], 1 - at_ref[1])
     share = half // chips
     place = at % half // share
-    ahead = place // groups
     far = jnp.zeros_like(place)
-    bits = (chips // groups).bit_length() - 1
+    bits = chips.bit_length() - 1
     for bit in range(bits):
-        far = far + (ahead // 2**bit) % 2 * 2 ** (bits - 1 - bit)
-    period = chips // groups
-    chip = place % groups * period + (at_ref[0] + (1 - 2 * core) * far + chips) % period
+        far = far + (place // 2**bit) % 2 * 2 ** (bits - 1 - bit)
+    chip = (at_ref[0] + (1 - 2 * core) * far + chips) % chips
     target = (2 * chip + core) * share + at % share
     hidden = dot(hidden, jnp.where(unit == target, 1.0, 0.0).astype(BF), ((1,), (0,))).astype(BF)
     tail[...] = got_ref[:, experts_rows(width) :, :].astype(F32)
@@ -142,18 +149,19 @@
         send_ref[:, at] = part[half:].astype(BF)
 
 
-def grad_kernel(experts, arrived_ref, factor_ref, gate_ref, up_ref, down_ref, out_ref, tail):
-    width = arrived_ref.shape[1]
-    hidden_units = down_ref.shape[1]
+def hidden_kernel(arrived_ref, factor_ref, down_ref, out_ref):
     grad_hidden = dot(arrived_ref[...], down_ref[0], ((1,), (1,)))
-    grad_gate = (grad_hidden * factor_ref[:, :hidden_units]).astype(BF)
-    grad_up = (grad_hidden * factor_ref[:, hidden_units:]).astype(BF)
-    for pair in range(width // (2 * LANES)):
-        at = slice(pair * 2 * LANES, (pair + 1) * 2 * LANES)
-        part = dot(grad_gate, gate_ref[0, at, :], ((1,), (1,)))
-        part = part + dot(grad_up, up_ref[0, at, :], ((1,), (1,)))
-        write_block(out_ref, tail, pair, part[:, :LANES], part[:, LANES:], experts)
-    out_ref[:, experts_rows(width) :, :] = tail[...].astype(BF)
+    out_ref[...] = (jnp.concatenate([grad_hidden, grad_hidden], axis=1) * factor_ref[...]).astype(BF)
+
+
+def grad_kernel(experts, hidden_ref, gate_ref, up_ref, out_hbm, out_ref, tail, sems):
+    hidden = hidden_ref[...]
+
+    def columns(at):
+        weight = jnp.concatenate([gate_ref[0, at, :], up_ref[0, at, :]], axis=1)
+        return dot(hidden, weight, ((1,), (1,)))
+
+    write_all(columns, gate_ref.shape[1], experts, out_ref, out_hbm, tail, [sems.at[i] for i in range(PARTS)])
 
 
 def combine_kernel(experts, pick_ref, got_ref, out_ref, tail):
@@ -167,18 +175,18 @@
         ).astype(BF)
 
 
-def fold_kernel(total_ref, coming_ref, out_ref, lines):
+def fold_kernel(total_ref, coming_ref, keep_ref, send_ref, lines):
     for c in range(lines.shape[1]):
         at = slice(c * LANES, (c + 1) * LANES)
         lines[:, c, :] = total_ref[:, at] + coming_ref[:, at].astype(F32)
-    out_ref[...] = lines[...].reshape(out_ref.shape).astype(BF)
-
-
-def finish_kernel(scale, coming_ref, out_ref, lines):
-    total = coming_ref[0].astype(F32)
-    for g in range(1, coming_ref.shape[0]):
-        total = total + coming_ref[g].astype(F32)
-    lines[...] = (total * scale).reshape(lines.shape)
+    count = keep_ref.shape[0]
+    pieces = lines[...].reshape((2 * count,) + keep_ref.shape[1:])
+    keep_ref[...] = pieces[:count]
+    send_ref[...] = pieces[count:].astype(BF)
+
+
+def finish_kernel(scale, total_ref, coming_ref, out_ref, lines):
+    lines[...] = ((total_ref[0] + coming_ref[0].astype(F32)) * scale).reshape(lines.shape)
     for c in range(lines.shape[1]):
         out_ref[0, :, c * LANES : (c + 1) * LANES] = lines[:, c, :]
 
@@ -194,8 +202,6 @@
     block_rows = capacity * width // LANES
     chips = replicas // 2
     assert chips & (chips - 1) == 0 and hidden_units % replicas == 0
-    groups = 4
-    period = chips // groups
     shape = jax.ShapeDtypeStruct
     vmem = pl.BlockSpec(memory_space=pltpu.VMEM)
     smem = pl.BlockSpec(memory_space=pltpu.SMEM)
@@ -213,7 +219,7 @@
             pltpu.VMEM(route_weight.T.shape, F32),
             pltpu.VMEM((experts, block_rows, LANES), BF),
             tail,
-            pltpu.SemaphoreType.DMA((7,)),
+            pltpu.SemaphoreType.DMA((3 + PARTS,)),
         ],
         compiler_params=PARAMS,
         name="dispatch_rows",
@@ -223,7 +229,7 @@
     own = lax.axis_index("dp")
     half = hidden_units // 2
     arrived, keep, send, factor = pl.pallas_call(
-        functools.partial(partial_kernel, experts, chips, groups),
+        functools.partial(partial_kernel, experts, chips),
         out_shape=(
             shape((rows, width), BF),
             shape((half, width), F32),
@@ -238,42 +244,65 @@
     )(jnp.stack([own // 2, own % 2]), got, pre_act)
     other = lax.ppermute(send, "dp", [(i, i ^ 1) for i in range(replicas)])
 
+    grad_hidden = pl.pallas_call(
+        hidden_kernel,
+        out_shape=shape((rows, 2 * hidden_units), BF),
+        in_specs=[vmem] * 3,
+        out_specs=vmem,
+        compiler_params=PARAMS,
+        name="grad_hidden",
+    )(arrived, factor, down_weight)
+    other, grad_hidden = lax.optimization_barrier((other, grad_hidden))
     going_back = pl.pallas_call(
         functools.partial(grad_kernel, experts),
-        out_shape=block,
-        in_specs=[vmem] * 5,
-        out_specs=vmem,
-        scratch_shapes=[tail],
+        out_shape=pltpu.HBM(block.shape, BF),
+        in_specs=[vmem] * 3,
+        out_specs=pl.BlockSpec(memory_space=pltpu.HBM),
+        scratch_shapes=[
+            pltpu.VMEM((experts, block_rows, LANES), BF),
+            tail,
+            pltpu.SemaphoreType.DMA((PARTS,)),
+        ],
         compiler_params=PARAMS,
         name="grad_rows",
-    )(arrived, factor, gate_weight, up_weight, down_weight)
-    returned = lax.all_to_all(going_back, "expert", split_axis=0, concat_axis=0, tiled=True)
-
-    total, coming, count, distance = keep, other, half, 1
-    while distance < period:
-        count //= 2
-        going = (total[count:] + coming[count:].astype(F32)).astype(BF)
+    )(grad_hidden, gate_weight, up_weight)
+    def pass_on(going, distance):
         hops = [
             (2 * z + c, 2 * ((z + (distance if c == 0 else -distance)) % chips) + c)
             for z in range(chips)
             for c in range(2)
         ]
-        total = lax.optimization_barrier(total[:count] + coming[:count].astype(F32))
-        coming = lax.ppermute(going, "dp", hops)
-        distance *= 2
+        return lax.ppermute(going, "dp", hops)
+
     share = hidden_units // replicas
     lines = share * width // LANES
-    going = pl.pallas_call(
+    total, coming, count, distance = keep, other, half, 1
+    while count > 8:
+        count //= 2
+        going = (total[count:] + coming[count:].astype(F32)).astype(BF)
+        total = lax.optimization_barrier(total[:count] + coming[:count].astype(F32))
+        coming = pass_on(going, distance)
+        if distance == 1:
+            coming, going_back = lax.optimization_barrier((coming, going_back))
+        distance *= 2
+    returned = lax.all_to_all(going_back, "expert", split_axis=0, concat_axis=0, tiled=True)
+    count = count // share // 2
+    total, going = pl.pallas_call(
         fold_kernel,
-        out_shape=shape((groups, lines, LANES), BF),
+        out_shape=(shape((count, lines, LANES), F32), shape((count, lines, LANES), BF)),
         in_specs=[vmem] * 2,
-        out_specs=vmem,
-        scratch_shapes=[pltpu.VMEM((count, width // LANES, LANES), F32)],
+        out_specs=(vmem, vmem),
+        scratch_shapes=[pltpu.VMEM((2 * count * share, width // LANES, LANES), F32)],
         compiler_params=PARAMS,
         name="fold",
     )(total, coming)
-    members = [[2 * (g * period + i) + c for g in range(groups)] for i in range(period) for c in range(2)]
-    coming = lax.all_to_all(going, "dp", 0, 0, axis_index_groups=members, tiled=True)
+    coming = pass_on(going, distance)
+    while count > 1:
+        count //= 2
+        distance *= 2
+        going = (total[count:] + coming[count:].astype(F32)).astype(BF)
+        total = lax.optimization_barrier(total[:count] + coming[:count].astype(F32))
+        coming = pass_on(going, distance)
     grad_tokens = pl.pallas_call(
         functools.partial(combine_kernel, experts),
         out_shape=shape((tokens, width), BF),
@@ -287,12 +316,12 @@
     grad_down = pl.pallas_call(
         functools.partial(finish_kernel, 1.0 / replicas),
         out_shape=shape((1, share, width), F32),
-        in_specs=[vmem],
+        in_specs=[vmem] * 2,
         out_specs=vmem,
         scratch_shapes=[pltpu.VMEM((share, width // LANES, LANES), F32)],
         compiler_params=PARAMS,
         name="finish",
-    )(coming)
+    )(total, coming)
     return (grad_tokens, grad_down)
 
 

time: 150 us -> 140 us (0.933)
  the two profiles are of different devices: /device:TPU:32 before, /device:TPU:8 now
where the time goes in v4:
time: 140 us
  waiting for transfers between devices  78.9 us (56%)
  starting transfers between devices  49.6 us (35%)
  Pallas kernels  10 us (7%)
    ppermute x5, waiting for transfers between devices, pass_on(): return lax.ppermute(going, 'dp', hops)  57.8 us
    ppermute x5, starting transfers between devices, pass_on(): return lax.ppermute(going, 'dp', hops)  26 us
    all_to_all x1, waiting for transfers between devices, per_device(): lax.all_to_all(outgoing, 'expert', split_axis=0, concat_axis=0, tiled=True)  19.4 us
    all_to_all x1, starting transfers between devices, per_device(): lax.all_to_all(outgoing, 'expert', split_axis=0, concat_axis=0, tiled=True)  16.8 us
    all_to_all x1, starting transfers between devices, per_device(): lax.all_to_all(going_back, 'expert', split_axis=0, concat_axis=0, tiled=T...  4.9 us
  transfers between devices with their start and end apart: 8, of which 7 were waited for; matrix products, arithmetic and copies ran while one was open for 0% of the time, Pallas kernels for 3%

profile of v4, /device:TPU:8, one launch (start us, length us, event | category | flops | bytes accessed | tf_op | source)
XLA Modules:
  0.0 139.7 jit_solution(13164069615289893033)
XLA Ops:
  0.6 2.7 %dispatch_rows.1 = (bf16[16,504,128]{2,1,0:T(8,128)(2,1)}, bf16[144,32]{1,0:T(8,128)(2,1)S(1)}) custom-call(bf16[32,7168]{1,0:T(8,128)(2,1)} %dy_hbm.1, s32[4,32]{1,0:T(4,128)} %bitcast.4, f32[4,32]{1,0:T(4,128)} %bitcast.5), custom_call_target="tpu_custom_call" | custom-call | tf_op jit(solution)/shard_map/dispatch_rows/pallas_call | solution.py:211
  3.4 0.0 copy-start.3
  3.4 16.8 %all-to-all-start = ((bf16[16,504,128]{2,1,0:T(8,128)(2,1)}), bf16[16,504,128]{2,1,0:T(8,128)(2,1)S(1)}, u32[]{:S(2)}, u32[]{:S(2)}) async-start(bf16[16,504,128]{2,1,0:T(8,128)(2,1)} %get-tuple-element.16), calls=%async_computation | async-start | bytes 4128768 | tf_op jit(solution)/shard_map/all_to_all | solution.py:227
  20.1 0.1 pad_add_fusion.at_ref
  20.2 19.4 %all-to-all-done.got_ref = bf16[16,504,128]{2,1,0:T(8,128)(2,1)S(1)} async-done(((bf16[16,504,128]{2,1,0:T(8,128)(2,1)}), bf16[16,504,128]{2,1,0:T(8,128)(2,1)S(1)}, u32[]{:S(2)}, u32[]{:S(2)}) %all-to-all-start) | async-done | bytes 2064416 | tf_op jit(solution)/shard_map/all_to_all | solution.py:227
  39.6 0.0 copy-done.3
  39.6 0.0 copy-start
  39.6 2.0 %down_partial.1 = (bf16[144,7168]{1,0:T(8,128)(2,1)S(1)}, f32[64,7168]{1,0:T(8,128)S(1)}, bf16[64,7168]{1,0:T(8,128)(2,1)S(1)}, f32[144,256]{1,0:T(8,128)S(1)}) custom-call(s32[2]{0:T(128)S(1)} %pad_add_fusion.at_ref, bf16[16,504,128]{2,1,0:T(8,128)(2,1)S(1)} %all-to-all-done.got_ref, bf16[144,256]{1,0:T(8,128)(2,1)S(1)} %copy-done.3), custom_call_target="tpu_custom_call" | custom-call | tf_op jit(solution)/shard_map/down_partial/pallas_call | solution.py:231
  41.6 1.9 %collective-permute-start = (bf16[64,7168]{1,0:T(8,128)(2,1)S(1)}, bf16[64,7168]{1,0:T(8,128)(2,1)S(1)}, u32[]{:S(2)}, u32[]{:S(2)}) collective-permute-start(bf16[64,7168]{1,0:T(8,128)(2,1)S(1)} %get-tuple-element.18), channel_id=1, source_target_pairs={{0,16},{16,0},{32,48},{48,32},{64,80},{80,64},{96,112},{112,96},{1... | collective-permute-start | bytes 2752520 | tf_op jit(solution)/shard_map/ppermute | solution.py:245
  43.5 0.0 copy-done
  43.5 0.7 grad_hidden.1.hidden_ref
  44.2 1.7 %collective-permute-done = bf16[64,7168]{1,0:T(8,128)(2,1)S(1)} collective-permute-done((bf16[64,7168]{1,0:T(8,128)(2,1)S(1)}, bf16[64,7168]{1,0:T(8,128)(2,1)S(1)}, u32[]{:S(2)}, u32[]{:S(2)}) %collective-permute-start) | collective-permute-done | bytes 917536 | tf_op jit(solution)/shard_map/ppermute | solution.py:245
  45.9 0.0 copy-start.1
  45.9 0.0 copy-start.2
  46.0 0.2 add_convert_fusion
  46.2 5.3 %collective-permute-start.1 = (bf16[32,7168]{1,0:T(8,128)(2,1)S(1)}, bf16[32,7168]{1,0:T(8,128)(2,1)S(1)}, u32[]{:S(2)}, u32[]{:S(2)}) collective-permute-start(bf16[32,7168]{1,0:T(8,128)(2,1)S(1)} %get-tuple-element.30), channel_id=1, source_target_pairs={{0,32},{16,1008},{32,64},{48,16},{64,96},{80,48},{96,128},{112,80}... | collective-permute-start | bytes 1376264 | tf_op jit(solution)/shard_map/ppermute | solution.py:275
  51.5 0.0 copy-done.1
  51.5 0.0 copy-done.2
  51.5 2.3 %grad_rows.1 = bf16[16,504,128]{2,1,0:T(8,128)(2,1)} custom-call(bf16[144,256]{1,0:T(8,128)(2,1)S(1)} %grad_hidden.1.hidden_ref, bf16[1,7168,128]{2,1,0:T(8,128)(2,1)S(1)} %copy-done.1, bf16[1,7168,128]{2,1,0:T(8,128)(2,1)S(1)} %copy-done.2), custom_call_target="tpu_custom_call" | custom-call | tf_op jit(solution)/shard_map/grad_rows/pallas_call | solution.py:256
  53.9 18.9 %collective-permute-done.1 = bf16[32,7168]{1,0:T(8,128)(2,1)S(1)} collective-permute-done((bf16[32,7168]{1,0:T(8,128)(2,1)S(1)}, bf16[32,7168]{1,0:T(8,128)(2,1)S(1)}, u32[]{:S(2)}, u32[]{:S(2)}) %collective-permute-start.1) | collective-permute-done | bytes 458784 | tf_op jit(solution)/shard_map/ppermute | solution.py:275
  72.8 0.1 fusion
  72.9 1.9 %collective-permute-start.2 = (bf16[16,7168]{1,0:T(8,128)(2,1)S(1)}, bf16[16,7168]{1,0:T(8,128)(2,1)S(1)}, u32[]{:S(2)}, u32[]{:S(2)}) collective-permute-start(bf16[16,7168]{1,0:T(8,128)(2,1)S(1)} %get-tuple-element.32), channel_id=1, source_target_pairs={{0,64},{16,976},{32,96},{48,1008},{64,128},{80,16},{96,160},{112,4... | collective-permute-start | bytes 688136 | tf_op jit(solution)/shard_map/ppermute | solution.py:275
  74.9 4.9 %all-to-all-start.1 = ((bf16[16,504,128]{2,1,0:T(8,128)(2,1)}), bf16[16,504,128]{2,1,0:T(8,128)(2,1)S(1)}, u32[]{:S(2)}, u32[]{:S(2)}) async-start(bf16[16,504,128]{2,1,0:T(8,128)(2,1)} %grad_rows.1), calls=%async_computation.1 | async-start | bytes 4128768 | tf_op jit(solution)/shard_map/all_to_all | solution.py:288
  79.8 5.5 %collective-permute-done.2 = bf16[16,7168]{1,0:T(8,128)(2,1)S(1)} collective-permute-done((bf16[16,7168]{1,0:T(8,128)(2,1)S(1)}, bf16[16,7168]{1,0:T(8,128)(2,1)S(1)}, u32[]{:S(2)}, u32[]{:S(2)}) %collective-permute-start.2) | collective-permute-done | bytes 229408 | tf_op jit(solution)/shard_map/ppermute | solution.py:275
  85.3 1.9 %collective-permute-start.3 = (bf16[8,7168]{1,0:T(8,128)(2,1)S(1)}, bf16[8,7168]{1,0:T(8,128)(2,1)S(1)}, u32[]{:S(2)}, u32[]{:S(2)}) collective-permute-start(bf16[8,7168]{1,0:T(8,128)(2,1)S(1)} %get-tuple-element.34), channel_id=1, source_target_pairs={{0,128},{16,912},{32,160},{48,944},{64,192},{80,976},{96,224},{112... | collective-permute-start | bytes 344072 | tf_op jit(solution)/shard_map/ppermute | solution.py:275
  87.2 12.4 %collective-permute-done.3.coming_ref = bf16[8,7168]{1,0:T(8,128)(2,1)S(1)} collective-permute-done((bf16[8,7168]{1,0:T(8,128)(2,1)S(1)}, bf16[8,7168]{1,0:T(8,128)(2,1)S(1)}, u32[]{:S(2)}, u32[]{:S(2)}) %collective-permute-start.3) | collective-permute-done | bytes 114720 | tf_op jit(solution)/shard_map/ppermute | solution.py:275
  99.6 0.2 fold.1
  99.7 1.9 %collective-permute-start.4 = (bf16[2,112,128]{2,1,0:T(8,128)(2,1)S(1)}, bf16[2,112,128]{2,1,0:T(8,128)(2,1)S(1)}, u32[]{:S(2)}, u32[]{:S(2)}) collective-permute-start(bf16[2,112,128]{2,1,0:T(8,128)(2,1)S(1)} %get-tuple-element.25), channel_id=1, source_target_pairs={{0,256},{16,784},{32,288},{48,816},{64,320},{80,848},{96,352},{112... | collective-permute-start | bytes 172040 | tf_op jit(solution)/shard_map/ppermute | solution.py:275
  101.7 13.3 %collective-permute-done.4 = bf16[2,112,128]{2,1,0:T(8,128)(2,1)S(1)} collective-permute-done((bf16[2,112,128]{2,1,0:T(8,128)(2,1)S(1)}, bf16[2,112,128]{2,1,0:T(8,128)(2,1)S(1)}, u32[]{:S(2)}, u32[]{:S(2)}) %collective-permute-start.4) | collective-permute-done | bytes 57376 | tf_op jit(solution)/shard_map/ppermute | solution.py:275
  114.9 14.9 %collective-permute-start.5 = (bf16[1,112,128]{2,1,0:T(8,128)(2,1)S(1)}, bf16[1,112,128]{2,1,0:T(8,128)(2,1)S(1)}, u32[]{:S(2)}, u32[]{:S(2)}) collective-permute-start(bf16[1,112,128]{2,1,0:T(8,128)(2,1)S(1)} %get-tuple-element.37), channel_id=1, source_target_pairs={{0,512},{16,528},{32,544},{48,560},{64,576},{80,592},{96,608},{112... | collective-permute-start | bytes 86024 | tf_op jit(solution)/shard_map/ppermute | solution.py:275
  129.9 0.0 all-to-all-done.1.got_ref
  129.9 1.4 %combine_rows.1 = bf16[32,7168]{1,0:T(8,128)(2,1)} custom-call(bf16[144,32]{1,0:T(8,128)(2,1)S(1)} %get-tuple-element.26.pick_ref, bf16[16,504,128]{2,1,0:T(8,128)(2,1)S(1)} %all-to-all-done.1.got_ref), custom_call_target="tpu_custom_call" | custom-call | tf_op jit(solution)/shard_map/combine_rows/pallas_call | solution.py:306
  131.3 7.8 %collective-permute-done.5.coming_ref = bf16[1,112,128]{2,1,0:T(8,128)(2,1)S(1)} collective-permute-done((bf16[1,112,128]{2,1,0:T(8,128)(2,1)S(1)}, bf16[1,112,128]{2,1,0:T(8,128)(2,1)S(1)}, u32[]{:S(2)}, u32[]{:S(2)}) %collective-permute-start.5) | collective-permute-done | bytes 28704 | tf_op jit(solution)/shard_map/ppermute | solution.py:275
  139.0 0.7 finish.1
  (2 shorter events, 0.1 us)
Async XLA Ops:
  3.4 36.2 %copy-start.3 = (bf16[144,256]{1,0:T(8,128)(2,1)S(1)}, bf16[144,256]{1,0:T(8,128)(2,1)}, u32[]{:S(2)}) copy-start(bf16[144,256]{1,0:T(8,128)(2,1)} %pre_ref.1) | copy-start | bytes 221188
  3.4 36.2 %all-to-all-start = ((bf16[16,504,128]{2,1,0:T(8,128)(2,1)}), bf16[16,504,128]{2,1,0:T(8,128)(2,1)S(1)}, u32[]{:S(2)}, u32[]{:S(2)}) async-start(bf16[16,504,128]{2,1,0:T(8,128)(2,1)} %get-tuple-element.16), calls=%async_computation | async-start | bytes 4128768 | tf_op jit(solution)/shard_map/all_to_all | solution.py:227
  39.6 3.9 %copy-start = (bf16[1,128,7168]{2,1,0:T(8,128)(2,1)S(1)}, bf16[1,128,7168]{2,1,0:T(8,128)(2,1)}, u32[]{:S(2)}) copy-start(bf16[1,128,7168]{2,1,0:T(8,128)(2,1)} %down_ref.1) | copy-start | bytes 5505028
  41.6 4.4 %collective-permute-start = (bf16[64,7168]{1,0:T(8,128)(2,1)S(1)}, bf16[64,7168]{1,0:T(8,128)(2,1)S(1)}, u32[]{:S(2)}, u32[]{:S(2)}) collective-permute-start(bf16[64,7168]{1,0:T(8,128)(2,1)S(1)} %get-tuple-element.18), channel_id=1, source_target_pairs={{0,16},{16,0},{32,48},{48,32},{64,80},{80,64},{96,112},{112,96},{1... | collective-permute-start | bytes 2752520 | tf_op jit(solution)/shard_map/ppermute | solution.py:245
  45.9 5.6 %copy-start.1 = (bf16[1,7168,128]{2,1,0:T(8,128)(2,1)S(1)}, bf16[1,7168,128]{2,1,0:T(8,128)(2,1)}, u32[]{:S(2)}) copy-start(bf16[1,7168,128]{2,1,0:T(8,128)(2,1)} %gate_ref.1) | copy-start | bytes 5505028
  45.9 5.6 %copy-start.2 = (bf16[1,7168,128]{2,1,0:T(8,128)(2,1)S(1)}, bf16[1,7168,128]{2,1,0:T(8,128)(2,1)}, u32[]{:S(2)}) copy-start(bf16[1,7168,128]{2,1,0:T(8,128)(2,1)} %up_ref.1) | copy-start | bytes 5505028
  46.2 26.7 %collective-permute-start.1 = (bf16[32,7168]{1,0:T(8,128)(2,1)S(1)}, bf16[32,7168]{1,0:T(8,128)(2,1)S(1)}, u32[]{:S(2)}, u32[]{:S(2)}) collective-permute-start(bf16[32,7168]{1,0:T(8,128)(2,1)S(1)} %get-tuple-element.30), channel_id=1, source_target_pairs={{0,32},{16,1008},{32,64},{48,16},{64,96},{80,48},{96,128},{112,80}... | collective-permute-start | bytes 1376264 | tf_op jit(solution)/shard_map/ppermute | solution.py:275
  72.9 12.3 %collective-permute-start.2 = (bf16[16,7168]{1,0:T(8,128)(2,1)S(1)}, bf16[16,7168]{1,0:T(8,128)(2,1)S(1)}, u32[]{:S(2)}, u32[]{:S(2)}) collective-permute-start(bf16[16,7168]{1,0:T(8,128)(2,1)S(1)} %get-tuple-element.32), channel_id=1, source_target_pairs={{0,64},{16,976},{32,96},{48,1008},{64,128},{80,16},{96,160},{112,4... | collective-permute-start | bytes 688136 | tf_op jit(solution)/shard_map/ppermute | solution.py:275
  74.9 55.0 %all-to-all-start.1 = ((bf16[16,504,128]{2,1,0:T(8,128)(2,1)}), bf16[16,504,128]{2,1,0:T(8,128)(2,1)S(1)}, u32[]{:S(2)}, u32[]{:S(2)}) async-start(bf16[16,504,128]{2,1,0:T(8,128)(2,1)} %grad_rows.1), calls=%async_computation.1 | async-start | bytes 4128768 | tf_op jit(solution)/shard_map/all_to_all | solution.py:288
  85.3 14.3 %collective-permute-start.3 = (bf16[8,7168]{1,0:T(8,128)(2,1)S(1)}, bf16[8,7168]{1,0:T(8,128)(2,1)S(1)}, u32[]{:S(2)}, u32[]{:S(2)}) collective-permute-start(bf16[8,7168]{1,0:T(8,128)(2,1)S(1)} %get-tuple-element.34), channel_id=1, source_target_pairs={{0,128},{16,912},{32,160},{48,944},{64,192},{80,976},{96,224},{112... | collective-permute-start | bytes 344072 | tf_op jit(solution)/shard_map/ppermute | solution.py:275
  99.7 15.2 %collective-permute-start.4 = (bf16[2,112,128]{2,1,0:T(8,128)(2,1)S(1)}, bf16[2,112,128]{2,1,0:T(8,128)(2,1)S(1)}, u32[]{:S(2)}, u32[]{:S(2)}) collective-permute-start(bf16[2,112,128]{2,1,0:T(8,128)(2,1)S(1)} %get-tuple-element.25), channel_id=1, source_target_pairs={{0,256},{16,784},{32,288},{48,816},{64,320},{80,848},{96,352},{112... | collective-permute-start | bytes 172040 | tf_op jit(solution)/shard_map/ppermute | solution.py:275
  114.9 24.1 %collective-permute-start.5 = (bf16[1,112,128]{2,1,0:T(8,128)(2,1)S(1)}, bf16[1,112,128]{2,1,0:T(8,128)(2,1)S(1)}, u32[]{:S(2)}, u32[]{:S(2)}) collective-permute-start(bf16[1,112,128]{2,1,0:T(8,128)(2,1)S(1)} %get-tuple-element.37), channel_id=1, source_target_pairs={{0,512},{16,528},{32,544},{48,560},{64,576},{80,592},{96,608},{112... | collective-permute-start | bytes 86024 | tf_op jit(solution)/shard_map/ppermute | solution.py:275

commit v5 on v4

--- a/solution.py
+++ b/solution.py
@@ -12,6 +12,8 @@
 LANES = 128
 FIRST = 8
 PARTS = 4
+HOPS = (1, -2, 4)
+RING = 4
 PARAMS = pltpu.CompilerParams(vmem_limit_bytes=16 * 1024 * 1024)
 
 
@@ -132,11 +134,10 @@
     core = jnp.where(at < half, at_ref[1], 1 - at_ref[1])
     share = half // chips
     place = at % half // share
-    far = jnp.zeros_like(place)
-    bits = chips.bit_length() - 1
-    for bit in range(bits):
-        far = far + (place // 2**bit) % 2 * 2 ** (bits - 1 - bit)
-    chip = (at_ref[0] + (1 - 2 * core) * far + chips) % chips
+    far = place % RING * (HOPS[-1] * 2 * -1)
+    for bit, hop in enumerate(reversed(HOPS)):
+        far = far + place // (RING * 2**bit) % 2 * hop
+    chip = (at_ref[0] + (1 - 2 * core) * far + 2 * chips) % chips
     target = (2 * chip + core) * share + at % share
     hidden = dot(hidden, jnp.where(unit == target, 1.0, 0.0).astype(BF), ((1,), (0,))).astype(BF)
     tail[...] = got_ref[:, experts_rows(width) :, :].astype(F32)
@@ -175,18 +176,23 @@
         ).astype(BF)
 
 
-def fold_kernel(total_ref, coming_ref, keep_ref, send_ref, lines):
+def fold_kernel(total_ref, coming_ref, own_ref, next_ref, opposite_ref, previous_ref, lines):
     for c in range(lines.shape[1]):
         at = slice(c * LANES, (c + 1) * LANES)
         lines[:, c, :] = total_ref[:, at] + coming_ref[:, at].astype(F32)
-    count = keep_ref.shape[0]
-    pieces = lines[...].reshape((2 * count,) + keep_ref.shape[1:])
-    keep_ref[...] = pieces[:count]
-    send_ref[...] = pieces[count:].astype(BF)
-
-
-def finish_kernel(scale, total_ref, coming_ref, out_ref, lines):
-    lines[...] = ((total_ref[0] + coming_ref[0].astype(F32)) * scale).reshape(lines.shape)
+    pieces = lines[...].reshape((RING,) + own_ref.shape)
+    own_ref[...] = pieces[0]
+    next_ref[...] = pieces[1].astype(BF)
+    opposite_ref[...] = pieces[2].astype(BF)
+    previous_ref[...] = pieces[3].astype(BF)
+
+
+def finish_kernel(scale, own_ref, *refs):
+    *coming, out_ref, lines = refs
+    total = own_ref[...]
+    for ref in coming:
+        total = total + ref[...].astype(F32)
+    lines[...] = (total * scale).reshape(lines.shape)
     for c in range(lines.shape[1]):
         out_ref[0, :, c * LANES : (c + 1) * LANES] = lines[:, c, :]
 
@@ -201,7 +207,7 @@
     assert capacity == FIRST + 1
     block_rows = capacity * width // LANES
     chips = replicas // 2
-    assert chips & (chips - 1) == 0 and hidden_units % replicas == 0
+    assert chips == 2 ** len(HOPS) * RING and hidden_units % replicas == 0
     shape = jax.ShapeDtypeStruct
     vmem = pl.BlockSpec(memory_space=pltpu.VMEM)
     smem = pl.BlockSpec(memory_space=pltpu.SMEM)
@@ -275,34 +281,27 @@
         return lax.ppermute(going, "dp", hops)
 
     share = hidden_units // replicas
-    lines = share * width // LANES
-    total, coming, count, distance = keep, other, half, 1
-    while count > 8:
+    total, coming, count = keep, other, half
+    for hop in HOPS:
         count //= 2
         going = (total[count:] + coming[count:].astype(F32)).astype(BF)
         total = lax.optimization_barrier(total[:count] + coming[:count].astype(F32))
-        coming = pass_on(going, distance)
-        if distance == 1:
+        coming = pass_on(going, hop)
+        if hop == HOPS[0]:
             coming, going_back = lax.optimization_barrier((coming, going_back))
-        distance *= 2
     returned = lax.all_to_all(going_back, "expert", split_axis=0, concat_axis=0, tiled=True)
-    count = count // share // 2
-    total, going = pl.pallas_call(
+    piece = (share * width // LANES, LANES)
+    own, ahead, opposite, previous = pl.pallas_call(
         fold_kernel,
-        out_shape=(shape((count, lines, LANES), F32), shape((count, lines, LANES), BF)),
+        out_shape=(shape(piece, F32),) + (shape(piece, BF),) * 3,
         in_specs=[vmem] * 2,
-        out_specs=(vmem, vmem),
-        scratch_shapes=[pltpu.VMEM((2 * count * share, width // LANES, LANES), F32)],
+        out_specs=(vmem,) * 4,
+        scratch_shapes=[pltpu.VMEM((count, width // LANES, LANES), F32)],
         compiler_params=PARAMS,
         name="fold",
     )(total, coming)
-    coming = pass_on(going, distance)
-    while count > 1:
-        count //= 2
-        distance *= 2
-        going = (total[count:] + coming[count:].astype(F32)).astype(BF)
-        total = lax.optimization_barrier(total[:count] + coming[:count].astype(F32))
-        coming = pass_on(going, distance)
+    stride = -2 * HOPS[-1]
+    parts = [pass_on(opposite, 2 * stride), pass_on(ahead, stride), pass_on(previous, -stride)]
     grad_tokens = pl.pallas_call(
         functools.partial(combine_kernel, experts),
         out_shape=shape((tokens, width), BF),
@@ -312,16 +311,16 @@
         compiler_params=PARAMS,
         name="combine_rows",
     )(pick, returned)
-    coming, grad_tokens = lax.optimization_barrier((coming, grad_tokens))
+    parts[0], grad_tokens = lax.optimization_barrier((parts[0], grad_tokens))
     grad_down = pl.pallas_call(
         functools.partial(finish_kernel, 1.0 / replicas),
         out_shape=shape((1, share, width), F32),
-        in_specs=[vmem] * 2,
+        in_specs=[vmem] * RING,
         out_specs=vmem,
         scratch_shapes=[pltpu.VMEM((share, width // LANES, LANES), F32)],
         compiler_params=PARAMS,
         name="finish",
-    )(total, coming)
+    )(own, *parts)
     return (grad_tokens, grad_down)
 
 

time: 140 us -> 131 us (0.936)
  the two profiles are of different devices: /device:TPU:8 before, /device:TPU:33 now
where the time goes in v5:
time: 131 us; the launch traced here: 130 us
  waiting for transfers between devices  60 us (46%)
  starting transfers between devices  59 us (45%)
  Pallas kernels  10 us (8%)
    ppermute x6, starting transfers between devices, pass_on(): return lax.ppermute(going, 'dp', hops)  44.3 us
    all_to_all x1, waiting for transfers between devices, per_device(): lax.all_to_all(outgoing, 'expert', split_axis=0, concat_axis=0, tiled=True)  29.9 us
    ppermute x6, waiting for transfers between devices, pass_on(): return lax.ppermute(going, 'dp', hops)  28.7 us
    all_to_all x1, starting transfers between devices, per_device(): lax.all_to_all(outgoing, 'expert', split_axis=0, concat_axis=0, tiled=True)  6.9 us
    ppermute x1, starting transfers between devices, per_device(): other = lax.ppermute(send, 'dp', [(i, i ^ 1) for i in range(replicas)])  4.04 us
    all_to_all x1, starting transfers between devices, per_device(): lax.all_to_all(going_back, 'expert', split_axis=0, concat_axis=0, tiled=T...  3.73 us
    pallas_call x1, Pallas kernels, per_device(): pl.pallas_call(functools.partial(dispatch_kernel, experts), out_shape=(pl...  2.71 us
  transfers between devices with their start and end apart: 9, of which 6 were waited for; matrix products, arithmetic and copies ran while one was open for 0% of the time, Pallas kernels for 4%

profile of v5, /device:TPU:33, one launch (start us, length us, event | category | flops | bytes accessed | tf_op | source)
XLA Modules:
  0.0 130.2 jit_solution(8424290775586259904)
XLA Ops:
  0.6 2.7 %dispatch_rows.1 = (bf16[16,504,128]{2,1,0:T(8,128)(2,1)}, bf16[144,32]{1,0:T(8,128)(2,1)S(1)}) custom-call(bf16[32,7168]{1,0:T(8,128)(2,1)} %dy_hbm.1, s32[4,32]{1,0:T(4,128)} %bitcast.4, f32[4,32]{1,0:T(4,128)} %bitcast.5), custom_call_target="tpu_custom_call" | custom-call | tf_op jit(solution)/shard_map/dispatch_rows/pallas_call | solution.py:217
  3.3 0.0 copy-start.3
  3.4 6.9 %all-to-all-start = ((bf16[16,504,128]{2,1,0:T(8,128)(2,1)}), bf16[16,504,128]{2,1,0:T(8,128)(2,1)S(1)}, u32[]{:S(2)}, u32[]{:S(2)}) async-start(bf16[16,504,128]{2,1,0:T(8,128)(2,1)} %get-tuple-element.18), calls=%async_computation | async-start | bytes 4128768 | tf_op jit(solution)/shard_map/all_to_all | solution.py:233
  10.3 0.1 pad_add_fusion.at_ref
  10.4 29.9 %all-to-all-done.got_ref = bf16[16,504,128]{2,1,0:T(8,128)(2,1)S(1)} async-done(((bf16[16,504,128]{2,1,0:T(8,128)(2,1)}), bf16[16,504,128]{2,1,0:T(8,128)(2,1)S(1)}, u32[]{:S(2)}, u32[]{:S(2)}) %all-to-all-start) | async-done | bytes 2064416 | tf_op jit(solution)/shard_map/all_to_all | solution.py:233
  40.3 0.0 copy-done.3
  40.3 0.0 copy-start
  40.3 2.0 %down_partial.1 = (bf16[144,7168]{1,0:T(8,128)(2,1)S(1)}, f32[64,7168]{1,0:T(8,128)S(1)}, bf16[64,7168]{1,0:T(8,128)(2,1)S(1)}, f32[144,256]{1,0:T(8,128)S(1)}) custom-call(s32[2]{0:T(128)S(1)} %pad_add_fusion.at_ref, bf16[16,504,128]{2,1,0:T(8,128)(2,1)S(1)} %all-to-all-done.got_ref, bf16[144,256]{1,0:T(8,128)(2,1)S(1)} %copy-done.3), custom_call_target="tpu_custom_call" | custom-call | tf_op jit(solution)/shard_map/down_partial/pallas_call | solution.py:237
  42.3 4.0 %collective-permute-start = (bf16[64,7168]{1,0:T(8,128)(2,1)S(1)}, bf16[64,7168]{1,0:T(8,128)(2,1)S(1)}, u32[]{:S(2)}, u32[]{:S(2)}) collective-permute-start(bf16[64,7168]{1,0:T(8,128)(2,1)S(1)} %get-tuple-element.20), channel_id=1, source_target_pairs={{0,16},{16,0},{32,48},{48,32},{64,80},{80,64},{96,112},{112,96},{1... | collective-permute-start | bytes 2752520 | tf_op jit(solution)/shard_map/ppermute | solution.py:251
  46.3 0.0 copy-done
  46.4 0.7 grad_hidden.1.hidden_ref
  47.1 1.4 %collective-permute-done = bf16[64,7168]{1,0:T(8,128)(2,1)S(1)} collective-permute-done((bf16[64,7168]{1,0:T(8,128)(2,1)S(1)}, bf16[64,7168]{1,0:T(8,128)(2,1)S(1)}, u32[]{:S(2)}, u32[]{:S(2)}) %collective-permute-start) | collective-permute-done | bytes 917536 | tf_op jit(solution)/shard_map/ppermute | solution.py:251
  48.4 0.0 copy-start.1
  48.4 0.0 copy-start.2
  48.4 0.2 add_convert_fusion
  48.6 2.2 %collective-permute-start.1 = (bf16[32,7168]{1,0:T(8,128)(2,1)S(1)}, bf16[32,7168]{1,0:T(8,128)(2,1)S(1)}, u32[]{:S(2)}, u32[]{:S(2)}) collective-permute-start(bf16[32,7168]{1,0:T(8,128)(2,1)S(1)} %get-tuple-element.34), channel_id=1, source_target_pairs={{0,32},{16,1008},{32,64},{48,16},{64,96},{80,48},{96,128},{112,80}... | collective-permute-start | bytes 1376264 | tf_op jit(solution)/shard_map/ppermute | solution.py:281
  50.9 0.0 copy-done.1
  50.9 0.0 copy-done.2
  50.9 2.3 %grad_rows.1 = bf16[16,504,128]{2,1,0:T(8,128)(2,1)} custom-call(bf16[144,256]{1,0:T(8,128)(2,1)S(1)} %grad_hidden.1.hidden_ref, bf16[1,7168,128]{2,1,0:T(8,128)(2,1)S(1)} %copy-done.1, bf16[1,7168,128]{2,1,0:T(8,128)(2,1)S(1)} %copy-done.2), custom_call_target="tpu_custom_call" | custom-call | tf_op jit(solution)/shard_map/grad_rows/pallas_call | solution.py:262
  53.2 5.4 %collective-permute-done.1 = bf16[32,7168]{1,0:T(8,128)(2,1)S(1)} collective-permute-done((bf16[32,7168]{1,0:T(8,128)(2,1)S(1)}, bf16[32,7168]{1,0:T(8,128)(2,1)S(1)}, u32[]{:S(2)}, u32[]{:S(2)}) %collective-permute-start.1) | collective-permute-done | bytes 458784 | tf_op jit(solution)/shard_map/ppermute | solution.py:281
  58.6 0.1 fusion
  58.7 5.8 %collective-permute-start.2 = (bf16[16,7168]{1,0:T(8,128)(2,1)S(1)}, bf16[16,7168]{1,0:T(8,128)(2,1)S(1)}, u32[]{:S(2)}, u32[]{:S(2)}) collective-permute-start(bf16[16,7168]{1,0:T(8,128)(2,1)S(1)} %get-tuple-element.36), channel_id=1, source_target_pairs={{0,960},{16,80},{32,992},{48,112},{64,0},{80,144},{96,32},{112,176... | collective-permute-start | bytes 688136 | tf_op jit(solution)/shard_map/ppermute | solution.py:281
  64.5 3.7 %all-to-all-start.1 = ((bf16[16,504,128]{2,1,0:T(8,128)(2,1)}), bf16[16,504,128]{2,1,0:T(8,128)(2,1)S(1)}, u32[]{:S(2)}, u32[]{:S(2)}) async-start(bf16[16,504,128]{2,1,0:T(8,128)(2,1)} %grad_rows.1), calls=%async_computation.1 | async-start | bytes 4128768 | tf_op jit(solution)/shard_map/all_to_all | solution.py:292
  68.3 15.0 %collective-permute-done.2 = bf16[16,7168]{1,0:T(8,128)(2,1)S(1)} collective-permute-done((bf16[16,7168]{1,0:T(8,128)(2,1)S(1)}, bf16[16,7168]{1,0:T(8,128)(2,1)S(1)}, u32[]{:S(2)}, u32[]{:S(2)}) %collective-permute-start.2) | collective-permute-done | bytes 229408 | tf_op jit(solution)/shard_map/ppermute | solution.py:281
  83.3 5.5 %collective-permute-start.3 = (bf16[8,7168]{1,0:T(8,128)(2,1)S(1)}, bf16[8,7168]{1,0:T(8,128)(2,1)S(1)}, u32[]{:S(2)}, u32[]{:S(2)}) collective-permute-start(bf16[8,7168]{1,0:T(8,128)(2,1)S(1)} %get-tuple-element.38), channel_id=1, source_target_pairs={{0,128},{16,912},{32,160},{48,944},{64,192},{80,976},{96,224},{112... | collective-permute-start | bytes 344072 | tf_op jit(solution)/shard_map/ppermute | solution.py:281
  88.8 4.3 %collective-permute-done.3.coming_ref = bf16[8,7168]{1,0:T(8,128)(2,1)S(1)} collective-permute-done((bf16[8,7168]{1,0:T(8,128)(2,1)S(1)}, bf16[8,7168]{1,0:T(8,128)(2,1)S(1)}, u32[]{:S(2)}, u32[]{:S(2)}) %collective-permute-start.3) | collective-permute-done | bytes 114720 | tf_op jit(solution)/shard_map/ppermute | solution.py:281
  93.0 0.2 fold.1
  93.2 16.8 %collective-permute-start.4 = (bf16[112,128]{1,0:T(8,128)(2,1)S(1)}, bf16[112,128]{1,0:T(8,128)(2,1)S(1)}, u32[]{:S(2)}, u32[]{:S(2)}) collective-permute-start(bf16[112,128]{1,0:T(8,128)(2,1)S(1)} %get-tuple-element.26), channel_id=1, source_target_pairs={{0,512},{16,528},{32,544},{48,560},{64,576},{80,592},{96,608},{112... | collective-permute-start | bytes 86024 | tf_op jit(solution)/shard_map/ppermute | solution.py:281
  110.0 5.1 %collective-permute-start.5 = (bf16[112,128]{1,0:T(8,128)(2,1)S(1)}, bf16[112,128]{1,0:T(8,128)(2,1)S(1)}, u32[]{:S(2)}, u32[]{:S(2)}) collective-permute-start(bf16[112,128]{1,0:T(8,128)(2,1)S(1)} %get-tuple-element.32), channel_id=1, source_target_pairs={{0,768},{16,272},{32,800},{48,304},{64,832},{80,336},{96,864},{112... | collective-permute-start | bytes 86024 | tf_op jit(solution)/shard_map/ppermute | solution.py:281
  115.1 8.9 %collective-permute-start.6 = (bf16[112,128]{1,0:T(8,128)(2,1)S(1)}, bf16[112,128]{1,0:T(8,128)(2,1)S(1)}, u32[]{:S(2)}, u32[]{:S(2)}) collective-permute-start(bf16[112,128]{1,0:T(8,128)(2,1)S(1)} %get-tuple-element.33), channel_id=1, source_target_pairs={{0,256},{16,784},{32,288},{48,816},{64,320},{80,848},{96,352},{112... | collective-permute-start | bytes 86024 | tf_op jit(solution)/shard_map/ppermute | solution.py:281
  124.0 0.0 all-to-all-done.1.got_ref
  124.0 1.4 %combine_rows.1 = bf16[32,7168]{1,0:T(8,128)(2,1)} custom-call(bf16[144,32]{1,0:T(8,128)(2,1)S(1)} %get-tuple-element.27.pick_ref, bf16[16,504,128]{2,1,0:T(8,128)(2,1)S(1)} %all-to-all-done.1.got_ref), custom_call_target="tpu_custom_call" | custom-call | tf_op jit(solution)/shard_map/combine_rows/pallas_call | solution.py:305
  125.5 0.0 collective-permute-done.4.refs_0_
  125.5 0.0 collective-permute-done.5.refs_1_
  125.5 4.1 %collective-permute-done.6.refs_2_ = bf16[112,128]{1,0:T(8,128)(2,1)S(1)} collective-permute-done((bf16[112,128]{1,0:T(8,128)(2,1)S(1)}, bf16[112,128]{1,0:T(8,128)(2,1)S(1)}, u32[]{:S(2)}, u32[]{:S(2)}) %collective-permute-start.6) | collective-permute-done | bytes 28704 | tf_op jit(solution)/shard_map/ppermute | solution.py:281
  129.5 0.7 finish.1
  (1 shorter events, 0.0 us)
Async XLA Ops:
  3.3 36.9 %copy-start.3 = (bf16[144,256]{1,0:T(8,128)(2,1)S(1)}, bf16[144,256]{1,0:T(8,128)(2,1)}, u32[]{:S(2)}) copy-start(bf16[144,256]{1,0:T(8,128)(2,1)} %pre_ref.1) | copy-start | bytes 221188
  3.4 36.9 %all-to-all-start = ((bf16[16,504,128]{2,1,0:T(8,128)(2,1)}), bf16[16,504,128]{2,1,0:T(8,128)(2,1)S(1)}, u32[]{:S(2)}, u32[]{:S(2)}) async-start(bf16[16,504,128]{2,1,0:T(8,128)(2,1)} %get-tuple-element.18), calls=%async_computation | async-start | bytes 4128768 | tf_op jit(solution)/shard_map/all_to_all | solution.py:233
  40.3 6.1 %copy-start = (bf16[1,128,7168]{2,1,0:T(8,128)(2,1)S(1)}, bf16[1,128,7168]{2,1,0:T(8,128)(2,1)}, u32[]{:S(2)}) copy-start(bf16[1,128,7168]{2,1,0:T(8,128)(2,1)} %down_ref.1) | copy-start | bytes 5505028
  42.3 6.1 %collective-permute-start = (bf16[64,7168]{1,0:T(8,128)(2,1)S(1)}, bf16[64,7168]{1,0:T(8,128)(2,1)S(1)}, u32[]{:S(2)}, u32[]{:S(2)}) collective-permute-start(bf16[64,7168]{1,0:T(8,128)(2,1)S(1)} %get-tuple-element.20), channel_id=1, source_target_pairs={{0,16},{16,0},{32,48},{48,32},{64,80},{80,64},{96,112},{112,96},{1... | collective-permute-start | bytes 2752520 | tf_op jit(solution)/shard_map/ppermute | solution.py:251
  48.4 2.5 %copy-start.1 = (bf16[1,7168,128]{2,1,0:T(8,128)(2,1)S(1)}, bf16[1,7168,128]{2,1,0:T(8,128)(2,1)}, u32[]{:S(2)}) copy-start(bf16[1,7168,128]{2,1,0:T(8,128)(2,1)} %gate_ref.1) | copy-start | bytes 5505028
  48.4 2.5 %copy-start.2 = (bf16[1,7168,128]{2,1,0:T(8,128)(2,1)S(1)}, bf16[1,7168,128]{2,1,0:T(8,128)(2,1)}, u32[]{:S(2)}) copy-start(bf16[1,7168,128]{2,1,0:T(8,128)(2,1)} %up_ref.1) | copy-start | bytes 5505028
  48.6 10.0 %collective-permute-start.1 = (bf16[32,7168]{1,0:T(8,128)(2,1)S(1)}, bf16[32,7168]{1,0:T(8,128)(2,1)S(1)}, u32[]{:S(2)}, u32[]{:S(2)}) collective-permute-start(bf16[32,7168]{1,0:T(8,128)(2,1)S(1)} %get-tuple-element.34), channel_id=1, source_target_pairs={{0,32},{16,1008},{32,64},{48,16},{64,96},{80,48},{96,128},{112,80}... | collective-permute-start | bytes 1376264 | tf_op jit(solution)/shard_map/ppermute | solution.py:281
  58.7 24.5 %collective-permute-start.2 = (bf16[16,7168]{1,0:T(8,128)(2,1)S(1)}, bf16[16,7168]{1,0:T(8,128)(2,1)S(1)}, u32[]{:S(2)}, u32[]{:S(2)}) collective-permute-start(bf16[16,7168]{1,0:T(8,128)(2,1)S(1)} %get-tuple-element.36), channel_id=1, source_target_pairs={{0,960},{16,80},{32,992},{48,112},{64,0},{80,144},{96,32},{112,176... | collective-permute-start | bytes 688136 | tf_op jit(solution)/shard_map/ppermute | solution.py:281
  64.5 59.5 %all-to-all-start.1 = ((bf16[16,504,128]{2,1,0:T(8,128)(2,1)}), bf16[16,504,128]{2,1,0:T(8,128)(2,1)S(1)}, u32[]{:S(2)}, u32[]{:S(2)}) async-start(bf16[16,504,128]{2,1,0:T(8,128)(2,1)} %grad_rows.1), calls=%async_computation.1 | async-start | bytes 4128768 | tf_op jit(solution)/shard_map/all_to_all | solution.py:292
  83.3 9.7 %collective-permute-start.3 = (bf16[8,7168]{1,0:T(8,128)(2,1)S(1)}, bf16[8,7168]{1,0:T(8,128)(2,1)S(1)}, u32[]{:S(2)}, u32[]{:S(2)}) collective-permute-start(bf16[8,7168]{1,0:T(8,128)(2,1)S(1)} %get-tuple-element.38), channel_id=1, source_target_pairs={{0,128},{16,912},{32,160},{48,944},{64,192},{80,976},{96,224},{112... | collective-permute-start | bytes 344072 | tf_op jit(solution)/shard_map/ppermute | solution.py:281
  93.2 32.3 %collective-permute-start.4 = (bf16[112,128]{1,0:T(8,128)(2,1)S(1)}, bf16[112,128]{1,0:T(8,128)(2,1)S(1)}, u32[]{:S(2)}, u32[]{:S(2)}) collective-permute-start(bf16[112,128]{1,0:T(8,128)(2,1)S(1)} %get-tuple-element.26), channel_id=1, source_target_pairs={{0,512},{16,528},{32,544},{48,560},{64,576},{80,592},{96,608},{112... | collective-permute-start | bytes 86024 | tf_op jit(solution)/shard_map/ppermute | solution.py:281
  110.0 15.4 %collective-permute-start.5 = (bf16[112,128]{1,0:T(8,128)(2,1)S(1)}, bf16[112,128]{1,0:T(8,128)(2,1)S(1)}, u32[]{:S(2)}, u32[]{:S(2)}) collective-permute-start(bf16[112,128]{1,0:T(8,128)(2,1)S(1)} %get-tuple-element.32), channel_id=1, source_target_pairs={{0,768},{16,272},{32,800},{48,304},{64,832},{80,336},{96,864},{112... | collective-permute-start | bytes 86024 | tf_op jit(solution)/shard_map/ppermute | solution.py:281
  115.1 14.4 %collective-permute-start.6 = (bf16[112,128]{1,0:T(8,128)(2,1)S(1)}, bf16[112,128]{1,0:T(8,128)(2,1)S(1)}, u32[]{:S(2)}, u32[]{:S(2)}) collective-permute-start(bf16[112,128]{1,0:T(8,128)(2,1)S(1)} %get-tuple-element.33), channel_id=1, source_target_pairs={{0,256},{16,784},{32,288},{48,816},{64,320},{80,848},{96,352},{112... | collective-permute-start | bytes 86024 | tf_op jit(solution)/shard_map/ppermute | solution.py:281

commit v6 on v5

--- a/solution.py
+++ b/solution.py
@@ -12,8 +12,8 @@
 LANES = 128
 FIRST = 8
 PARTS = 4
-HOPS = (1, -2, 4)
-RING = 4
+NEAR = (0, -2, -4, 2)
+FAR = (0, 8, 16, -8)
 PARAMS = pltpu.CompilerParams(vmem_limit_bytes=16 * 1024 * 1024)
 
 
@@ -134,9 +134,10 @@
     core = jnp.where(at < half, at_ref[1], 1 - at_ref[1])
     share = half // chips
     place = at % half // share
-    far = place % RING * (HOPS[-1] * 2 * -1)
-    for bit, hop in enumerate(reversed(HOPS)):
-        far = far + place // (RING * 2**bit) % 2 * hop
+    far = place // (len(NEAR) * len(FAR))
+    for move in range(len(NEAR)):
+        far = far + jnp.where(place // len(FAR) % len(NEAR) == move, NEAR[move], 0)
+        far = far + jnp.where(place % len(FAR) == move, FAR[move], 0)
     chip = (at_ref[0] + (1 - 2 * core) * far + 2 * chips) % chips
     target = (2 * chip + core) * share + at % share
     hidden = dot(hidden, jnp.where(unit == target, 1.0, 0.0).astype(BF), ((1,), (0,))).astype(BF)
@@ -176,15 +177,19 @@
         ).astype(BF)
 
 
-def fold_kernel(total_ref, coming_ref, own_ref, next_ref, opposite_ref, previous_ref, lines):
+def fold_kernel(total_ref, *refs):
+    *coming, own_ref, first_ref, second_ref, third_ref, lines = refs
     for c in range(lines.shape[1]):
         at = slice(c * LANES, (c + 1) * LANES)
-        lines[:, c, :] = total_ref[:, at] + coming_ref[:, at].astype(F32)
-    pieces = lines[...].reshape((RING,) + own_ref.shape)
+        total = total_ref[:, at]
+        for ref in coming:
+            total = total + ref[:, at].astype(F32)
+        lines[:, c, :] = total
+    pieces = lines[...].reshape((len(FAR),) + own_ref.shape)
     own_ref[...] = pieces[0]
-    next_ref[...] = pieces[1].astype(BF)
-    opposite_ref[...] = pieces[2].astype(BF)
-    previous_ref[...] = pieces[3].astype(BF)
+    first_ref[...] = pieces[1].astype(BF)
+    second_ref[...] = pieces[2].astype(BF)
+    third_ref[...] = pieces[3].astype(BF)
 
 
 def finish_kernel(scale, own_ref, *refs):
@@ -207,7 +212,7 @@
     assert capacity == FIRST + 1
     block_rows = capacity * width // LANES
     chips = replicas // 2
-    assert chips == 2 ** len(HOPS) * RING and hidden_units % replicas == 0
+    assert chips == 2 * len(NEAR) * len(FAR) and hidden_units % replicas == 0
     shape = jax.ShapeDtypeStruct
     vmem = pl.BlockSpec(memory_space=pltpu.VMEM)
     smem = pl.BlockSpec(memory_space=pltpu.SMEM)
@@ -281,27 +286,28 @@
         return lax.ppermute(going, "dp", hops)
 
     share = hidden_units // replicas
-    total, coming, count = keep, other, half
-    for hop in HOPS:
-        count //= 2
-        going = (total[count:] + coming[count:].astype(F32)).astype(BF)
-        total = lax.optimization_barrier(total[:count] + coming[:count].astype(F32))
-        coming = pass_on(going, hop)
-        if hop == HOPS[0]:
-            coming, going_back = lax.optimization_barrier((coming, going_back))
+    count = half // 2
+    total = lax.optimization_barrier(keep[:count] + other[:count].astype(F32))
+    coming = pass_on((keep[count:] + other[count:].astype(F32)).astype(BF), 1)
+    coming, _ = lax.optimization_barrier((coming, going_back))
+    count = count // len(NEAR)
+    total, *going = [
+        total[at : at + count] + coming[at : at + count].astype(F32)
+        for at in range(0, half // 2, count)
+    ]
+    parts = [pass_on(x.astype(BF), move) for x, move in zip(going, NEAR[1:])]
     returned = lax.all_to_all(going_back, "expert", split_axis=0, concat_axis=0, tiled=True)
     piece = (share * width // LANES, LANES)
-    own, ahead, opposite, previous = pl.pallas_call(
+    own, *going = pl.pallas_call(
         fold_kernel,
         out_shape=(shape(piece, F32),) + (shape(piece, BF),) * 3,
-        in_specs=[vmem] * 2,
-        out_specs=(vmem,) * 4,
+        in_specs=[vmem] * len(NEAR),
+        out_specs=(vmem,) * len(FAR),
         scratch_shapes=[pltpu.VMEM((count, width // LANES, LANES), F32)],
         compiler_params=PARAMS,
         name="fold",
-    )(total, coming)
-    stride = -2 * HOPS[-1]
-    parts = [pass_on(opposite, 2 * stride), pass_on(ahead, stride), pass_on(previous, -stride)]
+    )(total, *parts)
+    parts = [pass_on(x, move) for x, move in zip(going, FAR[1:])]
     grad_tokens = pl.pallas_call(
         functools.partial(combine_kernel, experts),
         out_shape=shape((tokens, width), BF),
@@ -315,7 +321,7 @@
     grad_down = pl.pallas_call(
         functools.partial(finish_kernel, 1.0 / replicas),
         out_shape=shape((1, share, width), F32),
-        in_specs=[vmem] * RING,
+        in_specs=[vmem] * len(FAR),
         out_specs=vmem,
         scratch_shapes=[pltpu.VMEM((share, width // LANES, LANES), F32)],
         compiler_params=PARAMS,

time: 131 us -> 130 us (level)
  the two profiles are of different devices: /device:TPU:33 before, /device:TPU:8 now
where the time goes in v6:
time: 130 us
  starting transfers between devices  74 us (57%)
  waiting for transfers between devices  43.7 us (34%)
  Pallas kernels  10 us (8%)
    ppermute x7, starting transfers between devices, pass_on(): return lax.ppermute(going, 'dp', hops)  50.4 us
    ppermute x7, waiting for transfers between devices, pass_on(): return lax.ppermute(going, 'dp', hops)  22.6 us
    all_to_all x1, waiting for transfers between devices, per_device(): lax.all_to_all(outgoing, 'expert', split_axis=0, concat_axis=0, tiled=True)  19.4 us
    all_to_all x1, starting transfers between devices, per_device(): lax.all_to_all(outgoing, 'expert', split_axis=0, concat_axis=0, tiled=True)  16.8 us
    all_to_all x1, starting transfers between devices, per_device(): lax.all_to_all(going_back, 'expert', split_axis=0, concat_axis=0, tiled=T...  4.9 us
    pallas_call x1, Pallas kernels, per_device(): pl.pallas_call(functools.partial(dispatch_kernel, experts), out_shape=(pl...  2.72 us
  transfers between devices with their start and end apart: 10, of which 5 were waited for; matrix products, arithmetic and copies ran while one was open for 0% of the time, Pallas kernels for 4%

profile of v6, /device:TPU:8, one launch (start us, length us, event | category | flops | bytes accessed | tf_op | source)
XLA Modules:
  0.0 129.6 jit_solution(14617087116110648563)
XLA Ops:
  0.6 2.7 %dispatch_rows.1 = (bf16[16,504,128]{2,1,0:T(8,128)(2,1)}, bf16[144,32]{1,0:T(8,128)(2,1)S(1)}) custom-call(bf16[32,7168]{1,0:T(8,128)(2,1)} %dy_hbm.1, s32[4,32]{1,0:T(4,128)} %bitcast.4, f32[4,32]{1,0:T(4,128)} %bitcast.5), custom_call_target="tpu_custom_call" | custom-call | tf_op jit(solution)/shard_map/dispatch_rows/pallas_call | solution.py:222
  3.4 0.0 copy-start.3
  3.4 16.8 %all-to-all-start = ((bf16[16,504,128]{2,1,0:T(8,128)(2,1)}), bf16[16,504,128]{2,1,0:T(8,128)(2,1)S(1)}, u32[]{:S(2)}, u32[]{:S(2)}) async-start(bf16[16,504,128]{2,1,0:T(8,128)(2,1)} %get-tuple-element.17), calls=%async_computation | async-start | bytes 4128768 | tf_op jit(solution)/shard_map/all_to_all | solution.py:238
  20.1 0.1 pad_add_fusion.at_ref
  20.2 19.4 %all-to-all-done.got_ref = bf16[16,504,128]{2,1,0:T(8,128)(2,1)S(1)} async-done(((bf16[16,504,128]{2,1,0:T(8,128)(2,1)}), bf16[16,504,128]{2,1,0:T(8,128)(2,1)S(1)}, u32[]{:S(2)}, u32[]{:S(2)}) %all-to-all-start) | async-done | bytes 2064416 | tf_op jit(solution)/shard_map/all_to_all | solution.py:238
  39.6 0.0 copy-done.3
  39.6 0.0 copy-start
  39.6 2.0 %down_partial.1 = (bf16[144,7168]{1,0:T(8,128)(2,1)S(1)}, f32[64,7168]{1,0:T(8,128)S(1)}, bf16[64,7168]{1,0:T(8,128)(2,1)S(1)}, f32[144,256]{1,0:T(8,128)S(1)}) custom-call(s32[2]{0:T(128)S(1)} %pad_add_fusion.at_ref, bf16[16,504,128]{2,1,0:T(8,128)(2,1)S(1)} %all-to-all-done.got_ref, bf16[144,256]{1,0:T(8,128)(2,1)S(1)} %copy-done.3), custom_call_target="tpu_custom_call" | custom-call | tf_op jit(solution)/shard_map/down_partial/pallas_call | solution.py:242
  41.6 1.9 %collective-permute-start = (bf16[64,7168]{1,0:T(8,128)(2,1)S(1)}, bf16[64,7168]{1,0:T(8,128)(2,1)S(1)}, u32[]{:S(2)}, u32[]{:S(2)}) collective-permute-start(bf16[64,7168]{1,0:T(8,128)(2,1)S(1)} %get-tuple-element.19), channel_id=1, source_target_pairs={{0,16},{16,0},{32,48},{48,32},{64,80},{80,64},{96,112},{112,96},{1... | collective-permute-start | bytes 2752520 | tf_op jit(solution)/shard_map/ppermute | solution.py:256
  43.5 0.0 copy-done
  43.5 0.7 grad_hidden.1.hidden_ref
  44.2 1.7 %collective-permute-done = bf16[64,7168]{1,0:T(8,128)(2,1)S(1)} collective-permute-done((bf16[64,7168]{1,0:T(8,128)(2,1)S(1)}, bf16[64,7168]{1,0:T(8,128)(2,1)S(1)}, u32[]{:S(2)}, u32[]{:S(2)}) %collective-permute-start) | collective-permute-done | bytes 917536 | tf_op jit(solution)/shard_map/ppermute | solution.py:256
  45.9 0.0 copy-start.1
  45.9 0.0 copy-start.2
  45.9 1.0 add_convert_fusion
  46.9 5.2 %collective-permute-start.1 = (bf16[32,7168]{1,0:T(8,128)(2,1)}, bf16[32,7168]{1,0:T(8,128)(2,1)S(1)}, u32[]{:S(2)}, u32[]{:S(2)}) collective-permute-start(bf16[32,7168]{1,0:T(8,128)(2,1)} %get-tuple-element.32), channel_id=1, source_target_pairs={{0,32},{16,1008},{32,64},{48,16},{64,96},{80,48},{96,128},{112,80}... | collective-permute-start | bytes 1376264 | tf_op jit(solution)/shard_map/ppermute | solution.py:286
  52.1 0.0 copy-done.1
  52.1 0.0 copy-done.2
  52.1 2.3 %grad_rows.1 = bf16[16,504,128]{2,1,0:T(8,128)(2,1)} custom-call(bf16[144,256]{1,0:T(8,128)(2,1)S(1)} %grad_hidden.1.hidden_ref, bf16[1,7168,128]{2,1,0:T(8,128)(2,1)S(1)} %copy-done.1, bf16[1,7168,128]{2,1,0:T(8,128)(2,1)S(1)} %copy-done.2), custom_call_target="tpu_custom_call" | custom-call | tf_op jit(solution)/shard_map/grad_rows/pallas_call | solution.py:267
  54.5 4.9 %all-to-all-start.1 = ((bf16[16,504,128]{2,1,0:T(8,128)(2,1)}), bf16[16,504,128]{2,1,0:T(8,128)(2,1)S(1)}, u32[]{:S(2)}, u32[]{:S(2)}) async-start(bf16[16,504,128]{2,1,0:T(8,128)(2,1)} %grad_rows.1), calls=%async_computation.1 | async-start | bytes 4128768 | tf_op jit(solution)/shard_map/all_to_all | solution.py:299
  59.4 14.3 %collective-permute-done.1 = bf16[32,7168]{1,0:T(8,128)(2,1)S(1)} collective-permute-done((bf16[32,7168]{1,0:T(8,128)(2,1)}, bf16[32,7168]{1,0:T(8,128)(2,1)S(1)}, u32[]{:S(2)}, u32[]{:S(2)}) %collective-permute-start.1) | collective-permute-done | bytes 458784 | tf_op jit(solution)/shard_map/ppermute | solution.py:286
  73.6 0.1 fusion
  73.7 1.9 %collective-permute-start.4 = (bf16[8,7168]{1,0:T(8,128)(2,1)S(1)}, bf16[8,7168]{1,0:T(8,128)(2,1)S(1)}, u32[]{:S(2)}, u32[]{:S(2)}) collective-permute-start(bf16[8,7168]{1,0:T(8,128)(2,1)S(1)} %get-tuple-element.34), channel_id=1, source_target_pairs={{0,64},{16,976},{32,96},{48,1008},{64,128},{80,16},{96,160},{112,4... | collective-permute-start | bytes 344072 | tf_op jit(solution)/shard_map/ppermute | solution.py:286
  75.7 6.7 %collective-permute-start.3 = (bf16[8,7168]{1,0:T(8,128)(2,1)S(1)}, bf16[8,7168]{1,0:T(8,128)(2,1)S(1)}, u32[]{:S(2)}, u32[]{:S(2)}) collective-permute-start(bf16[8,7168]{1,0:T(8,128)(2,1)S(1)} %get-tuple-element.35), channel_id=1, source_target_pairs={{0,896},{16,144},{32,928},{48,176},{64,960},{80,208},{96,992},{112... | collective-permute-start | bytes 344072 | tf_op jit(solution)/shard_map/ppermute | solution.py:286
  82.4 5.8 %collective-permute-start.2 = (bf16[8,7168]{1,0:T(8,128)(2,1)S(1)}, bf16[8,7168]{1,0:T(8,128)(2,1)S(1)}, u32[]{:S(2)}, u32[]{:S(2)}) collective-permute-start(bf16[8,7168]{1,0:T(8,128)(2,1)S(1)} %get-tuple-element.36), channel_id=1, source_target_pairs={{0,960},{16,80},{32,992},{48,112},{64,0},{80,144},{96,32},{112,176... | collective-permute-start | bytes 344072 | tf_op jit(solution)/shard_map/ppermute | solution.py:286
  88.1 0.0 collective-permute-done.4.refs_2_
  88.2 0.0 collective-permute-done.3.refs_1_
  88.2 3.2 %collective-permute-done.2.refs_0_ = bf16[8,7168]{1,0:T(8,128)(2,1)S(1)} collective-permute-done((bf16[8,7168]{1,0:T(8,128)(2,1)S(1)}, bf16[8,7168]{1,0:T(8,128)(2,1)S(1)}, u32[]{:S(2)}, u32[]{:S(2)}) %collective-permute-start.2) | collective-permute-done | bytes 114720 | tf_op jit(solution)/shard_map/ppermute | solution.py:286
  91.4 0.2 fold.1
  91.5 5.0 %collective-permute-start.5 = (bf16[112,128]{1,0:T(8,128)(2,1)S(1)}, bf16[112,128]{1,0:T(8,128)(2,1)S(1)}, u32[]{:S(2)}, u32[]{:S(2)}) collective-permute-start(bf16[112,128]{1,0:T(8,128)(2,1)S(1)} %get-tuple-element.25), channel_id=1, source_target_pairs={{0,256},{16,784},{32,288},{48,816},{64,320},{80,848},{96,352},{112... | collective-permute-start | bytes 86024 | tf_op jit(solution)/shard_map/ppermute | solution.py:286
  96.6 17.4 %collective-permute-start.6 = (bf16[112,128]{1,0:T(8,128)(2,1)S(1)}, bf16[112,128]{1,0:T(8,128)(2,1)S(1)}, u32[]{:S(2)}, u32[]{:S(2)}) collective-permute-start(bf16[112,128]{1,0:T(8,128)(2,1)S(1)} %get-tuple-element.30), channel_id=1, source_target_pairs={{0,512},{16,528},{32,544},{48,560},{64,576},{80,592},{96,608},{112... | collective-permute-start | bytes 86024 | tf_op jit(solution)/shard_map/ppermute | solution.py:286
  114.0 8.4 %collective-permute-start.7 = (bf16[112,128]{1,0:T(8,128)(2,1)S(1)}, bf16[112,128]{1,0:T(8,128)(2,1)S(1)}, u32[]{:S(2)}, u32[]{:S(2)}) collective-permute-start(bf16[112,128]{1,0:T(8,128)(2,1)S(1)} %get-tuple-element.31), channel_id=1, source_target_pairs={{0,768},{16,272},{32,800},{48,304},{64,832},{80,336},{96,864},{112... | collective-permute-start | bytes 86024 | tf_op jit(solution)/shard_map/ppermute | solution.py:286
  122.4 0.0 all-to-all-done.1.got_ref
  122.4 1.4 %combine_rows.1 = bf16[32,7168]{1,0:T(8,128)(2,1)} custom-call(bf16[144,32]{1,0:T(8,128)(2,1)S(1)} %get-tuple-element.26.pick_ref, bf16[16,504,128]{2,1,0:T(8,128)(2,1)S(1)} %all-to-all-done.1.got_ref), custom_call_target="tpu_custom_call" | custom-call | tf_op jit(solution)/shard_map/combine_rows/pallas_call | solution.py:311
  123.8 0.0 collective-permute-done.5.refs_0_
  123.8 0.0 collective-permute-done.6.refs_1_
  123.8 5.2 %collective-permute-done.7.refs_2_ = bf16[112,128]{1,0:T(8,128)(2,1)S(1)} collective-permute-done((bf16[112,128]{1,0:T(8,128)(2,1)S(1)}, bf16[112,128]{1,0:T(8,128)(2,1)S(1)}, u32[]{:S(2)}, u32[]{:S(2)}) %collective-permute-start.7) | collective-permute-done | bytes 28704 | tf_op jit(solution)/shard_map/ppermute | solution.py:286
  129.0 0.7 finish.1
Async XLA Ops:
  3.4 36.2 %copy-start.3 = (bf16[144,256]{1,0:T(8,128)(2,1)S(1)}, bf16[144,256]{1,0:T(8,128)(2,1)}, u32[]{:S(2)}) copy-start(bf16[144,256]{1,0:T(8,128)(2,1)} %pre_ref.1) | copy-start | bytes 221188
  3.4 36.2 %all-to-all-start = ((bf16[16,504,128]{2,1,0:T(8,128)(2,1)}), bf16[16,504,128]{2,1,0:T(8,128)(2,1)S(1)}, u32[]{:S(2)}, u32[]{:S(2)}) async-start(bf16[16,504,128]{2,1,0:T(8,128)(2,1)} %get-tuple-element.17), calls=%async_computation | async-start | bytes 4128768 | tf_op jit(solution)/shard_map/all_to_all | solution.py:238
  39.6 3.9 %copy-start = (bf16[1,128,7168]{2,1,0:T(8,128)(2,1)S(1)}, bf16[1,128,7168]{2,1,0:T(8,128)(2,1)}, u32[]{:S(2)}) copy-start(bf16[1,128,7168]{2,1,0:T(8,128)(2,1)} %down_ref.1) | copy-start | bytes 5505028
  41.6 4.4 %collective-permute-start = (bf16[64,7168]{1,0:T(8,128)(2,1)S(1)}, bf16[64,7168]{1,0:T(8,128)(2,1)S(1)}, u32[]{:S(2)}, u32[]{:S(2)}) collective-permute-start(bf16[64,7168]{1,0:T(8,128)(2,1)S(1)} %get-tuple-element.19), channel_id=1, source_target_pairs={{0,16},{16,0},{32,48},{48,32},{64,80},{80,64},{96,112},{112,96},{1... | collective-permute-start | bytes 2752520 | tf_op jit(solution)/shard_map/ppermute | solution.py:256
  45.9 6.2 %copy-start.1 = (bf16[1,7168,128]{2,1,0:T(8,128)(2,1)S(1)}, bf16[1,7168,128]{2,1,0:T(8,128)(2,1)}, u32[]{:S(2)}) copy-start(bf16[1,7168,128]{2,1,0:T(8,128)(2,1)} %gate_ref.1) | copy-start | bytes 5505028
  45.9 6.2 %copy-start.2 = (bf16[1,7168,128]{2,1,0:T(8,128)(2,1)S(1)}, bf16[1,7168,128]{2,1,0:T(8,128)(2,1)}, u32[]{:S(2)}) copy-start(bf16[1,7168,128]{2,1,0:T(8,128)(2,1)} %up_ref.1) | copy-start | bytes 5505028
  46.9 26.7 %collective-permute-start.1 = (bf16[32,7168]{1,0:T(8,128)(2,1)}, bf16[32,7168]{1,0:T(8,128)(2,1)S(1)}, u32[]{:S(2)}, u32[]{:S(2)}) collective-permute-start(bf16[32,7168]{1,0:T(8,128)(2,1)} %get-tuple-element.32), channel_id=1, source_target_pairs={{0,32},{16,1008},{32,64},{48,16},{64,96},{80,48},{96,128},{112,80}... | collective-permute-start | bytes 1376264 | tf_op jit(solution)/shard_map/ppermute | solution.py:286
  54.5 67.9 %all-to-all-start.1 = ((bf16[16,504,128]{2,1,0:T(8,128)(2,1)}), bf16[16,504,128]{2,1,0:T(8,128)(2,1)S(1)}, u32[]{:S(2)}, u32[]{:S(2)}) async-start(bf16[16,504,128]{2,1,0:T(8,128)(2,1)} %grad_rows.1), calls=%async_computation.1 | async-start | bytes 4128768 | tf_op jit(solution)/shard_map/all_to_all | solution.py:299
  73.7 14.4 %collective-permute-start.4 = (bf16[8,7168]{1,0:T(8,128)(2,1)S(1)}, bf16[8,7168]{1,0:T(8,128)(2,1)S(1)}, u32[]{:S(2)}, u32[]{:S(2)}) collective-permute-start(bf16[8,7168]{1,0:T(8,128)(2,1)S(1)} %get-tuple-element.34), channel_id=1, source_target_pairs={{0,64},{16,976},{32,96},{48,1008},{64,128},{80,16},{96,160},{112,4... | collective-permute-start | bytes 344072 | tf_op jit(solution)/shard_map/ppermute | solution.py:286
  75.7 12.5 %collective-permute-start.3 = (bf16[8,7168]{1,0:T(8,128)(2,1)S(1)}, bf16[8,7168]{1,0:T(8,128)(2,1)S(1)}, u32[]{:S(2)}, u32[]{:S(2)}) collective-permute-start(bf16[8,7168]{1,0:T(8,128)(2,1)S(1)} %get-tuple-element.35), channel_id=1, source_target_pairs={{0,896},{16,144},{32,928},{48,176},{64,960},{80,208},{96,992},{112... | collective-permute-start | bytes 344072 | tf_op jit(solution)/shard_map/ppermute | solution.py:286
  82.4 9.0 %collective-permute-start.2 = (bf16[8,7168]{1,0:T(8,128)(2,1)S(1)}, bf16[8,7168]{1,0:T(8,128)(2,1)S(1)}, u32[]{:S(2)}, u32[]{:S(2)}) collective-permute-start(bf16[8,7168]{1,0:T(8,128)(2,1)S(1)} %get-tuple-element.36), channel_id=1, source_target_pairs={{0,960},{16,80},{32,992},{48,112},{64,0},{80,144},{96,32},{112,176... | collective-permute-start | bytes 344072 | tf_op jit(solution)/shard_map/ppermute | solution.py:286
  91.5 32.2 %collective-permute-start.5 = (bf16[112,128]{1,0:T(8,128)(2,1)S(1)}, bf16[112,128]{1,0:T(8,128)(2,1)S(1)}, u32[]{:S(2)}, u32[]{:S(2)}) collective-permute-start(bf16[112,128]{1,0:T(8,128)(2,1)S(1)} %get-tuple-element.25), channel_id=1, source_target_pairs={{0,256},{16,784},{32,288},{48,816},{64,320},{80,848},{96,352},{112... | collective-permute-start | bytes 86024 | tf_op jit(solution)/shard_map/ppermute | solution.py:286
  96.6 27.2 %collective-permute-start.6 = (bf16[112,128]{1,0:T(8,128)(2,1)S(1)}, bf16[112,128]{1,0:T(8,128)(2,1)S(1)}, u32[]{:S(2)}, u32[]{:S(2)}) collective-permute-start(bf16[112,128]{1,0:T(8,128)(2,1)S(1)} %get-tuple-element.30), channel_id=1, source_target_pairs={{0,512},{16,528},{32,544},{48,560},{64,576},{80,592},{96,608},{112... | collective-permute-start | bytes 86024 | tf_op jit(solution)/shard_map/ppermute | solution.py:286
  114.0 15.0 %collective-permute-start.7 = (bf16[112,128]{1,0:T(8,128)(2,1)S(1)}, bf16[112,128]{1,0:T(8,128)(2,1)S(1)}, u32[]{:S(2)}, u32[]{:S(2)}) collective-permute-start(bf16[112,128]{1,0:T(8,128)(2,1)S(1)} %get-tuple-element.31), channel_id=1, source_target_pairs={{0,768},{16,272},{32,800},{48,304},{64,832},{80,336},{96,864},{112... | collective-permute-start | bytes 86024 | tf_op jit(solution)/shard_map/ppermute | solution.py:286

commit v7 on v6

--- a/solution.py
+++ b/solution.py
@@ -12,8 +12,8 @@
 LANES = 128
 FIRST = 8
 PARTS = 4
-NEAR = (0, -2, -4, 2)
-FAR = (0, 8, 16, -8)
+NEAR = (0, -2, 2, -4)
+FAR = (0, 16, 8, -8)
 PARAMS = pltpu.CompilerParams(vmem_limit_bytes=16 * 1024 * 1024)
 
 
@@ -44,7 +44,7 @@
 
 
 def dispatch_kernel(
-    experts, dy_hbm, routing_hbm, weight_hbm, out_hbm, pick_ref, dy_ref, routing_ref, weight_ref, out_ref, tail, sems
+    experts, dy_hbm, routing_hbm, weight_hbm, out_ref, pick_ref, dy_ref, routing_ref, weight_ref, tail, sems
 ):
     loads = [
         pltpu.make_async_copy(source, target, sems.at[i])
@@ -77,10 +77,11 @@
     row_weight = jnp.sum(pick * scale, axis=1, keepdims=True)
     loads[2].wait()
 
-    def columns(at):
-        return dot(chosen, dy_ref[:, at], ((1,), (0,))) * row_weight
-
-    write_all(columns, width, experts, out_ref, out_hbm, tail, [sems.at[3 + i] for i in range(PARTS)])
+    for pair in range(width // (2 * LANES)):
+        at = slice(pair * 2 * LANES, (pair + 1) * 2 * LANES)
+        part = dot(chosen, dy_ref[:, at], ((1,), (0,))) * row_weight
+        write_block(out_ref, tail, pair, part[:, :LANES], part[:, LANES:], experts)
+    out_ref[:, experts_rows(width) :, :] = tail[...].astype(BF)
 
 
 def write_all(columns, width, experts, out_ref, out_hbm, tail, sems):
@@ -221,23 +222,25 @@
 
     outgoing, pick = pl.pallas_call(
         functools.partial(dispatch_kernel, experts),
-        out_shape=(pltpu.HBM(block.shape, BF), shape((rows, tokens), BF)),
+        out_shape=(block, shape((rows, tokens), BF)),
         in_specs=[pl.BlockSpec(memory_space=pl.ANY)] * 3,
-        out_specs=(pl.BlockSpec(memory_space=pltpu.HBM), vmem),
+        out_specs=(vmem, vmem),
         scratch_shapes=[
             pltpu.VMEM((tokens, width), BF),
             pltpu.VMEM(routing.T.shape, jnp.int32),
             pltpu.VMEM(route_weight.T.shape, F32),
-            pltpu.VMEM((experts, block_rows, LANES), BF),
             tail,
-            pltpu.SemaphoreType.DMA((3 + PARTS,)),
+            pltpu.SemaphoreType.DMA((3,)),
         ],
         compiler_params=PARAMS,
         name="dispatch_rows",
     )(*(pltpu.with_memory_space_constraint(x, pltpu.HBM) for x in (dy_tokens, routing.T, route_weight.T)))
+    own = lax.axis_index("dp")
+    outgoing, place, pre_act = lax.optimization_barrier(
+        (outgoing, jnp.stack([own // 2, own % 2]), pre_act)
+    )
     got = lax.all_to_all(outgoing, "expert", split_axis=0, concat_axis=0, tiled=True)
 
-    own = lax.axis_index("dp")
     half = hidden_units // 2
     arrived, keep, send, factor = pl.pallas_call(
         functools.partial(partial_kernel, experts, chips),
@@ -252,7 +255,7 @@
         scratch_shapes=[tail],
         compiler_params=PARAMS,
         name="down_partial",
-    )(jnp.stack([own // 2, own % 2]), got, pre_act)
+    )(place, got, pre_act)
     other = lax.ppermute(send, "dp", [(i, i ^ 1) for i in range(replicas)])
 
     grad_hidden = pl.pallas_call(
@@ -287,8 +290,9 @@
 
     share = hidden_units // replicas
     count = half // 2
+    coming = pass_on((keep[count:] + other[count:].astype(F32)).astype(BF), 1)
+    keep, other = lax.optimization_barrier((keep, other))
     total = lax.optimization_barrier(keep[:count] + other[:count].astype(F32))
-    coming = pass_on((keep[count:] + other[count:].astype(F32)).astype(BF), 1)
     coming, _ = lax.optimization_barrier((coming, going_back))
     count = count // len(NEAR)
     total, *going = [

time: 130 us -> 126 us (0.969)
  the two profiles are of different devices: /device:TPU:8 before, /device:TPU:10 now
where the time goes in v7:
time: 126 us; the launch traced here: 125 us
  starting transfers between devices  58.4 us (46%)
  blocking collectives  32.1 us (25%)
  waiting for transfers between devices  22.1 us (18%)
  Pallas kernels  9.11 us (7%)
  other arithmetic  2.59 us (2%)
    ppermute x7, starting transfers between devices, pass_on(): return lax.ppermute(going, 'dp', hops)  49.4 us
    all_to_all x1, blocking collectives, per_device(): lax.all_to_all(outgoing, 'expert', split_axis=0, concat_axis=0, tiled=True)  32.1 us
    ppermute x7, waiting for transfers between devices, pass_on(): return lax.ppermute(going, 'dp', hops)  20.4 us
    all_to_all x1, starting transfers between devices, per_device(): lax.all_to_all(going_back, 'expert', split_axis=0, concat_axis=0, tiled=T...  7.12 us
  transfers between devices with their start and end apart: 9, of which 7 were waited for; matrix products, arithmetic and copies ran while one was open for 2% of the time, Pallas kernels for 4%

profile of v7, /device:TPU:10, one launch (start us, length us, event | category | flops | bytes accessed | tf_op | source)
XLA Modules:
  0.0 125.2 jit_solution(17348228880903898603)
XLA Ops:
  0.6 0.1 pad_add_fusion.at_ref
  0.7 1.8 %dispatch_rows.1 = (bf16[16,504,128]{2,1,0:T(8,128)(2,1)S(1)}, bf16[144,32]{1,0:T(8,128)(2,1)S(1)}) custom-call(bf16[32,7168]{1,0:T(8,128)(2,1)} %dy_hbm.1, s32[4,32]{1,0:T(4,128)} %bitcast.4, f32[4,32]{1,0:T(4,128)} %bitcast.5), custom_call_target="tpu_custom_call" | custom-call | tf_op jit(solution)/shard_map/dispatch_rows/pallas_call | solution.py:223
  2.5 0.0 copy-start.4
  2.5 32.1 %all_to_all.10.got_ref = bf16[16,504,128]{2,1,0:T(8,128)(2,1)S(1)} all-to-all(bf16[16,504,128]{2,1,0:T(8,128)(2,1)S(1)} %get-tuple-element.24), channel_id=1, replica_groups=mesh['dp'=64,'expert'=16] {'expert'}, dimensions={0} | all-to-all | bytes 4128768 | tf_op jit(solution)/shard_map/all_to_all | solution.py:242
  34.7 0.0 copy-done.4
  34.7 0.0 copy-start.1
  34.7 2.0 %down_partial.1 = (bf16[144,7168]{1,0:T(8,128)(2,1)S(1)}, f32[64,7168]{1,0:T(8,128)S(1)}, bf16[64,7168]{1,0:T(8,128)(2,1)S(1)}, f32[144,256]{1,0:T(8,128)S(1)}) custom-call(s32[2]{0:T(128)S(1)} %pad_add_fusion.at_ref, bf16[16,504,128]{2,1,0:T(8,128)(2,1)S(1)} %all_to_all.10.got_ref, bf16[144,256]{1,0:T(8,128)(2,1)S(1)} %copy-done.4), custom_call_target="tpu_custom_call" | custom-call | tf_op jit(solution)/shard_map/down_partial/pallas_call | solution.py:245
  36.6 0.0 copy-start
  36.7 1.9 %collective-permute-start = (bf16[64,7168]{1,0:T(8,128)(2,1)S(1)}, bf16[64,7168]{1,0:T(8,128)(2,1)S(1)}, u32[]{:S(2)}, u32[]{:S(2)}) collective-permute-start(bf16[64,7168]{1,0:T(8,128)(2,1)S(1)} %get-tuple-element.27), channel_id=1, source_target_pairs={{0,16},{16,0},{32,48},{48,32},{64,80},{80,64},{96,112},{112,96},{1... | collective-permute-start | bytes 2752520 | tf_op jit(solution)/shard_map/ppermute | solution.py:259
  38.6 0.0 copy-done.1
  38.6 0.0 copy-start.3
  38.6 0.7 grad_hidden.1.hidden_ref
  39.3 0.0 copy-start.2
  39.3 1.7 %collective-permute-done = bf16[64,7168]{1,0:T(8,128)(2,1)S(1)} collective-permute-done((bf16[64,7168]{1,0:T(8,128)(2,1)S(1)}, bf16[64,7168]{1,0:T(8,128)(2,1)S(1)}, u32[]{:S(2)}, u32[]{:S(2)}) %collective-permute-start) | collective-permute-done | bytes 917536 | tf_op jit(solution)/shard_map/ppermute | solution.py:259
  41.0 0.0 copy-done
  41.0 0.1 add_convert_fusion
  41.1 3.6 %collective-permute-start.1 = (bf16[32,7168]{1,0:T(8,128)(2,1)S(1)}, bf16[32,7168]{1,0:T(8,128)(2,1)}, u32[]{:S(2)}, u32[]{:S(2)}) collective-permute-start(bf16[32,7168]{1,0:T(8,128)(2,1)S(1)} %add_convert_fusion), channel_id=1, source_target_pairs={{0,32},{16,1008},{32,64},{48,16},{64,96},{80,48},{96,128},{112,80}... | collective-permute-start | bytes 1376264 | tf_op jit(solution)/shard_map/ppermute | solution.py:289
  44.7 0.0 copy-done.3
  44.7 0.0 copy-done.2
  44.7 2.4 %grad_rows.1 = bf16[16,504,128]{2,1,0:T(8,128)(2,1)} custom-call(bf16[144,256]{1,0:T(8,128)(2,1)S(1)} %grad_hidden.1.hidden_ref, bf16[1,7168,128]{2,1,0:T(8,128)(2,1)S(1)} %copy-done.2, bf16[1,7168,128]{2,1,0:T(8,128)(2,1)S(1)} %copy-done.3), custom_call_target="tpu_custom_call" | custom-call | tf_op jit(solution)/shard_map/grad_rows/pallas_call | solution.py:270
  47.1 7.1 %all-to-all-start.1 = ((bf16[16,504,128]{2,1,0:T(8,128)(2,1)}), bf16[16,504,128]{2,1,0:T(8,128)(2,1)S(1)}, u32[]{:S(2)}, u32[]{:S(2)}) async-start(bf16[16,504,128]{2,1,0:T(8,128)(2,1)} %grad_rows.1), calls=%async_computation.1 | async-start | bytes 4128768 | tf_op jit(solution)/shard_map/all_to_all | solution.py:303
  54.2 1.3 %convert_add_fusion = f32[32,7168]{1,0:T(8,128)S(1)} fusion(f32[64,7168]{1,0:T(8,128)} %copy-done, bf16[64,7168]{1,0:T(8,128)(2,1)S(1)} %collective-permute-done), kind=kLoop, calls=%fused_computation.1 | loop fusion | flops 458752 | bytes 2293760 | tf_op jit(solution)/shard_map/add | solution.py:295
  55.5 10.6 %collective-permute-done.1 = bf16[32,7168]{1,0:T(8,128)(2,1)} collective-permute-done((bf16[32,7168]{1,0:T(8,128)(2,1)S(1)}, bf16[32,7168]{1,0:T(8,128)(2,1)}, u32[]{:S(2)}, u32[]{:S(2)}) %collective-permute-start.1) | collective-permute-done | bytes 458784 | tf_op jit(solution)/shard_map/ppermute | solution.py:289
  66.1 1.1 fusion
  67.2 8.5 %collective-permute-start.4 = (bf16[8,7168]{1,0:T(8,128)(2,1)S(1)}, bf16[8,7168]{1,0:T(8,128)(2,1)S(1)}, u32[]{:S(2)}, u32[]{:S(2)}) collective-permute-start(bf16[8,7168]{1,0:T(8,128)(2,1)S(1)} %get-tuple-element.42), channel_id=1, source_target_pairs={{0,896},{16,144},{32,928},{48,176},{64,960},{80,208},{96,992},{112... | collective-permute-start | bytes 344072 | tf_op jit(solution)/shard_map/ppermute | solution.py:289
  75.8 3.4 %collective-permute-start.3 = (bf16[8,7168]{1,0:T(8,128)(2,1)S(1)}, bf16[8,7168]{1,0:T(8,128)(2,1)S(1)}, u32[]{:S(2)}, u32[]{:S(2)}) collective-permute-start(bf16[8,7168]{1,0:T(8,128)(2,1)S(1)} %get-tuple-element.43), channel_id=1, source_target_pairs={{0,64},{16,976},{32,96},{48,1008},{64,128},{80,16},{96,160},{112,4... | collective-permute-start | bytes 344072 | tf_op jit(solution)/shard_map/ppermute | solution.py:289
  79.1 4.6 %collective-permute-start.2 = (bf16[8,7168]{1,0:T(8,128)(2,1)S(1)}, bf16[8,7168]{1,0:T(8,128)(2,1)S(1)}, u32[]{:S(2)}, u32[]{:S(2)}) collective-permute-start(bf16[8,7168]{1,0:T(8,128)(2,1)S(1)} %get-tuple-element.44), channel_id=1, source_target_pairs={{0,960},{16,80},{32,992},{48,112},{64,0},{80,144},{96,32},{112,176... | collective-permute-start | bytes 344072 | tf_op jit(solution)/shard_map/ppermute | solution.py:289
  83.7 0.1 collective-permute-done.4.refs_2_
  83.9 3.1 %collective-permute-done.3.refs_1_ = bf16[8,7168]{1,0:T(8,128)(2,1)S(1)} collective-permute-done((bf16[8,7168]{1,0:T(8,128)(2,1)S(1)}, bf16[8,7168]{1,0:T(8,128)(2,1)S(1)}, u32[]{:S(2)}, u32[]{:S(2)}) %collective-permute-start.3) | collective-permute-done | bytes 114720 | tf_op jit(solution)/shard_map/ppermute | solution.py:289
  86.9 0.5 collective-permute-done.2.refs_0_
  87.5 0.2 fold.1
  87.7 14.8 %collective-permute-start.5 = (bf16[112,128]{1,0:T(8,128)(2,1)S(1)}, bf16[112,128]{1,0:T(8,128)(2,1)S(1)}, u32[]{:S(2)}, u32[]{:S(2)}) collective-permute-start(bf16[112,128]{1,0:T(8,128)(2,1)S(1)} %get-tuple-element.35), channel_id=1, source_target_pairs={{0,512},{16,528},{32,544},{48,560},{64,576},{80,592},{96,608},{112... | collective-permute-start | bytes 86024 | tf_op jit(solution)/shard_map/ppermute | solution.py:289
  102.5 7.3 %collective-permute-start.6 = (bf16[112,128]{1,0:T(8,128)(2,1)S(1)}, bf16[112,128]{1,0:T(8,128)(2,1)S(1)}, u32[]{:S(2)}, u32[]{:S(2)}) collective-permute-start(bf16[112,128]{1,0:T(8,128)(2,1)S(1)} %get-tuple-element.40), channel_id=1, source_target_pairs={{0,256},{16,784},{32,288},{48,816},{64,320},{80,848},{96,352},{112... | collective-permute-start | bytes 86024 | tf_op jit(solution)/shard_map/ppermute | solution.py:289
  109.8 7.3 %collective-permute-start.7 = (bf16[112,128]{1,0:T(8,128)(2,1)S(1)}, bf16[112,128]{1,0:T(8,128)(2,1)S(1)}, u32[]{:S(2)}, u32[]{:S(2)}) collective-permute-start(bf16[112,128]{1,0:T(8,128)(2,1)S(1)} %get-tuple-element.41), channel_id=1, source_target_pairs={{0,768},{16,272},{32,800},{48,304},{64,832},{80,336},{96,864},{112... | collective-permute-start | bytes 86024 | tf_op jit(solution)/shard_map/ppermute | solution.py:289
  117.1 0.0 all-to-all-done.1.got_ref
  117.1 1.4 %combine_rows.1 = bf16[32,7168]{1,0:T(8,128)(2,1)} custom-call(bf16[144,32]{1,0:T(8,128)(2,1)S(1)} %get-tuple-element.36.pick_ref, bf16[16,504,128]{2,1,0:T(8,128)(2,1)S(1)} %all-to-all-done.1.got_ref), custom_call_target="tpu_custom_call" | custom-call | tf_op jit(solution)/shard_map/combine_rows/pallas_call | solution.py:315
  118.5 0.0 collective-permute-done.5.refs_0_
  118.5 0.8 collective-permute-done.6.refs_1_
  119.3 5.2 %collective-permute-done.7.refs_2_ = bf16[112,128]{1,0:T(8,128)(2,1)S(1)} collective-permute-done((bf16[112,128]{1,0:T(8,128)(2,1)S(1)}, bf16[112,128]{1,0:T(8,128)(2,1)S(1)}, u32[]{:S(2)}, u32[]{:S(2)}) %collective-permute-start.7) | collective-permute-done | bytes 28704 | tf_op jit(solution)/shard_map/ppermute | solution.py:289
  124.5 0.7 finish.1
Async XLA Ops:
  2.5 32.1 %copy-start.4 = (bf16[144,256]{1,0:T(8,128)(2,1)S(1)}, bf16[144,256]{1,0:T(8,128)(2,1)}, u32[]{:S(2)}) copy-start(bf16[144,256]{1,0:T(8,128)(2,1)} %pre_ref) | copy-start | bytes 221188
  34.7 3.9 %copy-start.1 = (bf16[1,128,7168]{2,1,0:T(8,128)(2,1)S(1)}, bf16[1,128,7168]{2,1,0:T(8,128)(2,1)}, u32[]{:S(2)}) copy-start(bf16[1,128,7168]{2,1,0:T(8,128)(2,1)} %down_ref.1) | copy-start | bytes 5505028
  36.6 4.4 %copy-start = (f32[64,7168]{1,0:T(8,128)}, f32[64,7168]{1,0:T(8,128)S(1)}, u32[]{:S(2)}) copy-start(f32[64,7168]{1,0:T(8,128)S(1)} %get-tuple-element.31) | copy-start | bytes 5505028
  36.7 4.4 %collective-permute-start = (bf16[64,7168]{1,0:T(8,128)(2,1)S(1)}, bf16[64,7168]{1,0:T(8,128)(2,1)S(1)}, u32[]{:S(2)}, u32[]{:S(2)}) collective-permute-start(bf16[64,7168]{1,0:T(8,128)(2,1)S(1)} %get-tuple-element.27), channel_id=1, source_target_pairs={{0,16},{16,0},{32,48},{48,32},{64,80},{80,64},{96,112},{112,96},{1... | collective-permute-start | bytes 2752520 | tf_op jit(solution)/shard_map/ppermute | solution.py:259
  38.6 6.1 %copy-start.3 = (bf16[1,7168,128]{2,1,0:T(8,128)(2,1)S(1)}, bf16[1,7168,128]{2,1,0:T(8,128)(2,1)}, u32[]{:S(2)}) copy-start(bf16[1,7168,128]{2,1,0:T(8,128)(2,1)} %up_ref.1) | copy-start | bytes 5505028
  39.3 5.4 %copy-start.2 = (bf16[1,7168,128]{2,1,0:T(8,128)(2,1)S(1)}, bf16[1,7168,128]{2,1,0:T(8,128)(2,1)}, u32[]{:S(2)}) copy-start(bf16[1,7168,128]{2,1,0:T(8,128)(2,1)} %gate_ref.1) | copy-start | bytes 5505028
  41.1 25.0 %collective-permute-start.1 = (bf16[32,7168]{1,0:T(8,128)(2,1)S(1)}, bf16[32,7168]{1,0:T(8,128)(2,1)}, u32[]{:S(2)}, u32[]{:S(2)}) collective-permute-start(bf16[32,7168]{1,0:T(8,128)(2,1)S(1)} %add_convert_fusion), channel_id=1, source_target_pairs={{0,32},{16,1008},{32,64},{48,16},{64,96},{80,48},{96,128},{112,80}... | collective-permute-start | bytes 1376264 | tf_op jit(solution)/shard_map/ppermute | solution.py:289
  47.1 70.0 %all-to-all-start.1 = ((bf16[16,504,128]{2,1,0:T(8,128)(2,1)}), bf16[16,504,128]{2,1,0:T(8,128)(2,1)S(1)}, u32[]{:S(2)}, u32[]{:S(2)}) async-start(bf16[16,504,128]{2,1,0:T(8,128)(2,1)} %grad_rows.1), calls=%async_computation.1 | async-start | bytes 4128768 | tf_op jit(solution)/shard_map/all_to_all | solution.py:303
  67.2 16.6 %collective-permute-start.4 = (bf16[8,7168]{1,0:T(8,128)(2,1)S(1)}, bf16[8,7168]{1,0:T(8,128)(2,1)S(1)}, u32[]{:S(2)}, u32[]{:S(2)}) collective-permute-start(bf16[8,7168]{1,0:T(8,128)(2,1)S(1)} %get-tuple-element.42), channel_id=1, source_target_pairs={{0,896},{16,144},{32,928},{48,176},{64,960},{80,208},{96,992},{112... | collective-permute-start | bytes 344072 | tf_op jit(solution)/shard_map/ppermute | solution.py:289
  75.8 11.2 %collective-permute-start.3 = (bf16[8,7168]{1,0:T(8,128)(2,1)S(1)}, bf16[8,7168]{1,0:T(8,128)(2,1)S(1)}, u32[]{:S(2)}, u32[]{:S(2)}) collective-permute-start(bf16[8,7168]{1,0:T(8,128)(2,1)S(1)} %get-tuple-element.43), channel_id=1, source_target_pairs={{0,64},{16,976},{32,96},{48,1008},{64,128},{80,16},{96,160},{112,4... | collective-permute-start | bytes 344072 | tf_op jit(solution)/shard_map/ppermute | solution.py:289
  79.1 8.4 %collective-permute-start.2 = (bf16[8,7168]{1,0:T(8,128)(2,1)S(1)}, bf16[8,7168]{1,0:T(8,128)(2,1)S(1)}, u32[]{:S(2)}, u32[]{:S(2)}) collective-permute-start(bf16[8,7168]{1,0:T(8,128)(2,1)S(1)} %get-tuple-element.44), channel_id=1, source_target_pairs={{0,960},{16,80},{32,992},{48,112},{64,0},{80,144},{96,32},{112,176... | collective-permute-start | bytes 344072 | tf_op jit(solution)/shard_map/ppermute | solution.py:289
  87.7 30.8 %collective-permute-start.5 = (bf16[112,128]{1,0:T(8,128)(2,1)S(1)}, bf16[112,128]{1,0:T(8,128)(2,1)S(1)}, u32[]{:S(2)}, u32[]{:S(2)}) collective-permute-start(bf16[112,128]{1,0:T(8,128)(2,1)S(1)} %get-tuple-element.35), channel_id=1, source_target_pairs={{0,512},{16,528},{32,544},{48,560},{64,576},{80,592},{96,608},{112... | collective-permute-start | bytes 86024 | tf_op jit(solution)/shard_map/ppermute | solution.py:289
  102.5 16.8 %collective-permute-start.6 = (bf16[112,128]{1,0:T(8,128)(2,1)S(1)}, bf16[112,128]{1,0:T(8,128)(2,1)S(1)}, u32[]{:S(2)}, u32[]{:S(2)}) collective-permute-start(bf16[112,128]{1,0:T(8,128)(2,1)S(1)} %get-tuple-element.40), channel_id=1, source_target_pairs={{0,256},{16,784},{32,288},{48,816},{64,320},{80,848},{96,352},{112... | collective-permute-start | bytes 86024 | tf_op jit(solution)/shard_map/ppermute | solution.py:289
  109.8 14.7 %collective-permute-start.7 = (bf16[112,128]{1,0:T(8,128)(2,1)S(1)}, bf16[112,128]{1,0:T(8,128)(2,1)S(1)}, u32[]{:S(2)}, u32[]{:S(2)}) collective-permute-start(bf16[112,128]{1,0:T(8,128)(2,1)S(1)} %get-tuple-element.41), channel_id=1, source_target_pairs={{0,768},{16,272},{32,800},{48,304},{64,832},{80,336},{96,864},{112... | collective-permute-start | bytes 86024 | tf_op jit(solution)/shard_map/ppermute | solution.py:289

commit v8 on v7

--- a/solution.py
+++ b/solution.py
@@ -13,7 +13,7 @@
 FIRST = 8
 PARTS = 4
 NEAR = (0, -2, 2, -4)
-FAR = (0, 16, 8, -8)
+FAR = (0, 16, -8, 8)
 PARAMS = pltpu.CompilerParams(vmem_limit_bytes=16 * 1024 * 1024)
 
 
@@ -135,11 +135,12 @@
     core = jnp.where(at < half, at_ref[1], 1 - at_ref[1])
     share = half // chips
     place = at % half // share
-    far = place // (len(NEAR) * len(FAR))
+    sign = 1 - 2 * core
+    far = place // (len(NEAR) * len(FAR)) * sign
     for move in range(len(NEAR)):
-        far = far + jnp.where(place // len(FAR) % len(NEAR) == move, NEAR[move], 0)
+        far = far + jnp.where(place // len(FAR) % len(NEAR) == move, NEAR[move], 0) * sign
         far = far + jnp.where(place % len(FAR) == move, FAR[move], 0)
-    chip = (at_ref[0] + (1 - 2 * core) * far + 2 * chips) % chips
+    chip = (at_ref[0] + far + 2 * chips) % chips
     target = (2 * chip + core) * share + at % share
     hidden = dot(hidden, jnp.where(unit == target, 1.0, 0.0).astype(BF), ((1,), (0,))).astype(BF)
     tail[...] = got_ref[:, experts_rows(width) :, :].astype(F32)
@@ -266,7 +267,6 @@
         compiler_params=PARAMS,
         name="grad_hidden",
     )(arrived, factor, down_weight)
-    other, grad_hidden = lax.optimization_barrier((other, grad_hidden))
     going_back = pl.pallas_call(
         functools.partial(grad_kernel, experts),
         out_shape=pltpu.HBM(block.shape, BF),
@@ -280,26 +280,23 @@
         compiler_params=PARAMS,
         name="grad_rows",
     )(grad_hidden, gate_weight, up_weight)
-    def pass_on(going, distance):
-        hops = [
-            (2 * z + c, 2 * ((z + (distance if c == 0 else -distance)) % chips) + c)
-            for z in range(chips)
-            for c in range(2)
-        ]
+    def pass_on(going, moves):
+        hops = [(2 * z + c, 2 * ((z + moves[c]) % chips) + c) for z in range(chips) for c in range(2)]
         return lax.ppermute(going, "dp", hops)
 
     share = hidden_units // replicas
     count = half // 2
-    coming = pass_on((keep[count:] + other[count:].astype(F32)).astype(BF), 1)
-    keep, other = lax.optimization_barrier((keep, other))
+    other, _ = lax.optimization_barrier((other, going_back))
     total = lax.optimization_barrier(keep[:count] + other[:count].astype(F32))
-    coming, _ = lax.optimization_barrier((coming, going_back))
+    going = (keep[count:] + other[count:].astype(F32)).astype(BF)
+    going, going_back = lax.optimization_barrier((going, going_back))
+    coming = pass_on(going, (1, -1))
     count = count // len(NEAR)
     total, *going = [
         total[at : at + count] + coming[at : at + count].astype(F32)
         for at in range(0, half // 2, count)
     ]
-    parts = [pass_on(x.astype(BF), move) for x, move in zip(going, NEAR[1:])]
+    parts = [pass_on(x.astype(BF), (move, -move)) for x, move in zip(going, NEAR[1:])]
     returned = lax.all_to_all(going_back, "expert", split_axis=0, concat_axis=0, tiled=True)
     piece = (share * width // LANES, LANES)
     own, *going = pl.pallas_call(
@@ -311,7 +308,7 @@
         compiler_params=PARAMS,
         name="fold",
     )(total, *parts)
-    parts = [pass_on(x, move) for x, move in zip(going, FAR[1:])]
+    parts = [pass_on(x, (move, move)) for x, move in zip(going, FAR[1:])]
     grad_tokens = pl.pallas_call(
         functools.partial(combine_kernel, experts),
         out_shape=shape((tokens, width), BF),

time: 126 us -> 122 us (0.968)
  the two profiles are of different devices: /device:TPU:10 before, /device:TPU:64 now
where the time goes in v8:
time: 122 us; the launch traced here: 121 us
  starting transfers between devices  65.1 us (53%)
  blocking collectives  35 us (29%)
  waiting for transfers between devices  10.3 us (8%)
  Pallas kernels  9.13 us (7%)
    ppermute x7, starting transfers between devices, pass_on(): return lax.ppermute(going, 'dp', hops)  59.2 us
    all_to_all x1, blocking collectives, per_device(): lax.all_to_all(outgoing, 'expert', split_axis=0, concat_axis=0, tiled=True)  35 us
    ppermute x7, waiting for transfers between devices, pass_on(): return lax.ppermute(going, 'dp', hops)  10.3 us
    all_to_all x1, starting transfers between devices, per_device(): lax.all_to_all(going_back, 'expert', split_axis=0, concat_axis=0, tiled=T...  3.73 us
  transfers between devices with their start and end apart: 9, of which 4 were waited for; matrix products, arithmetic and copies ran while one was open for 0% of the time, Pallas kernels for 4%

profile of v8, /device:TPU:64, one launch (start us, length us, event | category | flops | bytes accessed | tf_op | source)
XLA Modules:
  0.0 121.5 jit_solution(3142812908949794104)
XLA Ops:
  0.6 0.1 pad_add_fusion.at_ref
  0.7 1.8 %dispatch_rows.1 = (bf16[16,504,128]{2,1,0:T(8,128)(2,1)S(1)}, bf16[144,32]{1,0:T(8,128)(2,1)S(1)}) custom-call(bf16[32,7168]{1,0:T(8,128)(2,1)} %dy_hbm.1, s32[4,32]{1,0:T(4,128)} %bitcast.4, f32[4,32]{1,0:T(4,128)} %bitcast.5), custom_call_target="tpu_custom_call" | custom-call | tf_op jit(solution)/shard_map/dispatch_rows/pallas_call | solution.py:224
  2.5 0.0 copy-start.3
  2.6 35.0 %all_to_all.10.got_ref = bf16[16,504,128]{2,1,0:T(8,128)(2,1)S(1)} all-to-all(bf16[16,504,128]{2,1,0:T(8,128)(2,1)S(1)} %get-tuple-element.22), channel_id=1, replica_groups=mesh['dp'=64,'expert'=16] {'expert'}, dimensions={0} | all-to-all | bytes 4128768 | tf_op jit(solution)/shard_map/all_to_all | solution.py:243
  37.6 0.0 copy-done.3
  37.6 0.0 copy-start
  37.6 2.0 %down_partial.1 = (bf16[144,7168]{1,0:T(8,128)(2,1)S(1)}, f32[64,7168]{1,0:T(8,128)S(1)}, bf16[64,7168]{1,0:T(8,128)(2,1)S(1)}, f32[144,256]{1,0:T(8,128)S(1)}) custom-call(s32[2]{0:T(128)S(1)} %pad_add_fusion.at_ref, bf16[16,504,128]{2,1,0:T(8,128)(2,1)S(1)} %all_to_all.10.got_ref, bf16[144,256]{1,0:T(8,128)(2,1)S(1)} %copy-done.3), custom_call_target="tpu_custom_call" | custom-call | tf_op jit(solution)/shard_map/down_partial/pallas_call | solution.py:246
  39.6 0.0 copy-start.1
  39.6 0.0 copy-start.2
  39.6 2.2 %collective-permute-start = (bf16[64,7168]{1,0:T(8,128)(2,1)S(1)}, bf16[64,7168]{1,0:T(8,128)(2,1)S(1)}, u32[]{:S(2)}, u32[]{:S(2)}) collective-permute-start(bf16[64,7168]{1,0:T(8,128)(2,1)S(1)} %get-tuple-element.25), channel_id=1, source_target_pairs={{0,16},{16,0},{32,48},{48,32},{64,80},{80,64},{96,112},{112,96},{1... | collective-permute-start | bytes 2752520 | tf_op jit(solution)/shard_map/ppermute | solution.py:260
  41.8 0.0 copy-done
  41.8 0.7 grad_hidden.1.hidden_ref
  42.5 0.0 copy-done.1
  42.5 0.0 copy-done.2
  42.5 2.4 %grad_rows.1 = bf16[16,504,128]{2,1,0:T(8,128)(2,1)} custom-call(bf16[144,256]{1,0:T(8,128)(2,1)S(1)} %grad_hidden.1.hidden_ref, bf16[1,7168,128]{2,1,0:T(8,128)(2,1)S(1)} %copy-done.1, bf16[1,7168,128]{2,1,0:T(8,128)(2,1)S(1)} %copy-done.2), custom_call_target="tpu_custom_call" | custom-call | tf_op jit(solution)/shard_map/grad_rows/pallas_call | solution.py:270
  44.9 0.0 collective-permute-done
  44.9 1.0 add_convert_fusion
  45.9 3.8 %collective-permute-start.1 = (bf16[32,7168]{1,0:T(8,128)(2,1)}, bf16[32,7168]{1,0:T(8,128)(2,1)S(1)}, u32[]{:S(2)}, u32[]{:S(2)}) collective-permute-start(bf16[32,7168]{1,0:T(8,128)(2,1)} %get-tuple-element.29), channel_id=1, source_target_pairs={{0,32},{16,1008},{32,64},{48,16},{64,96},{80,48},{96,128},{112,80}... | collective-permute-start | bytes 1376264 | tf_op jit(solution)/shard_map/ppermute | solution.py:285
  49.7 3.7 %all-to-all-start.1 = ((bf16[16,504,128]{2,1,0:T(8,128)(2,1)}), bf16[16,504,128]{2,1,0:T(8,128)(2,1)S(1)}, u32[]{:S(2)}, u32[]{:S(2)}) async-start(bf16[16,504,128]{2,1,0:T(8,128)(2,1)} %grad_rows.1), calls=%async_computation.1 | async-start | bytes 4128768 | tf_op jit(solution)/shard_map/all_to_all | solution.py:300
  53.4 3.0 %collective-permute-done.1 = bf16[32,7168]{1,0:T(8,128)(2,1)S(1)} collective-permute-done((bf16[32,7168]{1,0:T(8,128)(2,1)}, bf16[32,7168]{1,0:T(8,128)(2,1)S(1)}, u32[]{:S(2)}, u32[]{:S(2)}) %collective-permute-start.1) | collective-permute-done | bytes 458784 | tf_op jit(solution)/shard_map/ppermute | solution.py:285
  56.4 0.1 fusion
  56.5 18.2 %collective-permute-start.4 = (bf16[8,7168]{1,0:T(8,128)(2,1)S(1)}, bf16[8,7168]{1,0:T(8,128)(2,1)S(1)}, u32[]{:S(2)}, u32[]{:S(2)}) collective-permute-start(bf16[8,7168]{1,0:T(8,128)(2,1)S(1)} %get-tuple-element.40), channel_id=1, source_target_pairs={{0,896},{16,144},{32,928},{48,176},{64,960},{80,208},{96,992},{112... | collective-permute-start | bytes 344072 | tf_op jit(solution)/shard_map/ppermute | solution.py:285
  74.7 3.6 %collective-permute-start.3 = (bf16[8,7168]{1,0:T(8,128)(2,1)S(1)}, bf16[8,7168]{1,0:T(8,128)(2,1)S(1)}, u32[]{:S(2)}, u32[]{:S(2)}) collective-permute-start(bf16[8,7168]{1,0:T(8,128)(2,1)S(1)} %get-tuple-element.41), channel_id=1, source_target_pairs={{0,64},{16,976},{32,96},{48,1008},{64,128},{80,16},{96,160},{112,4... | collective-permute-start | bytes 344072 | tf_op jit(solution)/shard_map/ppermute | solution.py:285
  78.3 3.2 %collective-permute-start.2 = (bf16[8,7168]{1,0:T(8,128)(2,1)S(1)}, bf16[8,7168]{1,0:T(8,128)(2,1)S(1)}, u32[]{:S(2)}, u32[]{:S(2)}) collective-permute-start(bf16[8,7168]{1,0:T(8,128)(2,1)S(1)} %get-tuple-element.42), channel_id=1, source_target_pairs={{0,960},{16,80},{32,992},{48,112},{64,0},{80,144},{96,32},{112,176... | collective-permute-start | bytes 344072 | tf_op jit(solution)/shard_map/ppermute | solution.py:285
  81.5 0.0 collective-permute-done.4.refs_2_
  81.5 1.2 collective-permute-done.3.refs_1_
  82.7 5.1 %collective-permute-done.2.refs_0_ = bf16[8,7168]{1,0:T(8,128)(2,1)S(1)} collective-permute-done((bf16[8,7168]{1,0:T(8,128)(2,1)S(1)}, bf16[8,7168]{1,0:T(8,128)(2,1)S(1)}, u32[]{:S(2)}, u32[]{:S(2)}) %collective-permute-start.2) | collective-permute-done | bytes 114720 | tf_op jit(solution)/shard_map/ppermute | solution.py:285
  87.8 0.2 fold.1
  88.0 15.9 %collective-permute-start.5 = (bf16[112,128]{1,0:T(8,128)(2,1)S(1)}, bf16[112,128]{1,0:T(8,128)(2,1)S(1)}, u32[]{:S(2)}, u32[]{:S(2)}) collective-permute-start(bf16[112,128]{1,0:T(8,128)(2,1)S(1)} %get-tuple-element.30), channel_id=1, source_target_pairs={{0,512},{16,528},{32,544},{48,560},{64,576},{80,592},{96,608},{112... | collective-permute-start | bytes 86024 | tf_op jit(solution)/shard_map/ppermute | solution.py:285
  103.9 1.9 %collective-permute-start.6 = (bf16[112,128]{1,0:T(8,128)(2,1)S(1)}, bf16[112,128]{1,0:T(8,128)(2,1)S(1)}, u32[]{:S(2)}, u32[]{:S(2)}) collective-permute-start(bf16[112,128]{1,0:T(8,128)(2,1)S(1)} %get-tuple-element.36), channel_id=1, source_target_pairs={{0,768},{16,784},{32,800},{48,816},{64,832},{80,848},{96,864},{112... | collective-permute-start | bytes 86024 | tf_op jit(solution)/shard_map/ppermute | solution.py:285
  105.8 12.6 %collective-permute-start.7 = (bf16[112,128]{1,0:T(8,128)(2,1)S(1)}, bf16[112,128]{1,0:T(8,128)(2,1)S(1)}, u32[]{:S(2)}, u32[]{:S(2)}) collective-permute-start(bf16[112,128]{1,0:T(8,128)(2,1)S(1)} %get-tuple-element.37), channel_id=1, source_target_pairs={{0,256},{16,272},{32,288},{48,304},{64,320},{80,336},{96,352},{112... | collective-permute-start | bytes 86024 | tf_op jit(solution)/shard_map/ppermute | solution.py:285
  118.4 0.0 all-to-all-done.1.got_ref
  118.4 1.4 %combine_rows.1 = bf16[32,7168]{1,0:T(8,128)(2,1)} custom-call(bf16[144,32]{1,0:T(8,128)(2,1)S(1)} %get-tuple-element.31.pick_ref, bf16[16,504,128]{2,1,0:T(8,128)(2,1)S(1)} %all-to-all-done.1.got_ref), custom_call_target="tpu_custom_call" | custom-call | tf_op jit(solution)/shard_map/combine_rows/pallas_call | solution.py:312
  119.9 0.0 collective-permute-done.5.refs_0_
  119.9 0.0 collective-permute-done.6.refs_1_
  119.9 0.9 collective-permute-done.7.refs_2_
  120.8 0.7 finish.1
Async XLA Ops:
  2.5 35.0 %copy-start.3 = (bf16[144,256]{1,0:T(8,128)(2,1)S(1)}, bf16[144,256]{1,0:T(8,128)(2,1)}, u32[]{:S(2)}) copy-start(bf16[144,256]{1,0:T(8,128)(2,1)} %pre_ref) | copy-start | bytes 221188
  37.6 4.2 %copy-start = (bf16[1,128,7168]{2,1,0:T(8,128)(2,1)S(1)}, bf16[1,128,7168]{2,1,0:T(8,128)(2,1)}, u32[]{:S(2)}) copy-start(bf16[1,128,7168]{2,1,0:T(8,128)(2,1)} %down_ref.1) | copy-start | bytes 5505028
  39.6 2.9 %copy-start.1 = (bf16[1,7168,128]{2,1,0:T(8,128)(2,1)S(1)}, bf16[1,7168,128]{2,1,0:T(8,128)(2,1)}, u32[]{:S(2)}) copy-start(bf16[1,7168,128]{2,1,0:T(8,128)(2,1)} %gate_ref.1) | copy-start | bytes 5505028
  39.6 2.9 %copy-start.2 = (bf16[1,7168,128]{2,1,0:T(8,128)(2,1)S(1)}, bf16[1,7168,128]{2,1,0:T(8,128)(2,1)}, u32[]{:S(2)}) copy-start(bf16[1,7168,128]{2,1,0:T(8,128)(2,1)} %up_ref.1) | copy-start | bytes 5505028
  39.6 5.3 %collective-permute-start = (bf16[64,7168]{1,0:T(8,128)(2,1)S(1)}, bf16[64,7168]{1,0:T(8,128)(2,1)S(1)}, u32[]{:S(2)}, u32[]{:S(2)}) collective-permute-start(bf16[64,7168]{1,0:T(8,128)(2,1)S(1)} %get-tuple-element.25), channel_id=1, source_target_pairs={{0,16},{16,0},{32,48},{48,32},{64,80},{80,64},{96,112},{112,96},{1... | collective-permute-start | bytes 2752520 | tf_op jit(solution)/shard_map/ppermute | solution.py:260
  45.9 10.6 %collective-permute-start.1 = (bf16[32,7168]{1,0:T(8,128)(2,1)}, bf16[32,7168]{1,0:T(8,128)(2,1)S(1)}, u32[]{:S(2)}, u32[]{:S(2)}) collective-permute-start(bf16[32,7168]{1,0:T(8,128)(2,1)} %get-tuple-element.29), channel_id=1, source_target_pairs={{0,32},{16,1008},{32,64},{48,16},{64,96},{80,48},{96,128},{112,80}... | collective-permute-start | bytes 1376264 | tf_op jit(solution)/shard_map/ppermute | solution.py:285
  49.7 68.8 %all-to-all-start.1 = ((bf16[16,504,128]{2,1,0:T(8,128)(2,1)}), bf16[16,504,128]{2,1,0:T(8,128)(2,1)S(1)}, u32[]{:S(2)}, u32[]{:S(2)}) async-start(bf16[16,504,128]{2,1,0:T(8,128)(2,1)} %grad_rows.1), calls=%async_computation.1 | async-start | bytes 4128768 | tf_op jit(solution)/shard_map/all_to_all | solution.py:300
  56.5 25.0 %collective-permute-start.4 = (bf16[8,7168]{1,0:T(8,128)(2,1)S(1)}, bf16[8,7168]{1,0:T(8,128)(2,1)S(1)}, u32[]{:S(2)}, u32[]{:S(2)}) collective-permute-start(bf16[8,7168]{1,0:T(8,128)(2,1)S(1)} %get-tuple-element.40), channel_id=1, source_target_pairs={{0,896},{16,144},{32,928},{48,176},{64,960},{80,208},{96,992},{112... | collective-permute-start | bytes 344072 | tf_op jit(solution)/shard_map/ppermute | solution.py:285
  74.7 8.0 %collective-permute-start.3 = (bf16[8,7168]{1,0:T(8,128)(2,1)S(1)}, bf16[8,7168]{1,0:T(8,128)(2,1)S(1)}, u32[]{:S(2)}, u32[]{:S(2)}) collective-permute-start(bf16[8,7168]{1,0:T(8,128)(2,1)S(1)} %get-tuple-element.41), channel_id=1, source_target_pairs={{0,64},{16,976},{32,96},{48,1008},{64,128},{80,16},{96,160},{112,4... | collective-permute-start | bytes 344072 | tf_op jit(solution)/shard_map/ppermute | solution.py:285
  78.3 9.5 %collective-permute-start.2 = (bf16[8,7168]{1,0:T(8,128)(2,1)S(1)}, bf16[8,7168]{1,0:T(8,128)(2,1)S(1)}, u32[]{:S(2)}, u32[]{:S(2)}) collective-permute-start(bf16[8,7168]{1,0:T(8,128)(2,1)S(1)} %get-tuple-element.42), channel_id=1, source_target_pairs={{0,960},{16,80},{32,992},{48,112},{64,0},{80,144},{96,32},{112,176... | collective-permute-start | bytes 344072 | tf_op jit(solution)/shard_map/ppermute | solution.py:285
  88.0 31.9 %collective-permute-start.5 = (bf16[112,128]{1,0:T(8,128)(2,1)S(1)}, bf16[112,128]{1,0:T(8,128)(2,1)S(1)}, u32[]{:S(2)}, u32[]{:S(2)}) collective-permute-start(bf16[112,128]{1,0:T(8,128)(2,1)S(1)} %get-tuple-element.30), channel_id=1, source_target_pairs={{0,512},{16,528},{32,544},{48,560},{64,576},{80,592},{96,608},{112... | collective-permute-start | bytes 86024 | tf_op jit(solution)/shard_map/ppermute | solution.py:285
  103.9 16.0 %collective-permute-start.6 = (bf16[112,128]{1,0:T(8,128)(2,1)S(1)}, bf16[112,128]{1,0:T(8,128)(2,1)S(1)}, u32[]{:S(2)}, u32[]{:S(2)}) collective-permute-start(bf16[112,128]{1,0:T(8,128)(2,1)S(1)} %get-tuple-element.36), channel_id=1, source_target_pairs={{0,768},{16,784},{32,800},{48,816},{64,832},{80,848},{96,864},{112... | collective-permute-start | bytes 86024 | tf_op jit(solution)/shard_map/ppermute | solution.py:285
  105.8 15.0 %collective-permute-start.7 = (bf16[112,128]{1,0:T(8,128)(2,1)S(1)}, bf16[112,128]{1,0:T(8,128)(2,1)S(1)}, u32[]{:S(2)}, u32[]{:S(2)}) collective-permute-start(bf16[112,128]{1,0:T(8,128)(2,1)S(1)} %get-tuple-element.37), channel_id=1, source_target_pairs={{0,256},{16,272},{32,288},{48,304},{64,320},{80,336},{96,352},{112... | collective-permute-start | bytes 86024 | tf_op jit(solution)/shard_map/ppermute | solution.py:285

commit v9 on v8

--- a/solution.py
+++ b/solution.py
@@ -61,8 +61,8 @@
     main = experts * FIRST
     rows = main + experts
     slot = iota((rows, tokens), 0)
-    expert = jnp.where(slot < main, slot // FIRST, slot - main)
-    position = jnp.where(slot < main, slot % FIRST, FIRST)
+    expert = jnp.where(slot < main, slot >> 3, slot - main)
+    position = jnp.where(slot < main, slot & (FIRST - 1), FIRST)
     named = jnp.zeros((rows, tokens), F32)
     scale = jnp.zeros((rows, tokens), F32)
     for k in range(route_count):
@@ -120,7 +120,7 @@
     capacity = rows // experts
     new, old = iota((rows, rows), 0), iota((rows, rows), 1)
     source = jnp.where(
-        new < main, new // FIRST * capacity + new % FIRST, (new - main) * capacity + FIRST
+        new < main, (new >> 3) * capacity + (new & (FIRST - 1)), (new - main) * capacity + FIRST
     )
     order = jnp.where(source == old, 1.0, 0.0).astype(BF)
     pre = dot(order, pre_ref[...], ((1,), (0,)))
@@ -134,14 +134,15 @@
     unit, at = iota((hidden_units, hidden_units), 0), iota((hidden_units, hidden_units), 1)
     core = jnp.where(at < half, at_ref[1], 1 - at_ref[1])
     share = half // chips
-    place = at % half // share
+    place = (at & (half - 1)) >> 1
     sign = 1 - 2 * core
-    far = place // (len(NEAR) * len(FAR)) * sign
-    for move in range(len(NEAR)):
-        far = far + jnp.where(place // len(FAR) % len(NEAR) == move, NEAR[move], 0) * sign
-        far = far + jnp.where(place % len(FAR) == move, FAR[move], 0)
-    chip = (at_ref[0] + far + 2 * chips) % chips
-    target = (2 * chip + core) * share + at % share
+    far = jnp.zeros_like(place)
+    near = jnp.where(place >= len(NEAR) * len(FAR), 1, 0)
+    for move in range(1, len(NEAR)):
+        near = near + jnp.where((place >> 2) & 3 == move, NEAR[move], 0)
+        far = far + jnp.where(place & 3 == move, FAR[move], 0)
+    chip = (at_ref[0] + near * sign + far) & (chips - 1)
+    target = (2 * chip + core) * share + (at & 1)
     hidden = dot(hidden, jnp.where(unit == target, 1.0, 0.0).astype(BF), ((1,), (0,))).astype(BF)
     tail[...] = got_ref[:, experts_rows(width) :, :].astype(F32)
     for pair in range(width // (2 * LANES)):
@@ -214,7 +215,7 @@
     assert capacity == FIRST + 1
     block_rows = capacity * width // LANES
     chips = replicas // 2
-    assert chips == 2 * len(NEAR) * len(FAR) and hidden_units % replicas == 0
+    assert chips == 2 * len(NEAR) * len(FAR) and hidden_units == 2 * replicas and FIRST == 8
     shape = jax.ShapeDtypeStruct
     vmem = pl.BlockSpec(memory_space=pltpu.VMEM)
     smem = pl.BlockSpec(memory_space=pltpu.SMEM)

time: 122 us -> 122 us (level)
  no operation moved by 1% of the time
where the time goes in v9:
time: 122 us; the launch traced here: 121 us
  starting transfers between devices  65.1 us (53%)
  blocking collectives  35 us (29%)
  waiting for transfers between devices  10.3 us (8%)
  Pallas kernels  9.13 us (7%)
    ppermute x7, starting transfers between devices, pass_on(): return lax.ppermute(going, 'dp', hops)  59.2 us
    all_to_all x1, blocking collectives, per_device(): lax.all_to_all(outgoing, 'expert', split_axis=0, concat_axis=0, tiled=True)  35 us
    ppermute x7, waiting for transfers between devices, pass_on(): return lax.ppermute(going, 'dp', hops)  10.3 us
    all_to_all x1, starting transfers between devices, per_device(): lax.all_to_all(going_back, 'expert', split_axis=0, concat_axis=0, tiled=T...  3.73 us
  transfers between devices with their start and end apart: 9, of which 4 were waited for; matrix products, arithmetic and copies ran while one was open for 0% of the time, Pallas kernels for 4%

profile of v9, /device:TPU:64, one launch (start us, length us, event | category | flops | bytes accessed | tf_op | source)
XLA Modules:
  0.0 121.5 jit_solution(8153192355136089817)
XLA Ops:
  0.6 0.1 pad_add_fusion.at_ref
  0.7 1.8 %dispatch_rows.1 = (bf16[16,504,128]{2,1,0:T(8,128)(2,1)S(1)}, bf16[144,32]{1,0:T(8,128)(2,1)S(1)}) custom-call(bf16[32,7168]{1,0:T(8,128)(2,1)} %dy_hbm.1, s32[4,32]{1,0:T(4,128)} %bitcast.4, f32[4,32]{1,0:T(4,128)} %bitcast.5), custom_call_target="tpu_custom_call" | custom-call | tf_op jit(solution)/shard_map/dispatch_rows/pallas_call | solution.py:225
  2.5 0.0 copy-start.3
  2.5 35.0 %all_to_all.10.got_ref = bf16[16,504,128]{2,1,0:T(8,128)(2,1)S(1)} all-to-all(bf16[16,504,128]{2,1,0:T(8,128)(2,1)S(1)} %get-tuple-element.22), channel_id=1, replica_groups=mesh['dp'=64,'expert'=16] {'expert'}, dimensions={0} | all-to-all | bytes 4128768 | tf_op jit(solution)/shard_map/all_to_all | solution.py:244
  37.6 0.0 copy-done.3
  37.6 0.0 copy-start
  37.6 2.0 %down_partial.1 = (bf16[144,7168]{1,0:T(8,128)(2,1)S(1)}, f32[64,7168]{1,0:T(8,128)S(1)}, bf16[64,7168]{1,0:T(8,128)(2,1)S(1)}, f32[144,256]{1,0:T(8,128)S(1)}) custom-call(s32[2]{0:T(128)S(1)} %pad_add_fusion.at_ref, bf16[16,504,128]{2,1,0:T(8,128)(2,1)S(1)} %all_to_all.10.got_ref, bf16[144,256]{1,0:T(8,128)(2,1)S(1)} %copy-done.3), custom_call_target="tpu_custom_call" | custom-call | tf_op jit(solution)/shard_map/down_partial/pallas_call | solution.py:247
  39.6 0.0 copy-start.1
  39.6 0.0 copy-start.2
  39.6 2.2 %collective-permute-start = (bf16[64,7168]{1,0:T(8,128)(2,1)S(1)}, bf16[64,7168]{1,0:T(8,128)(2,1)S(1)}, u32[]{:S(2)}, u32[]{:S(2)}) collective-permute-start(bf16[64,7168]{1,0:T(8,128)(2,1)S(1)} %get-tuple-element.25), channel_id=1, source_target_pairs={{0,16},{16,0},{32,48},{48,32},{64,80},{80,64},{96,112},{112,96},{1... | collective-permute-start | bytes 2752520 | tf_op jit(solution)/shard_map/ppermute | solution.py:261
  41.8 0.0 copy-done
  41.8 0.7 grad_hidden.1.hidden_ref
  42.5 0.0 copy-done.1
  42.5 0.0 copy-done.2
  42.5 2.4 %grad_rows.1 = bf16[16,504,128]{2,1,0:T(8,128)(2,1)} custom-call(bf16[144,256]{1,0:T(8,128)(2,1)S(1)} %grad_hidden.1.hidden_ref, bf16[1,7168,128]{2,1,0:T(8,128)(2,1)S(1)} %copy-done.1, bf16[1,7168,128]{2,1,0:T(8,128)(2,1)S(1)} %copy-done.2), custom_call_target="tpu_custom_call" | custom-call | tf_op jit(solution)/shard_map/grad_rows/pallas_call | solution.py:271
  44.9 0.0 collective-permute-done
  44.9 1.0 add_convert_fusion
  45.9 3.8 %collective-permute-start.1 = (bf16[32,7168]{1,0:T(8,128)(2,1)}, bf16[32,7168]{1,0:T(8,128)(2,1)S(1)}, u32[]{:S(2)}, u32[]{:S(2)}) collective-permute-start(bf16[32,7168]{1,0:T(8,128)(2,1)} %get-tuple-element.29), channel_id=1, source_target_pairs={{0,32},{16,1008},{32,64},{48,16},{64,96},{80,48},{96,128},{112,80}... | collective-permute-start | bytes 1376264 | tf_op jit(solution)/shard_map/ppermute | solution.py:286
  49.7 3.7 %all-to-all-start.1 = ((bf16[16,504,128]{2,1,0:T(8,128)(2,1)}), bf16[16,504,128]{2,1,0:T(8,128)(2,1)S(1)}, u32[]{:S(2)}, u32[]{:S(2)}) async-start(bf16[16,504,128]{2,1,0:T(8,128)(2,1)} %grad_rows.1), calls=%async_computation.1 | async-start | bytes 4128768 | tf_op jit(solution)/shard_map/all_to_all | solution.py:301
  53.4 3.0 %collective-permute-done.1 = bf16[32,7168]{1,0:T(8,128)(2,1)S(1)} collective-permute-done((bf16[32,7168]{1,0:T(8,128)(2,1)}, bf16[32,7168]{1,0:T(8,128)(2,1)S(1)}, u32[]{:S(2)}, u32[]{:S(2)}) %collective-permute-start.1) | collective-permute-done | bytes 458784 | tf_op jit(solution)/shard_map/ppermute | solution.py:286
  56.4 0.1 fusion
  56.5 18.2 %collective-permute-start.4 = (bf16[8,7168]{1,0:T(8,128)(2,1)S(1)}, bf16[8,7168]{1,0:T(8,128)(2,1)S(1)}, u32[]{:S(2)}, u32[]{:S(2)}) collective-permute-start(bf16[8,7168]{1,0:T(8,128)(2,1)S(1)} %get-tuple-element.40), channel_id=1, source_target_pairs={{0,896},{16,144},{32,928},{48,176},{64,960},{80,208},{96,992},{112... | collective-permute-start | bytes 344072 | tf_op jit(solution)/shard_map/ppermute | solution.py:286
  74.7 3.6 %collective-permute-start.3 = (bf16[8,7168]{1,0:T(8,128)(2,1)S(1)}, bf16[8,7168]{1,0:T(8,128)(2,1)S(1)}, u32[]{:S(2)}, u32[]{:S(2)}) collective-permute-start(bf16[8,7168]{1,0:T(8,128)(2,1)S(1)} %get-tuple-element.41), channel_id=1, source_target_pairs={{0,64},{16,976},{32,96},{48,1008},{64,128},{80,16},{96,160},{112,4... | collective-permute-start | bytes 344072 | tf_op jit(solution)/shard_map/ppermute | solution.py:286
  78.3 3.2 %collective-permute-start.2 = (bf16[8,7168]{1,0:T(8,128)(2,1)S(1)}, bf16[8,7168]{1,0:T(8,128)(2,1)S(1)}, u32[]{:S(2)}, u32[]{:S(2)}) collective-permute-start(bf16[8,7168]{1,0:T(8,128)(2,1)S(1)} %get-tuple-element.42), channel_id=1, source_target_pairs={{0,960},{16,80},{32,992},{48,112},{64,0},{80,144},{96,32},{112,176... | collective-permute-start | bytes 344072 | tf_op jit(solution)/shard_map/ppermute | solution.py:286
  81.5 0.0 collective-permute-done.4.refs_2_
  81.5 1.2 collective-permute-done.3.refs_1_
  82.7 5.1 %collective-permute-done.2.refs_0_ = bf16[8,7168]{1,0:T(8,128)(2,1)S(1)} collective-permute-done((bf16[8,7168]{1,0:T(8,128)(2,1)S(1)}, bf16[8,7168]{1,0:T(8,128)(2,1)S(1)}, u32[]{:S(2)}, u32[]{:S(2)}) %collective-permute-start.2) | collective-permute-done | bytes 114720 | tf_op jit(solution)/shard_map/ppermute | solution.py:286
  87.8 0.2 fold.1
  88.0 15.9 %collective-permute-start.5 = (bf16[112,128]{1,0:T(8,128)(2,1)S(1)}, bf16[112,128]{1,0:T(8,128)(2,1)S(1)}, u32[]{:S(2)}, u32[]{:S(2)}) collective-permute-start(bf16[112,128]{1,0:T(8,128)(2,1)S(1)} %get-tuple-element.30), channel_id=1, source_target_pairs={{0,512},{16,528},{32,544},{48,560},{64,576},{80,592},{96,608},{112... | collective-permute-start | bytes 86024 | tf_op jit(solution)/shard_map/ppermute | solution.py:286
  103.9 1.9 %collective-permute-start.6 = (bf16[112,128]{1,0:T(8,128)(2,1)S(1)}, bf16[112,128]{1,0:T(8,128)(2,1)S(1)}, u32[]{:S(2)}, u32[]{:S(2)}) collective-permute-start(bf16[112,128]{1,0:T(8,128)(2,1)S(1)} %get-tuple-element.36), channel_id=1, source_target_pairs={{0,768},{16,784},{32,800},{48,816},{64,832},{80,848},{96,864},{112... | collective-permute-start | bytes 86024 | tf_op jit(solution)/shard_map/ppermute | solution.py:286
  105.8 12.6 %collective-permute-start.7 = (bf16[112,128]{1,0:T(8,128)(2,1)S(1)}, bf16[112,128]{1,0:T(8,128)(2,1)S(1)}, u32[]{:S(2)}, u32[]{:S(2)}) collective-permute-start(bf16[112,128]{1,0:T(8,128)(2,1)S(1)} %get-tuple-element.37), channel_id=1, source_target_pairs={{0,256},{16,272},{32,288},{48,304},{64,320},{80,336},{96,352},{112... | collective-permute-start | bytes 86024 | tf_op jit(solution)/shard_map/ppermute | solution.py:286
  118.4 0.0 all-to-all-done.1.got_ref
  118.4 1.4 %combine_rows.1 = bf16[32,7168]{1,0:T(8,128)(2,1)} custom-call(bf16[144,32]{1,0:T(8,128)(2,1)S(1)} %get-tuple-element.31.pick_ref, bf16[16,504,128]{2,1,0:T(8,128)(2,1)S(1)} %all-to-all-done.1.got_ref), custom_call_target="tpu_custom_call" | custom-call | tf_op jit(solution)/shard_map/combine_rows/pallas_call | solution.py:313
  119.9 0.0 collective-permute-done.5.refs_0_
  119.9 0.0 collective-permute-done.6.refs_1_
  119.9 0.9 collective-permute-done.7.refs_2_
  120.8 0.7 finish.1
Async XLA Ops:
  2.5 35.0 %copy-start.3 = (bf16[144,256]{1,0:T(8,128)(2,1)S(1)}, bf16[144,256]{1,0:T(8,128)(2,1)}, u32[]{:S(2)}) copy-start(bf16[144,256]{1,0:T(8,128)(2,1)} %pre_ref) | copy-start | bytes 221188
  37.6 4.2 %copy-start = (bf16[1,128,7168]{2,1,0:T(8,128)(2,1)S(1)}, bf16[1,128,7168]{2,1,0:T(8,128)(2,1)}, u32[]{:S(2)}) copy-start(bf16[1,128,7168]{2,1,0:T(8,128)(2,1)} %down_ref.1) | copy-start | bytes 5505028
  39.6 2.9 %copy-start.1 = (bf16[1,7168,128]{2,1,0:T(8,128)(2,1)S(1)}, bf16[1,7168,128]{2,1,0:T(8,128)(2,1)}, u32[]{:S(2)}) copy-start(bf16[1,7168,128]{2,1,0:T(8,128)(2,1)} %gate_ref.1) | copy-start | bytes 5505028
  39.6 2.9 %copy-start.2 = (bf16[1,7168,128]{2,1,0:T(8,128)(2,1)S(1)}, bf16[1,7168,128]{2,1,0:T(8,128)(2,1)}, u32[]{:S(2)}) copy-start(bf16[1,7168,128]{2,1,0:T(8,128)(2,1)} %up_ref.1) | copy-start | bytes 5505028
  39.6 5.3 %collective-permute-start = (bf16[64,7168]{1,0:T(8,128)(2,1)S(1)}, bf16[64,7168]{1,0:T(8,128)(2,1)S(1)}, u32[]{:S(2)}, u32[]{:S(2)}) collective-permute-start(bf16[64,7168]{1,0:T(8,128)(2,1)S(1)} %get-tuple-element.25), channel_id=1, source_target_pairs={{0,16},{16,0},{32,48},{48,32},{64,80},{80,64},{96,112},{112,96},{1... | collective-permute-start | bytes 2752520 | tf_op jit(solution)/shard_map/ppermute | solution.py:261
  45.9 10.6 %collective-permute-start.1 = (bf16[32,7168]{1,0:T(8,128)(2,1)}, bf16[32,7168]{1,0:T(8,128)(2,1)S(1)}, u32[]{:S(2)}, u32[]{:S(2)}) collective-permute-start(bf16[32,7168]{1,0:T(8,128)(2,1)} %get-tuple-element.29), channel_id=1, source_target_pairs={{0,32},{16,1008},{32,64},{48,16},{64,96},{80,48},{96,128},{112,80}... | collective-permute-start | bytes 1376264 | tf_op jit(solution)/shard_map/ppermute | solution.py:286
  49.7 68.8 %all-to-all-start.1 = ((bf16[16,504,128]{2,1,0:T(8,128)(2,1)}), bf16[16,504,128]{2,1,0:T(8,128)(2,1)S(1)}, u32[]{:S(2)}, u32[]{:S(2)}) async-start(bf16[16,504,128]{2,1,0:T(8,128)(2,1)} %grad_rows.1), calls=%async_computation.1 | async-start | bytes 4128768 | tf_op jit(solution)/shard_map/all_to_all | solution.py:301
  56.5 25.0 %collective-permute-start.4 = (bf16[8,7168]{1,0:T(8,128)(2,1)S(1)}, bf16[8,7168]{1,0:T(8,128)(2,1)S(1)}, u32[]{:S(2)}, u32[]{:S(2)}) collective-permute-start(bf16[8,7168]{1,0:T(8,128)(2,1)S(1)} %get-tuple-element.40), channel_id=1, source_target_pairs={{0,896},{16,144},{32,928},{48,176},{64,960},{80,208},{96,992},{112... | collective-permute-start | bytes 344072 | tf_op jit(solution)/shard_map/ppermute | solution.py:286
  74.7 8.0 %collective-permute-start.3 = (bf16[8,7168]{1,0:T(8,128)(2,1)S(1)}, bf16[8,7168]{1,0:T(8,128)(2,1)S(1)}, u32[]{:S(2)}, u32[]{:S(2)}) collective-permute-start(bf16[8,7168]{1,0:T(8,128)(2,1)S(1)} %get-tuple-element.41), channel_id=1, source_target_pairs={{0,64},{16,976},{32,96},{48,1008},{64,128},{80,16},{96,160},{112,4... | collective-permute-start | bytes 344072 | tf_op jit(solution)/shard_map/ppermute | solution.py:286
  78.3 9.5 %collective-permute-start.2 = (bf16[8,7168]{1,0:T(8,128)(2,1)S(1)}, bf16[8,7168]{1,0:T(8,128)(2,1)S(1)}, u32[]{:S(2)}, u32[]{:S(2)}) collective-permute-start(bf16[8,7168]{1,0:T(8,128)(2,1)S(1)} %get-tuple-element.42), channel_id=1, source_target_pairs={{0,960},{16,80},{32,992},{48,112},{64,0},{80,144},{96,32},{112,176... | collective-permute-start | bytes 344072 | tf_op jit(solution)/shard_map/ppermute | solution.py:286
  88.0 31.9 %collective-permute-start.5 = (bf16[112,128]{1,0:T(8,128)(2,1)S(1)}, bf16[112,128]{1,0:T(8,128)(2,1)S(1)}, u32[]{:S(2)}, u32[]{:S(2)}) collective-permute-start(bf16[112,128]{1,0:T(8,128)(2,1)S(1)} %get-tuple-element.30), channel_id=1, source_target_pairs={{0,512},{16,528},{32,544},{48,560},{64,576},{80,592},{96,608},{112... | collective-permute-start | bytes 86024 | tf_op jit(solution)/shard_map/ppermute | solution.py:286
  103.9 16.0 %collective-permute-start.6 = (bf16[112,128]{1,0:T(8,128)(2,1)S(1)}, bf16[112,128]{1,0:T(8,128)(2,1)S(1)}, u32[]{:S(2)}, u32[]{:S(2)}) collective-permute-start(bf16[112,128]{1,0:T(8,128)(2,1)S(1)} %get-tuple-element.36), channel_id=1, source_target_pairs={{0,768},{16,784},{32,800},{48,816},{64,832},{80,848},{96,864},{112... | collective-permute-start | bytes 86024 | tf_op jit(solution)/shard_map/ppermute | solution.py:286
  105.8 15.0 %collective-permute-start.7 = (bf16[112,128]{1,0:T(8,128)(2,1)S(1)}, bf16[112,128]{1,0:T(8,128)(2,1)S(1)}, u32[]{:S(2)}, u32[]{:S(2)}) collective-permute-start(bf16[112,128]{1,0:T(8,128)(2,1)S(1)} %get-tuple-element.37), channel_id=1, source_target_pairs={{0,256},{16,272},{32,288},{48,304},{64,320},{80,336},{96,352},{112... | collective-permute-start | bytes 86024 | tf_op jit(solution)/shard_map/ppermute | solution.py:286

commit v10 on v9

--- a/solution.py
+++ b/solution.py
@@ -112,7 +112,7 @@
 
 
 def partial_kernel(
-    experts, chips, at_ref, got_ref, pre_ref, arrived_ref, keep_ref, send_ref, factor_ref, tail
+    experts, chips, at_ref, got_ref, pre_ref, arrived_ref, own_ref, send_ref, factor_ref, tail
 ):
     rows, width = arrived_ref.shape
     hidden_units = pre_ref.shape[1] // 2
@@ -144,14 +144,21 @@
     chip = (at_ref[0] + near * sign + far) & (chips - 1)
     target = (2 * chip + core) * share + (at & 1)
     hidden = dot(hidden, jnp.where(unit == target, 1.0, 0.0).astype(BF), ((1,), (0,))).astype(BF)
+    own_ref[...] = hidden[:, :half]
+    going = hidden[:, half:]
     tail[...] = got_ref[:, experts_rows(width) :, :].astype(F32)
     for pair in range(width // (2 * LANES)):
         at = slice(pair * 2 * LANES, (pair + 1) * 2 * LANES)
         arrived = read_block(got_ref, tail, pair, experts).astype(BF)
         arrived_ref[:, at] = arrived
-        part = dot(hidden, arrived, ((0,), (0,)))
-        keep_ref[:, at] = part[:half]
-        send_ref[:, at] = part[half:].astype(BF)
+        send_ref[:, at] = dot(going, arrived, ((0,), (0,))).astype(BF)
+
+
+def kept_kernel(own_ref, arrived_ref, out_ref):
+    own = own_ref[...]
+    for pair in range(out_ref.shape[1] // (2 * LANES)):
+        at = slice(pair * 2 * LANES, (pair + 1) * 2 * LANES)
+        out_ref[:, at] = dot(own, arrived_ref[:, at], ((0,), (0,)))
 
 
 def hidden_kernel(arrived_ref, factor_ref, down_ref, out_ref):
@@ -244,11 +251,11 @@
     got = lax.all_to_all(outgoing, "expert", split_axis=0, concat_axis=0, tiled=True)
 
     half = hidden_units // 2
-    arrived, keep, send, factor = pl.pallas_call(
+    arrived, own_hidden, send, factor = pl.pallas_call(
         functools.partial(partial_kernel, experts, chips),
         out_shape=(
             shape((rows, width), BF),
-            shape((half, width), F32),
+            shape((rows, half), BF),
             shape((half, width), BF),
             shape((rows, 2 * hidden_units), F32),
         ),
@@ -259,6 +266,14 @@
         name="down_partial",
     )(place, got, pre_act)
     other = lax.ppermute(send, "dp", [(i, i ^ 1) for i in range(replicas)])
+    keep = pl.pallas_call(
+        kept_kernel,
+        out_shape=shape((half, width), F32),
+        in_specs=[vmem] * 2,
+        out_specs=vmem,
+        compiler_params=PARAMS,
+        name="down_kept",
+    )(own_hidden, arrived)
 
     grad_hidden = pl.pallas_call(
         hidden_kernel,
@@ -268,6 +283,7 @@
         compiler_params=PARAMS,
         name="grad_hidden",
     )(arrived, factor, down_weight)
+    other, grad_hidden, keep = lax.optimization_barrier((other, grad_hidden, keep))
     going_back = pl.pallas_call(
         functools.partial(grad_kernel, experts),
         out_shape=pltpu.HBM(block.shape, BF),
@@ -287,11 +303,10 @@
 
     share = hidden_units // replicas
     count = half // 2
-    other, _ = lax.optimization_barrier((other, going_back))
     total = lax.optimization_barrier(keep[:count] + other[:count].astype(F32))
     going = (keep[count:] + other[count:].astype(F32)).astype(BF)
-    going, going_back = lax.optimization_barrier((going, going_back))
     coming = pass_on(going, (1, -1))
+    coming, _ = lax.optimization_barrier((coming, going_back))
     count = count // len(NEAR)
     total, *going = [
         total[at : at + count] + coming[at : at + count].astype(F32)

time: 122 us -> 121 us (level)
    ppermute x7, waiting for transfers between devices: 10.3 us -> 8.19 us  [pass_on(): return lax.ppermute(going, 'dp', hops)]
    ppermute x1, waiting for transfers between devices: 0.01 us -> 1.24 us  [per_device(): other = lax.ppermute(send, 'dp', [(i, i ^ 1) for i in range(replicas)])]
  transfers between devices with their start and end apart: 9 -> 9, of which waited for: 4 -> 6; matrix products, arithmetic and copies ran while one was open for 0% -> 0% of each run, Pallas kernels for 4% -> 4%
where the time goes in v10:
time: 121 us; the launch traced here: 120 us
  starting transfers between devices  64.6 us (53%)
  blocking collectives  35 us (29%)
  waiting for transfers between devices  9.44 us (8%)
  Pallas kernels  9.3 us (8%)
    ppermute x7, starting transfers between devices, pass_on(): return lax.ppermute(going, 'dp', hops)  58.8 us
    all_to_all x1, blocking collectives, per_device(): lax.all_to_all(outgoing, 'expert', split_axis=0, concat_axis=0, tiled=True)  35 us
    ppermute x7, waiting for transfers between devices, pass_on(): return lax.ppermute(going, 'dp', hops)  8.19 us
    all_to_all x1, starting transfers between devices, per_device(): lax.all_to_all(going_back, 'expert', split_axis=0, concat_axis=0, tiled=T...  3.73 us
  transfers between devices with their start and end apart: 9, of which 6 were waited for; matrix products, arithmetic and copies ran while one was open for 0% of the time, Pallas kernels for 4%

profile of v10, /device:TPU:64, one launch (start us, length us, event | category | flops | bytes accessed | tf_op | source)
XLA Modules:
  0.0 120.3 jit_solution(17936877682440267791)
XLA Ops:
  0.6 0.1 pad_add_fusion.at_ref
  0.7 1.8 %dispatch_rows.1 = (bf16[16,504,128]{2,1,0:T(8,128)(2,1)S(1)}, bf16[144,32]{1,0:T(8,128)(2,1)S(1)}) custom-call(bf16[32,7168]{1,0:T(8,128)(2,1)} %dy_hbm.1, s32[4,32]{1,0:T(4,128)} %bitcast.4, f32[4,32]{1,0:T(4,128)} %bitcast.5), custom_call_target="tpu_custom_call" | custom-call | tf_op jit(solution)/shard_map/dispatch_rows/pallas_call | solution.py:232
  2.5 0.0 copy-start.3
  2.6 35.0 %all_to_all.10.got_ref = bf16[16,504,128]{2,1,0:T(8,128)(2,1)S(1)} all-to-all(bf16[16,504,128]{2,1,0:T(8,128)(2,1)S(1)} %get-tuple-element.23), channel_id=1, replica_groups=mesh['dp'=64,'expert'=16] {'expert'}, dimensions={0} | all-to-all | bytes 4128768 | tf_op jit(solution)/shard_map/all_to_all | solution.py:251
  37.6 0.0 copy-done.3
  37.6 1.7 %down_partial.1 = (bf16[144,7168]{1,0:T(8,128)(2,1)S(1)}, bf16[144,64]{1,0:T(8,128)(2,1)S(1)}, bf16[64,7168]{1,0:T(8,128)(2,1)S(1)}, f32[144,256]{1,0:T(8,128)S(1)}) custom-call(s32[2]{0:T(128)S(1)} %pad_add_fusion.at_ref, bf16[16,504,128]{2,1,0:T(8,128)(2,1)S(1)} %all_to_all.10.got_ref, bf16[144,256]{1,0:T(8,128)(2,1)S(1)} %copy-done.3), custom_call_target="tpu_custom_call" | custom-call | tf_op jit(solution)/shard_map/down_partial/pallas_call | solution.py:254
  39.2 0.0 copy-start
  39.2 2.1 %collective-permute-start = (bf16[64,7168]{1,0:T(8,128)(2,1)S(1)}, bf16[64,7168]{1,0:T(8,128)(2,1)S(1)}, u32[]{:S(2)}, u32[]{:S(2)}) collective-permute-start(bf16[64,7168]{1,0:T(8,128)(2,1)S(1)} %get-tuple-element.25), channel_id=1, source_target_pairs={{0,16},{16,0},{32,48},{48,32},{64,80},{80,64},{96,112},{112,96},{1... | collective-permute-start | bytes 2752520 | tf_op jit(solution)/shard_map/ppermute | solution.py:268
  41.3 0.5 down_kept.1
  41.8 0.0 copy-done
  41.8 0.7 grad_hidden.1.hidden_ref
  42.5 0.0 copy-start.1
  42.5 0.0 copy-start.2
  42.5 1.2 %collective-permute-done = bf16[64,7168]{1,0:T(8,128)(2,1)S(1)} collective-permute-done((bf16[64,7168]{1,0:T(8,128)(2,1)S(1)}, bf16[64,7168]{1,0:T(8,128)(2,1)S(1)}, u32[]{:S(2)}, u32[]{:S(2)}) %collective-permute-start) | collective-permute-done | bytes 917536 | tf_op jit(solution)/shard_map/ppermute | solution.py:268
  43.7 1.0 add_convert_fusion
  44.7 3.8 %collective-permute-start.1 = (bf16[32,7168]{1,0:T(8,128)(2,1)}, bf16[32,7168]{1,0:T(8,128)(2,1)S(1)}, u32[]{:S(2)}, u32[]{:S(2)}) collective-permute-start(bf16[32,7168]{1,0:T(8,128)(2,1)} %get-tuple-element.40), channel_id=1, source_target_pairs={{0,32},{16,1008},{32,64},{48,16},{64,96},{80,48},{96,128},{112,80}... | collective-permute-start | bytes 1376264 | tf_op jit(solution)/shard_map/ppermute | solution.py:302
  48.5 0.0 copy-done.1
  48.5 0.0 copy-done.2
  48.5 2.4 %grad_rows.1 = bf16[16,504,128]{2,1,0:T(8,128)(2,1)} custom-call(bf16[144,256]{1,0:T(8,128)(2,1)S(1)} %grad_hidden.1.hidden_ref, bf16[1,7168,128]{2,1,0:T(8,128)(2,1)S(1)} %copy-done.1, bf16[1,7168,128]{2,1,0:T(8,128)(2,1)S(1)} %copy-done.2), custom_call_target="tpu_custom_call" | custom-call | tf_op jit(solution)/shard_map/grad_rows/pallas_call | solution.py:287
  50.9 3.7 %all-to-all-start.1 = ((bf16[16,504,128]{2,1,0:T(8,128)(2,1)}), bf16[16,504,128]{2,1,0:T(8,128)(2,1)S(1)}, u32[]{:S(2)}, u32[]{:S(2)}) async-start(bf16[16,504,128]{2,1,0:T(8,128)(2,1)} %grad_rows.1), calls=%async_computation.1 | async-start | bytes 4128768 | tf_op jit(solution)/shard_map/all_to_all | solution.py:316
  54.7 0.6 collective-permute-done.1
  55.3 0.1 fusion
  55.4 18.2 %collective-permute-start.4 = (bf16[8,7168]{1,0:T(8,128)(2,1)S(1)}, bf16[8,7168]{1,0:T(8,128)(2,1)S(1)}, u32[]{:S(2)}, u32[]{:S(2)}) collective-permute-start(bf16[8,7168]{1,0:T(8,128)(2,1)S(1)} %get-tuple-element.42), channel_id=1, source_target_pairs={{0,896},{16,144},{32,928},{48,176},{64,960},{80,208},{96,992},{112... | collective-permute-start | bytes 344072 | tf_op jit(solution)/shard_map/ppermute | solution.py:302
  73.6 3.6 %collective-permute-start.3 = (bf16[8,7168]{1,0:T(8,128)(2,1)S(1)}, bf16[8,7168]{1,0:T(8,128)(2,1)S(1)}, u32[]{:S(2)}, u32[]{:S(2)}) collective-permute-start(bf16[8,7168]{1,0:T(8,128)(2,1)S(1)} %get-tuple-element.43), channel_id=1, source_target_pairs={{0,64},{16,976},{32,96},{48,1008},{64,128},{80,16},{96,160},{112,4... | collective-permute-start | bytes 344072 | tf_op jit(solution)/shard_map/ppermute | solution.py:302
  77.2 3.2 %collective-permute-start.2 = (bf16[8,7168]{1,0:T(8,128)(2,1)S(1)}, bf16[8,7168]{1,0:T(8,128)(2,1)S(1)}, u32[]{:S(2)}, u32[]{:S(2)}) collective-permute-start(bf16[8,7168]{1,0:T(8,128)(2,1)S(1)} %get-tuple-element.44), channel_id=1, source_target_pairs={{0,960},{16,80},{32,992},{48,112},{64,0},{80,144},{96,32},{112,176... | collective-permute-start | bytes 344072 | tf_op jit(solution)/shard_map/ppermute | solution.py:302
  80.3 0.0 collective-permute-done.4.refs_2_
  80.3 0.8 collective-permute-done.3.refs_1_
  81.2 5.5 %collective-permute-done.2.refs_0_ = bf16[8,7168]{1,0:T(8,128)(2,1)S(1)} collective-permute-done((bf16[8,7168]{1,0:T(8,128)(2,1)S(1)}, bf16[8,7168]{1,0:T(8,128)(2,1)S(1)}, u32[]{:S(2)}, u32[]{:S(2)}) %collective-permute-start.2) | collective-permute-done | bytes 114720 | tf_op jit(solution)/shard_map/ppermute | solution.py:302
  86.7 0.2 fold.1
  86.8 15.5 %collective-permute-start.5 = (bf16[112,128]{1,0:T(8,128)(2,1)S(1)}, bf16[112,128]{1,0:T(8,128)(2,1)S(1)}, u32[]{:S(2)}, u32[]{:S(2)}) collective-permute-start(bf16[112,128]{1,0:T(8,128)(2,1)S(1)} %get-tuple-element.33), channel_id=1, source_target_pairs={{0,512},{16,528},{32,544},{48,560},{64,576},{80,592},{96,608},{112... | collective-permute-start | bytes 86024 | tf_op jit(solution)/shard_map/ppermute | solution.py:302
  102.4 1.9 %collective-permute-start.6 = (bf16[112,128]{1,0:T(8,128)(2,1)S(1)}, bf16[112,128]{1,0:T(8,128)(2,1)S(1)}, u32[]{:S(2)}, u32[]{:S(2)}) collective-permute-start(bf16[112,128]{1,0:T(8,128)(2,1)S(1)} %get-tuple-element.38), channel_id=1, source_target_pairs={{0,768},{16,784},{32,800},{48,816},{64,832},{80,848},{96,864},{112... | collective-permute-start | bytes 86024 | tf_op jit(solution)/shard_map/ppermute | solution.py:302
  104.3 12.6 %collective-permute-start.7 = (bf16[112,128]{1,0:T(8,128)(2,1)S(1)}, bf16[112,128]{1,0:T(8,128)(2,1)S(1)}, u32[]{:S(2)}, u32[]{:S(2)}) collective-permute-start(bf16[112,128]{1,0:T(8,128)(2,1)S(1)} %get-tuple-element.39), channel_id=1, source_target_pairs={{0,256},{16,272},{32,288},{48,304},{64,320},{80,336},{96,352},{112... | collective-permute-start | bytes 86024 | tf_op jit(solution)/shard_map/ppermute | solution.py:302
  116.9 0.0 all-to-all-done.1.got_ref
  117.0 1.4 %combine_rows.1 = bf16[32,7168]{1,0:T(8,128)(2,1)} custom-call(bf16[144,32]{1,0:T(8,128)(2,1)S(1)} %get-tuple-element.34.pick_ref, bf16[16,504,128]{2,1,0:T(8,128)(2,1)S(1)} %all-to-all-done.1.got_ref), custom_call_target="tpu_custom_call" | custom-call | tf_op jit(solution)/shard_map/combine_rows/pallas_call | solution.py:328
  118.4 0.0 collective-permute-done.5.refs_0_
  118.4 0.5 collective-permute-done.6.refs_1_
  118.9 0.8 collective-permute-done.7.refs_2_
  119.7 0.7 finish.1
Async XLA Ops:
  2.5 35.0 %copy-start.3 = (bf16[144,256]{1,0:T(8,128)(2,1)S(1)}, bf16[144,256]{1,0:T(8,128)(2,1)}, u32[]{:S(2)}) copy-start(bf16[144,256]{1,0:T(8,128)(2,1)} %pre_ref) | copy-start | bytes 221188
  39.2 2.5 %copy-start = (bf16[1,128,7168]{2,1,0:T(8,128)(2,1)S(1)}, bf16[1,128,7168]{2,1,0:T(8,128)(2,1)}, u32[]{:S(2)}) copy-start(bf16[1,128,7168]{2,1,0:T(8,128)(2,1)} %down_ref.1) | copy-start | bytes 5505028
  39.2 4.5 %collective-permute-start = (bf16[64,7168]{1,0:T(8,128)(2,1)S(1)}, bf16[64,7168]{1,0:T(8,128)(2,1)S(1)}, u32[]{:S(2)}, u32[]{:S(2)}) collective-permute-start(bf16[64,7168]{1,0:T(8,128)(2,1)S(1)} %get-tuple-element.25), channel_id=1, source_target_pairs={{0,16},{16,0},{32,48},{48,32},{64,80},{80,64},{96,112},{112,96},{1... | collective-permute-start | bytes 2752520 | tf_op jit(solution)/shard_map/ppermute | solution.py:268
  42.5 6.0 %copy-start.1 = (bf16[1,7168,128]{2,1,0:T(8,128)(2,1)S(1)}, bf16[1,7168,128]{2,1,0:T(8,128)(2,1)}, u32[]{:S(2)}) copy-start(bf16[1,7168,128]{2,1,0:T(8,128)(2,1)} %gate_ref.1) | copy-start | bytes 5505028
  42.5 6.0 %copy-start.2 = (bf16[1,7168,128]{2,1,0:T(8,128)(2,1)S(1)}, bf16[1,7168,128]{2,1,0:T(8,128)(2,1)}, u32[]{:S(2)}) copy-start(bf16[1,7168,128]{2,1,0:T(8,128)(2,1)} %up_ref.1) | copy-start | bytes 5505028
  44.7 10.6 %collective-permute-start.1 = (bf16[32,7168]{1,0:T(8,128)(2,1)}, bf16[32,7168]{1,0:T(8,128)(2,1)S(1)}, u32[]{:S(2)}, u32[]{:S(2)}) collective-permute-start(bf16[32,7168]{1,0:T(8,128)(2,1)} %get-tuple-element.40), channel_id=1, source_target_pairs={{0,32},{16,1008},{32,64},{48,16},{64,96},{80,48},{96,128},{112,80}... | collective-permute-start | bytes 1376264 | tf_op jit(solution)/shard_map/ppermute | solution.py:302
  50.9 66.0 %all-to-all-start.1 = ((bf16[16,504,128]{2,1,0:T(8,128)(2,1)}), bf16[16,504,128]{2,1,0:T(8,128)(2,1)S(1)}, u32[]{:S(2)}, u32[]{:S(2)}) async-start(bf16[16,504,128]{2,1,0:T(8,128)(2,1)} %grad_rows.1), calls=%async_computation.1 | async-start | bytes 4128768 | tf_op jit(solution)/shard_map/all_to_all | solution.py:316
  55.4 25.0 %collective-permute-start.4 = (bf16[8,7168]{1,0:T(8,128)(2,1)S(1)}, bf16[8,7168]{1,0:T(8,128)(2,1)S(1)}, u32[]{:S(2)}, u32[]{:S(2)}) collective-permute-start(bf16[8,7168]{1,0:T(8,128)(2,1)S(1)} %get-tuple-element.42), channel_id=1, source_target_pairs={{0,896},{16,144},{32,928},{48,176},{64,960},{80,208},{96,992},{112... | collective-permute-start | bytes 344072 | tf_op jit(solution)/shard_map/ppermute | solution.py:302
  73.6 7.6 %collective-permute-start.3 = (bf16[8,7168]{1,0:T(8,128)(2,1)S(1)}, bf16[8,7168]{1,0:T(8,128)(2,1)S(1)}, u32[]{:S(2)}, u32[]{:S(2)}) collective-permute-start(bf16[8,7168]{1,0:T(8,128)(2,1)S(1)} %get-tuple-element.43), channel_id=1, source_target_pairs={{0,64},{16,976},{32,96},{48,1008},{64,128},{80,16},{96,160},{112,4... | collective-permute-start | bytes 344072 | tf_op jit(solution)/shard_map/ppermute | solution.py:302
  77.2 9.5 %collective-permute-start.2 = (bf16[8,7168]{1,0:T(8,128)(2,1)S(1)}, bf16[8,7168]{1,0:T(8,128)(2,1)S(1)}, u32[]{:S(2)}, u32[]{:S(2)}) collective-permute-start(bf16[8,7168]{1,0:T(8,128)(2,1)S(1)} %get-tuple-element.44), channel_id=1, source_target_pairs={{0,960},{16,80},{32,992},{48,112},{64,0},{80,144},{96,32},{112,176... | collective-permute-start | bytes 344072 | tf_op jit(solution)/shard_map/ppermute | solution.py:302
  86.8 31.6 %collective-permute-start.5 = (bf16[112,128]{1,0:T(8,128)(2,1)S(1)}, bf16[112,128]{1,0:T(8,128)(2,1)S(1)}, u32[]{:S(2)}, u32[]{:S(2)}) collective-permute-start(bf16[112,128]{1,0:T(8,128)(2,1)S(1)} %get-tuple-element.33), channel_id=1, source_target_pairs={{0,512},{16,528},{32,544},{48,560},{64,576},{80,592},{96,608},{112... | collective-permute-start | bytes 86024 | tf_op jit(solution)/shard_map/ppermute | solution.py:302
  102.4 16.5 %collective-permute-start.6 = (bf16[112,128]{1,0:T(8,128)(2,1)S(1)}, bf16[112,128]{1,0:T(8,128)(2,1)S(1)}, u32[]{:S(2)}, u32[]{:S(2)}) collective-permute-start(bf16[112,128]{1,0:T(8,128)(2,1)S(1)} %get-tuple-element.38), channel_id=1, source_target_pairs={{0,768},{16,784},{32,800},{48,816},{64,832},{80,848},{96,864},{112... | collective-permute-start | bytes 86024 | tf_op jit(solution)/shard_map/ppermute | solution.py:302
  104.3 15.4 %collective-permute-start.7 = (bf16[112,128]{1,0:T(8,128)(2,1)S(1)}, bf16[112,128]{1,0:T(8,128)(2,1)S(1)}, u32[]{:S(2)}, u32[]{:S(2)}) collective-permute-start(bf16[112,128]{1,0:T(8,128)(2,1)S(1)} %get-tuple-element.39), channel_id=1, source_target_pairs={{0,256},{16,272},{32,288},{48,304},{64,320},{80,336},{96,352},{112... | collective-permute-start | bytes 86024 | tf_op jit(solution)/shard_map/ppermute | solution.py:302

commit v11 on v10

--- a/solution.py
+++ b/solution.py
@@ -11,7 +11,6 @@
 F32 = jnp.float32
 LANES = 128
 FIRST = 8
-PARTS = 4
 NEAR = (0, -2, 2, -4)
 FAR = (0, 16, -8, 8)
 PARAMS = pltpu.CompilerParams(vmem_limit_bytes=16 * 1024 * 1024)
@@ -84,27 +83,11 @@
     out_ref[:, experts_rows(width) :, :] = tail[...].astype(BF)
 
 
-def write_all(columns, width, experts, out_ref, out_hbm, tail, sems):
-    pairs = width // (2 * LANES)
-    step = pairs // PARTS
-    stores = []
-    for pair in range(pairs):
+def write_all(columns, width, experts, out_ref, tail):
+    for pair in range(width // (2 * LANES)):
         part = columns(slice(pair * 2 * LANES, (pair + 1) * 2 * LANES))
         write_block(out_ref, tail, pair, part[:, :LANES], part[:, LANES:], experts)
-        if (pair + 1) % step == 0:
-            stop = (pair + 1) * 16
-            if pair + 1 == pairs:
-                out_ref[:, stop:, :] = tail[...].astype(BF)
-                stop = out_ref.shape[1]
-            rows = slice(len(stores) * step * 16, stop)
-            stores.append(
-                pltpu.make_async_copy(
-                    out_ref.at[:, rows, :], out_hbm.at[:, rows, :], sems[len(stores)]
-                )
-            )
-            stores[-1].start()
-    for store in stores:
-        store.wait()
+    out_ref[:, experts_rows(width) :, :] = tail[...].astype(BF)
 
 
 def experts_rows(width):
@@ -166,14 +149,17 @@
     out_ref[...] = (jnp.concatenate([grad_hidden, grad_hidden], axis=1) * factor_ref[...]).astype(BF)
 
 
-def grad_kernel(experts, hidden_ref, gate_ref, up_ref, out_hbm, out_ref, tail, sems):
+def grad_kernel(experts, hidden_ref, gate_ref, up_ref, out_hbm, out_ref, tail, sem):
     hidden = hidden_ref[...]
 
     def columns(at):
         weight = jnp.concatenate([gate_ref[0, at, :], up_ref[0, at, :]], axis=1)
         return dot(hidden, weight, ((1,), (1,)))
 
-    write_all(columns, gate_ref.shape[1], experts, out_ref, out_hbm, tail, [sems.at[i] for i in range(PARTS)])
+    write_all(columns, gate_ref.shape[1], experts, out_ref, tail)
+    store = pltpu.make_async_copy(out_ref, out_hbm, sem)
+    store.start()
+    store.wait()
 
 
 def combine_kernel(experts, pick_ref, got_ref, out_ref, tail):
@@ -292,7 +278,7 @@
         scratch_shapes=[
             pltpu.VMEM((experts, block_rows, LANES), BF),
             tail,
-            pltpu.SemaphoreType.DMA((PARTS,)),
+            pltpu.SemaphoreType.DMA,
         ],
         compiler_params=PARAMS,
         name="grad_rows",

time: 121 us -> 121 us (level)
  transfers between devices with their start and end apart: 9 -> 9, of which waited for: 6 -> 6; matrix products, arithmetic and copies ran while one was open for 0% -> 0% of each run, Pallas kernels for 4% -> 5%
where the time goes in v11:
time: 121 us; the launch traced here: 120 us
  starting transfers between devices  64.8 us (54%)
  blocking collectives  35 us (29%)
  Pallas kernels  9.7 us (8%)
  waiting for transfers between devices  9.02 us (7%)
    ppermute x7, starting transfers between devices, pass_on(): return lax.ppermute(going, 'dp', hops)  59 us
    all_to_all x1, blocking collectives, per_device(): lax.all_to_all(outgoing, 'expert', split_axis=0, concat_axis=0, tiled=True)  35 us
    ppermute x7, waiting for transfers between devices, pass_on(): return lax.ppermute(going, 'dp', hops)  7.78 us
    all_to_all x1, starting transfers between devices, per_device(): lax.all_to_all(going_back, 'expert', split_axis=0, concat_axis=0, tiled=T...  3.73 us
    pallas_call x1, Pallas kernels, per_device(): pl.pallas_call(functools.partial(grad_kernel, experts), out_shape=pltpu.H...  2.79 us
  transfers between devices with their start and end apart: 9, of which 6 were waited for; matrix products, arithmetic and copies ran while one was open for 0% of the time, Pallas kernels for 5%

profile of v11, /device:TPU:64, one launch (start us, length us, event | category | flops | bytes accessed | tf_op | source)
XLA Modules:
  0.0 120.5 jit_solution(4469232431596885948)
XLA Ops:
  0.6 0.1 pad_add_fusion.at_ref
  0.7 1.8 %dispatch_rows.1 = (bf16[16,504,128]{2,1,0:T(8,128)(2,1)S(1)}, bf16[144,32]{1,0:T(8,128)(2,1)S(1)}) custom-call(bf16[32,7168]{1,0:T(8,128)(2,1)} %dy_hbm.1, s32[4,32]{1,0:T(4,128)} %bitcast.4, f32[4,32]{1,0:T(4,128)} %bitcast.5), custom_call_target="tpu_custom_call" | custom-call | tf_op jit(solution)/shard_map/dispatch_rows/pallas_call | solution.py:218
  2.5 0.0 copy-start.3
  2.6 35.0 %all_to_all.10.got_ref = bf16[16,504,128]{2,1,0:T(8,128)(2,1)S(1)} all-to-all(bf16[16,504,128]{2,1,0:T(8,128)(2,1)S(1)} %get-tuple-element.23), channel_id=1, replica_groups=mesh['dp'=64,'expert'=16] {'expert'}, dimensions={0} | all-to-all | bytes 4128768 | tf_op jit(solution)/shard_map/all_to_all | solution.py:237
  37.6 0.0 copy-done.3
  37.6 1.7 %down_partial.1 = (bf16[144,7168]{1,0:T(8,128)(2,1)S(1)}, bf16[144,64]{1,0:T(8,128)(2,1)S(1)}, bf16[64,7168]{1,0:T(8,128)(2,1)S(1)}, f32[144,256]{1,0:T(8,128)S(1)}) custom-call(s32[2]{0:T(128)S(1)} %pad_add_fusion.at_ref, bf16[16,504,128]{2,1,0:T(8,128)(2,1)S(1)} %all_to_all.10.got_ref, bf16[144,256]{1,0:T(8,128)(2,1)S(1)} %copy-done.3), custom_call_target="tpu_custom_call" | custom-call | tf_op jit(solution)/shard_map/down_partial/pallas_call | solution.py:240
  39.2 0.0 copy-start
  39.2 2.1 %collective-permute-start = (bf16[64,7168]{1,0:T(8,128)(2,1)S(1)}, bf16[64,7168]{1,0:T(8,128)(2,1)S(1)}, u32[]{:S(2)}, u32[]{:S(2)}) collective-permute-start(bf16[64,7168]{1,0:T(8,128)(2,1)S(1)} %get-tuple-element.25), channel_id=1, source_target_pairs={{0,16},{16,0},{32,48},{48,32},{64,80},{80,64},{96,112},{112,96},{1... | collective-permute-start | bytes 2752520 | tf_op jit(solution)/shard_map/ppermute | solution.py:254
  41.3 0.5 down_kept.1
  41.8 0.0 copy-done
  41.8 0.7 grad_hidden.1.hidden_ref
  42.5 0.0 copy-start.1
  42.5 0.0 copy-start.2
  42.5 1.2 %collective-permute-done = bf16[64,7168]{1,0:T(8,128)(2,1)S(1)} collective-permute-done((bf16[64,7168]{1,0:T(8,128)(2,1)S(1)}, bf16[64,7168]{1,0:T(8,128)(2,1)S(1)}, u32[]{:S(2)}, u32[]{:S(2)}) %collective-permute-start) | collective-permute-done | bytes 917536 | tf_op jit(solution)/shard_map/ppermute | solution.py:254
  43.7 1.0 add_convert_fusion
  44.7 3.8 %collective-permute-start.1 = (bf16[32,7168]{1,0:T(8,128)(2,1)}, bf16[32,7168]{1,0:T(8,128)(2,1)S(1)}, u32[]{:S(2)}, u32[]{:S(2)}) collective-permute-start(bf16[32,7168]{1,0:T(8,128)(2,1)} %get-tuple-element.40), channel_id=1, source_target_pairs={{0,32},{16,1008},{32,64},{48,16},{64,96},{80,48},{96,128},{112,80}... | collective-permute-start | bytes 1376264 | tf_op jit(solution)/shard_map/ppermute | solution.py:288
  48.5 0.0 copy-done.1
  48.5 0.0 copy-done.2
  48.5 2.8 %grad_rows.1 = bf16[16,504,128]{2,1,0:T(8,128)(2,1)} custom-call(bf16[144,256]{1,0:T(8,128)(2,1)S(1)} %grad_hidden.1.hidden_ref, bf16[1,7168,128]{2,1,0:T(8,128)(2,1)S(1)} %copy-done.1, bf16[1,7168,128]{2,1,0:T(8,128)(2,1)S(1)} %copy-done.2), custom_call_target="tpu_custom_call" | custom-call | tf_op jit(solution)/shard_map/grad_rows/pallas_call | solution.py:273
  51.3 3.7 %all-to-all-start.1 = ((bf16[16,504,128]{2,1,0:T(8,128)(2,1)}), bf16[16,504,128]{2,1,0:T(8,128)(2,1)S(1)}, u32[]{:S(2)}, u32[]{:S(2)}) async-start(bf16[16,504,128]{2,1,0:T(8,128)(2,1)} %grad_rows.1), calls=%async_computation.1 | async-start | bytes 4128768 | tf_op jit(solution)/shard_map/all_to_all | solution.py:302
  55.1 0.2 collective-permute-done.1
  55.3 0.1 fusion
  55.4 18.2 %collective-permute-start.4 = (bf16[8,7168]{1,0:T(8,128)(2,1)S(1)}, bf16[8,7168]{1,0:T(8,128)(2,1)S(1)}, u32[]{:S(2)}, u32[]{:S(2)}) collective-permute-start(bf16[8,7168]{1,0:T(8,128)(2,1)S(1)} %get-tuple-element.42), channel_id=1, source_target_pairs={{0,896},{16,144},{32,928},{48,176},{64,960},{80,208},{96,992},{112... | collective-permute-start | bytes 344072 | tf_op jit(solution)/shard_map/ppermute | solution.py:288
  73.6 3.6 %collective-permute-start.3 = (bf16[8,7168]{1,0:T(8,128)(2,1)S(1)}, bf16[8,7168]{1,0:T(8,128)(2,1)S(1)}, u32[]{:S(2)}, u32[]{:S(2)}) collective-permute-start(bf16[8,7168]{1,0:T(8,128)(2,1)S(1)} %get-tuple-element.43), channel_id=1, source_target_pairs={{0,64},{16,976},{32,96},{48,1008},{64,128},{80,16},{96,160},{112,4... | collective-permute-start | bytes 344072 | tf_op jit(solution)/shard_map/ppermute | solution.py:288
  77.2 3.2 %collective-permute-start.2 = (bf16[8,7168]{1,0:T(8,128)(2,1)S(1)}, bf16[8,7168]{1,0:T(8,128)(2,1)S(1)}, u32[]{:S(2)}, u32[]{:S(2)}) collective-permute-start(bf16[8,7168]{1,0:T(8,128)(2,1)S(1)} %get-tuple-element.44), channel_id=1, source_target_pairs={{0,960},{16,80},{32,992},{48,112},{64,0},{80,144},{96,32},{112,176... | collective-permute-start | bytes 344072 | tf_op jit(solution)/shard_map/ppermute | solution.py:288
  80.3 0.0 collective-permute-done.4.refs_2_
  80.3 0.8 collective-permute-done.3.refs_1_
  81.2 5.5 %collective-permute-done.2.refs_0_ = bf16[8,7168]{1,0:T(8,128)(2,1)S(1)} collective-permute-done((bf16[8,7168]{1,0:T(8,128)(2,1)S(1)}, bf16[8,7168]{1,0:T(8,128)(2,1)S(1)}, u32[]{:S(2)}, u32[]{:S(2)}) %collective-permute-start.2) | collective-permute-done | bytes 114720 | tf_op jit(solution)/shard_map/ppermute | solution.py:288
  86.7 0.2 fold.1
  86.8 15.7 %collective-permute-start.5 = (bf16[112,128]{1,0:T(8,128)(2,1)S(1)}, bf16[112,128]{1,0:T(8,128)(2,1)S(1)}, u32[]{:S(2)}, u32[]{:S(2)}) collective-permute-start(bf16[112,128]{1,0:T(8,128)(2,1)S(1)} %get-tuple-element.33), channel_id=1, source_target_pairs={{0,512},{16,528},{32,544},{48,560},{64,576},{80,592},{96,608},{112... | collective-permute-start | bytes 86024 | tf_op jit(solution)/shard_map/ppermute | solution.py:288
  102.5 1.9 %collective-permute-start.6 = (bf16[112,128]{1,0:T(8,128)(2,1)S(1)}, bf16[112,128]{1,0:T(8,128)(2,1)S(1)}, u32[]{:S(2)}, u32[]{:S(2)}) collective-permute-start(bf16[112,128]{1,0:T(8,128)(2,1)S(1)} %get-tuple-element.38), channel_id=1, source_target_pairs={{0,768},{16,784},{32,800},{48,816},{64,832},{80,848},{96,864},{112... | collective-permute-start | bytes 86024 | tf_op jit(solution)/shard_map/ppermute | solution.py:288
  104.4 12.6 %collective-permute-start.7 = (bf16[112,128]{1,0:T(8,128)(2,1)S(1)}, bf16[112,128]{1,0:T(8,128)(2,1)S(1)}, u32[]{:S(2)}, u32[]{:S(2)}) collective-permute-start(bf16[112,128]{1,0:T(8,128)(2,1)S(1)} %get-tuple-element.39), channel_id=1, source_target_pairs={{0,256},{16,272},{32,288},{48,304},{64,320},{80,336},{96,352},{112... | collective-permute-start | bytes 86024 | tf_op jit(solution)/shard_map/ppermute | solution.py:288
  117.1 0.0 all-to-all-done.1.got_ref
  117.1 1.4 %combine_rows.1 = bf16[32,7168]{1,0:T(8,128)(2,1)} custom-call(bf16[144,32]{1,0:T(8,128)(2,1)S(1)} %get-tuple-element.34.pick_ref, bf16[16,504,128]{2,1,0:T(8,128)(2,1)S(1)} %all-to-all-done.1.got_ref), custom_call_target="tpu_custom_call" | custom-call | tf_op jit(solution)/shard_map/combine_rows/pallas_call | solution.py:314
  118.5 0.0 collective-permute-done.5.refs_0_
  118.5 0.3 collective-permute-done.6.refs_1_
  118.8 1.0 collective-permute-done.7.refs_2_
  119.8 0.7 finish.1
Async XLA Ops:
  2.5 35.0 %copy-start.3 = (bf16[144,256]{1,0:T(8,128)(2,1)S(1)}, bf16[144,256]{1,0:T(8,128)(2,1)}, u32[]{:S(2)}) copy-start(bf16[144,256]{1,0:T(8,128)(2,1)} %pre_ref) | copy-start | bytes 221188
  39.2 2.5 %copy-start = (bf16[1,128,7168]{2,1,0:T(8,128)(2,1)S(1)}, bf16[1,128,7168]{2,1,0:T(8,128)(2,1)}, u32[]{:S(2)}) copy-start(bf16[1,128,7168]{2,1,0:T(8,128)(2,1)} %down_ref.1) | copy-start | bytes 5505028
  39.2 4.5 %collective-permute-start = (bf16[64,7168]{1,0:T(8,128)(2,1)S(1)}, bf16[64,7168]{1,0:T(8,128)(2,1)S(1)}, u32[]{:S(2)}, u32[]{:S(2)}) collective-permute-start(bf16[64,7168]{1,0:T(8,128)(2,1)S(1)} %get-tuple-element.25), channel_id=1, source_target_pairs={{0,16},{16,0},{32,48},{48,32},{64,80},{80,64},{96,112},{112,96},{1... | collective-permute-start | bytes 2752520 | tf_op jit(solution)/shard_map/ppermute | solution.py:254
  42.5 6.0 %copy-start.1 = (bf16[1,7168,128]{2,1,0:T(8,128)(2,1)S(1)}, bf16[1,7168,128]{2,1,0:T(8,128)(2,1)}, u32[]{:S(2)}) copy-start(bf16[1,7168,128]{2,1,0:T(8,128)(2,1)} %gate_ref.1) | copy-start | bytes 5505028
  42.5 6.0 %copy-start.2 = (bf16[1,7168,128]{2,1,0:T(8,128)(2,1)S(1)}, bf16[1,7168,128]{2,1,0:T(8,128)(2,1)}, u32[]{:S(2)}) copy-start(bf16[1,7168,128]{2,1,0:T(8,128)(2,1)} %up_ref.1) | copy-start | bytes 5505028
  44.7 10.6 %collective-permute-start.1 = (bf16[32,7168]{1,0:T(8,128)(2,1)}, bf16[32,7168]{1,0:T(8,128)(2,1)S(1)}, u32[]{:S(2)}, u32[]{:S(2)}) collective-permute-start(bf16[32,7168]{1,0:T(8,128)(2,1)} %get-tuple-element.40), channel_id=1, source_target_pairs={{0,32},{16,1008},{32,64},{48,16},{64,96},{80,48},{96,128},{112,80}... | collective-permute-start | bytes 1376264 | tf_op jit(solution)/shard_map/ppermute | solution.py:288
  51.3 65.7 %all-to-all-start.1 = ((bf16[16,504,128]{2,1,0:T(8,128)(2,1)}), bf16[16,504,128]{2,1,0:T(8,128)(2,1)S(1)}, u32[]{:S(2)}, u32[]{:S(2)}) async-start(bf16[16,504,128]{2,1,0:T(8,128)(2,1)} %grad_rows.1), calls=%async_computation.1 | async-start | bytes 4128768 | tf_op jit(solution)/shard_map/all_to_all | solution.py:302
  55.4 25.0 %collective-permute-start.4 = (bf16[8,7168]{1,0:T(8,128)(2,1)S(1)}, bf16[8,7168]{1,0:T(8,128)(2,1)S(1)}, u32[]{:S(2)}, u32[]{:S(2)}) collective-permute-start(bf16[8,7168]{1,0:T(8,128)(2,1)S(1)} %get-tuple-element.42), channel_id=1, source_target_pairs={{0,896},{16,144},{32,928},{48,176},{64,960},{80,208},{96,992},{112... | collective-permute-start | bytes 344072 | tf_op jit(solution)/shard_map/ppermute | solution.py:288
  73.6 7.6 %collective-permute-start.3 = (bf16[8,7168]{1,0:T(8,128)(2,1)S(1)}, bf16[8,7168]{1,0:T(8,128)(2,1)S(1)}, u32[]{:S(2)}, u32[]{:S(2)}) collective-permute-start(bf16[8,7168]{1,0:T(8,128)(2,1)S(1)} %get-tuple-element.43), channel_id=1, source_target_pairs={{0,64},{16,976},{32,96},{48,1008},{64,128},{80,16},{96,160},{112,4... | collective-permute-start | bytes 344072 | tf_op jit(solution)/shard_map/ppermute | solution.py:288
  77.2 9.5 %collective-permute-start.2 = (bf16[8,7168]{1,0:T(8,128)(2,1)S(1)}, bf16[8,7168]{1,0:T(8,128)(2,1)S(1)}, u32[]{:S(2)}, u32[]{:S(2)}) collective-permute-start(bf16[8,7168]{1,0:T(8,128)(2,1)S(1)} %get-tuple-element.44), channel_id=1, source_target_pairs={{0,960},{16,80},{32,992},{48,112},{64,0},{80,144},{96,32},{112,176... | collective-permute-start | bytes 344072 | tf_op jit(solution)/shard_map/ppermute | solution.py:288
  86.8 31.7 %collective-permute-start.5 = (bf16[112,128]{1,0:T(8,128)(2,1)S(1)}, bf16[112,128]{1,0:T(8,128)(2,1)S(1)}, u32[]{:S(2)}, u32[]{:S(2)}) collective-permute-start(bf16[112,128]{1,0:T(8,128)(2,1)S(1)} %get-tuple-element.33), channel_id=1, source_target_pairs={{0,512},{16,528},{32,544},{48,560},{64,576},{80,592},{96,608},{112... | collective-permute-start | bytes 86024 | tf_op jit(solution)/shard_map/ppermute | solution.py:288
  102.5 16.3 %collective-permute-start.6 = (bf16[112,128]{1,0:T(8,128)(2,1)S(1)}, bf16[112,128]{1,0:T(8,128)(2,1)S(1)}, u32[]{:S(2)}, u32[]{:S(2)}) collective-permute-start(bf16[112,128]{1,0:T(8,128)(2,1)S(1)} %get-tuple-element.38), channel_id=1, source_target_pairs={{0,768},{16,784},{32,800},{48,816},{64,832},{80,848},{96,864},{112... | collective-permute-start | bytes 86024 | tf_op jit(solution)/shard_map/ppermute | solution.py:288
  104.4 15.3 %collective-permute-start.7 = (bf16[112,128]{1,0:T(8,128)(2,1)S(1)}, bf16[112,128]{1,0:T(8,128)(2,1)S(1)}, u32[]{:S(2)}, u32[]{:S(2)}) collective-permute-start(bf16[112,128]{1,0:T(8,128)(2,1)S(1)} %get-tuple-element.39), channel_id=1, source_target_pairs={{0,256},{16,272},{32,288},{48,304},{64,320},{80,336},{96,352},{112... | collective-permute-start | bytes 86024 | tf_op jit(solution)/shard_map/ppermute | solution.py:288
